TPU v7x, 32 devices: a whole 2x2x4 slice. The times are simulated.
32 devices in a mesh: pipe: 2 (over core), dp: 4 (over z), expert: 4 (over y, x).
Axes of the slice: x: 2, y: 2, z: 4, core: 2. Of those that a mesh axis runs over, the one named last changes fastest.
Arguments:
- section_input: bfloat16 [2, 2, 16, 64, 1536], P('pipe', None, ('dp', 'expert')), may hold values from -6 to 6
- out_grad: bfloat16 [2, 2, 16, 64, 1536], P('pipe', None, ('dp', 'expert')), may hold values from -6 to 6
- routes: int32 [2, 2, 16, 64, 2], P('pipe', None, ('dp', 'expert')), may hold values from 0 to 3, all different within a row; in each aligned block of 64 rows (0 to 63, 64 to 127, ..., all dimensions but the last counted through in order) at most 36 rows name the same one
- combine: float32 [2, 2, 16, 64, 2], P('pipe', None, ('dp', 'expert')), may hold values from 0.2 to 1
- kernel: float32 [2, 31, 1536], P('pipe'), may hold values from -1 to 1
- norm_gain: float32 [2, 1536], P('pipe'), may hold values from 0.5 to 1.5
- up_weight: bfloat16 [2, 4, 1536, 6144], P('pipe', 'expert', None, 'dp'), may hold values from -0.15625 to 0.15625
- down_weight: bfloat16 [2, 4, 6144, 1536], P('pipe', 'expert', 'dp'), may hold values from -0.078125 to 0.078125
Outputs:
- prev_grad: bfloat16 [2, 2, 16, 64, 1536], P('pipe', None, ('dp', 'expert'))
- kernel_grad: float32 [2, 31, 1536], P('pipe')
- gain_grad: float32 [2, 1536], P('pipe')
- up_grad: bfloat16 [2, 4, 1536, 6144], P('pipe', 'expert', None, 'dp')
- down_grad: bfloat16 [2, 4, 6144, 1536], P('pipe', 'expert', 'dp')
Inputs may be any that keep to these rules, and one draw needn't show every extreme that they name: `routes`: within each sequence of one micro-batch of one section, no expert is named by more than 36 choices, a bound that some block reaches there in every draw; the 2 experts of a frame differ.
All inputs are finite; a program needn't handle non-finite values.
Results may differ from a plain program's by a relative error of at most 0.0066.
Values may be sent and summed in bfloat16 or wider, within the bound.
No kernel may reach another device: no remote copies, remote signals or barrier semaphores. Data moves between devices by JAX's collectives and lax.ppermute only.
A program may use at most 128 MiB of HBM per device.

v0:
```python
import jax
import jax.numpy as jnp
from jax import lax
from jax.sharding import PartitionSpec as P

MB = 2


EPSILON = 1e-06


def passed_along(array, axis, by):
    peers = lax.axis_size(axis)
    return lax.ppermute(array, axis, [(i, (i + by) % peers) for i in range(peers)])


def silu_slope(values):
    gate_sig = jax.nn.sigmoid(values)
    return gate_sig * (1.0 + values * (1.0 - gate_sig))


def pad_frames(frames, margin):
    widths = [(0, 0)] * (frames.ndim - 2) + [(margin, margin), (0, 0)]
    return jnp.pad(frames, widths)


def depthwise(frames, conv_taps):
    tap_count = conv_taps.shape[0]
    margin = tap_count // 2
    length = frames.shape[-2]
    padded = pad_frames(frames, margin)
    result = jnp.zeros(frames.shape, jnp.float32)
    for offset in range(tap_count):
        result = result + conv_taps[offset] * lax.slice_in_dim(
            padded, offset, offset + length, axis=frames.ndim - 2
        )
    return result


def depthwise_transpose(grad_rows, conv_taps):
    tap_count = conv_taps.shape[0]
    margin = tap_count // 2
    length = grad_rows.shape[-2]
    padded = pad_frames(grad_rows, margin)
    result = jnp.zeros(grad_rows.shape, jnp.float32)
    for offset in range(tap_count):
        first = 2 * margin - offset
        result = result + conv_taps[offset] * lax.slice_in_dim(
            padded, first, first + length, axis=grad_rows.ndim - 2
        )
    return result


def depthwise_taps_grad(grad_rows, frames, tap_count):
    margin = tap_count // 2
    length = frames.shape[-2]
    padded = pad_frames(frames, margin)
    tap_rows = []
    for offset in range(tap_count):
        shifted = lax.slice_in_dim(padded, offset, offset + length, axis=frames.ndim - 2)
        tap_rows.append(jnp.sum(grad_rows * shifted, axis=tuple(range(frames.ndim - 1))))
    return jnp.stack(tap_rows)


def slot_targets(route_rows, experts, capacity):
    flat_ids = route_rows.reshape(-1)
    onehot = (flat_ids[:, None] == jnp.arange(experts, dtype=jnp.int32)[None, :]).astype(jnp.int32)
    rank_run = jnp.cumsum(onehot, axis=0) - 1
    slot_index = jnp.sum(onehot * rank_run, axis=1)
    return flat_ids * capacity + slot_index


def local(section_input, out_grad, routes, combine, kernel, norm_gain, up_weight, down_weight):
    experts = lax.axis_size("expert")
    frame_count = section_input.shape[3]
    feature_count = section_input.shape[4]
    top_count = routes.shape[4]
    capacity = 9 * frame_count * top_count // (8 * experts)
    total_slots = experts * capacity
    conv_taps = kernel[0]
    gain_vec = norm_gain[0]
    up_mat = up_weight[0, 0]
    down_mat = down_weight[0, 0]
    up_sum = jnp.zeros(up_mat.shape, jnp.float32)
    down_sum = jnp.zeros(down_mat.shape, jnp.float32)
    taps_sum = jnp.zeros(conv_taps.shape, jnp.float32)
    gain_sum = jnp.zeros(gain_vec.shape, jnp.float32)
    slot_ids = jnp.arange(total_slots, dtype=jnp.int32)
    handed = []
    for micro_step in range(MB):
        inputs = section_input[0, micro_step, 0].astype(jnp.float32)
        conv_out = depthwise(inputs, conv_taps)
        mixed = inputs + jax.nn.silu(conv_out)
        scale_inv = lax.rsqrt(jnp.mean(mixed * mixed, axis=-1, keepdims=True) + EPSILON)
        normed = (mixed * scale_inv * gain_vec).astype(jnp.bfloat16)
        upstream = out_grad[0, micro_step, 0].astype(jnp.float32)
        weighted = (combine[0, micro_step, 0][..., None] * upstream[:, None, :]).astype(
            jnp.bfloat16
        )
        copies = jnp.broadcast_to(normed[:, None, :], weighted.shape).reshape(
            frame_count * top_count, feature_count
        )
        weighted = weighted.reshape(frame_count * top_count, feature_count)
        targets = slot_targets(routes[0, micro_step, 0], experts, capacity)
        placing = (slot_ids[:, None] == targets[None, :]).astype(jnp.bfloat16)
        picking = (targets[:, None] == slot_ids[None, :]).astype(jnp.bfloat16)
        send_in = jnp.dot(placing, copies, preferred_element_type=jnp.float32).astype(jnp.bfloat16)
        send_grad = jnp.dot(placing, weighted, preferred_element_type=jnp.float32).astype(
            jnp.bfloat16
        )
        send_in = send_in.reshape(experts, capacity, feature_count)
        send_grad = send_grad.reshape(experts, capacity, feature_count)
        owner_in, owner_grad = (
            lax.all_to_all(send_in, "expert", split_axis=0, concat_axis=0, tiled=True),
            lax.all_to_all(send_grad, "expert", split_axis=0, concat_axis=0, tiled=True),
        )
        rows_in, rows_grad = (
            lax.all_gather(owner_in, "dp", axis=0, tiled=True),
            lax.all_gather(owner_grad, "dp", axis=0, tiled=True),
        )
        rows_in = rows_in.reshape(-1, feature_count)
        rows_grad = rows_grad.reshape(-1, feature_count)
        pre_act = jnp.dot(rows_in, up_mat, preferred_element_type=jnp.float32)
        activated = jax.nn.silu(pre_act).astype(jnp.bfloat16)
        down_sum = down_sum + jnp.dot(activated.T, rows_grad, preferred_element_type=jnp.float32)
        act_grad = jnp.dot(rows_grad, down_mat.T, preferred_element_type=jnp.float32)
        pre_grad = (act_grad * silu_slope(pre_act)).astype(jnp.bfloat16)
        up_sum = up_sum + jnp.dot(rows_in.T, pre_grad, preferred_element_type=jnp.float32)
        summed = lax.psum_scatter(
            jnp.dot(pre_grad, up_mat.T, preferred_element_type=jnp.float32),
            "dp",
            scatter_dimension=0,
            tiled=True,
        )
        returned = lax.all_to_all(
            summed.astype(jnp.bfloat16).reshape(experts, capacity, feature_count),
            "expert",
            split_axis=0,
            concat_axis=0,
            tiled=True,
        )
        gathered = jnp.dot(
            picking,
            returned.reshape(total_slots, feature_count),
            preferred_element_type=jnp.float32,
        )
        norm_grad = jnp.sum(gathered.reshape(frame_count, top_count, feature_count), axis=1)
        gain_term = jnp.sum(norm_grad * mixed * scale_inv, axis=0)
        scaled = norm_grad * gain_vec
        mixed_grad = (
            upstream
            + scale_inv * scaled
            - mixed * scale_inv**3 * jnp.mean(scaled * mixed, axis=-1, keepdims=True)
        )
        conv_grad = mixed_grad * silu_slope(conv_out)
        taps_term = depthwise_taps_grad(conv_grad, inputs, conv_taps.shape[0])
        frames_grad = (mixed_grad + depthwise_transpose(conv_grad, conv_taps)).astype(jnp.bfloat16)
        handed.append(passed_along(frames_grad, "pipe", -1))
        taps_total, gain_total = lax.psum((taps_term, gain_term), ("dp", "expert"))
        taps_sum = taps_sum + taps_total
        gain_sum = gain_sum + gain_total
    previous = jnp.stack(handed)[None, :, None]
    return (
        previous,
        taps_sum[None],
        gain_sum[None],
        up_sum.astype(jnp.bfloat16)[None, None],
        down_sum.astype(jnp.bfloat16)[None, None],
    )


def solution(mesh):
    placed = (
        P("pipe", None, ("dp", "expert"), None, None),
        P("pipe", None, ("dp", "expert"), None, None),
        P("pipe", None, ("dp", "expert"), None, None),
        P("pipe", None, ("dp", "expert"), None, None),
        P("pipe", None, None),
        P("pipe", None),
        P("pipe", "expert", None, "dp"),
        P("pipe", "expert", "dp", None),
    )
    return jax.shard_map(
        local,
        mesh=mesh,
        in_specs=placed,
        out_specs=(
            P("pipe", None, ("dp", "expert"), None, None),
            P("pipe", None, None),
            P("pipe", None),
            P("pipe", "expert", None, "dp"),
            P("pipe", "expert", "dp", None),
        ),
        check_vma=False,
    )
```

profile of v0, /device:TPU:0, one launch (start us, length us, event | category | flops | bytes accessed | tf_op | source)
XLA Modules:
  0.0 537.1 jit_solution(11973701828022411229)
XLA Ops:
  17.1 13.3 %all_to_all.30 = bf16[4,36,1536]{2,1,0:T(8,128)(2,1)} all-to-all(bf16[4,36,1536]{2,1,0:T(8,128)(2,1)S(1)} %reshape.271), channel_id=1, replica_groups=mesh['pipe'=2,'dp'=4,'expert'=4] {'expert'}, dimensions={0} | all-to-all | bytes 884736 | tf_op jit(solution)/shard_map/all_to_all | solution.py:114
  34.6 10.2 %all_to_all.31 = bf16[4,36,1536]{2,1,0:T(8,128)(2,1)} all-to-all(bf16[4,36,1536]{2,1,0:T(8,128)(2,1)S(1)} %reshape.268), channel_id=1, replica_groups=mesh['pipe'=2,'dp'=4,'expert'=4] {'expert'}, dimensions={0} | all-to-all | bytes 884736 | tf_op jit(solution)/shard_map/all_to_all | solution.py:115
  44.8 29.0 %all-gather.7.cloned.1.call-done = bf16[16,36,1536]{2,1,0:T(8,128)(2,1)} async-done(((bf16[4,36,1536]{2,1,0:T(8,128)(2,1)}), bf16[16,36,1536]{2,1,0:T(8,128)(2,1)}) %all-gather.7.cloned.1.call-update) | async-done | bytes 1769488 | tf_op jit(solution)/shard_map/all_gather | solution.py:118
  76.2 7.7 %fusion.8 = f32[576,1536]{1,0:T(8,128)} fusion(bf16[576,1536]{1,0:T(8,128)(2,1)S(1)} %reshape.272, bf16[1,1,1536,1536]{3,2,1,0:T(8,128)(2,1)} %param.14), kind=kOutput, calls=%fused_computation.10 | convolution fusion | flops 2717908992 | bytes 10027008 | tf_op jit(solution)/shard_map/dot_general | solution.py:123
  83.9 33.9 %all-gather.5.cloned.1.call-done = bf16[16,36,1536]{2,1,0:T(8,128)(2,1)} async-done(((bf16[4,36,1536]{2,1,0:T(8,128)(2,1)}), bf16[16,36,1536]{2,1,0:T(8,128)(2,1)}) %all-gather.5.cloned.1.call-update) | async-done | bytes 1769488 | tf_op jit(solution)/shard_map/all_gather | solution.py:119
  120.2 6.9 %multiply_convert_fusion.3 = bf16[576,1536]{1,0:T(8,128)(2,1)S(1)} fusion(f32[576,1536]{1,0:T(8,128)} %fusion.8, bf16[576,1536]{1,0:T(8,128)(2,1)S(1)} %reshape.269, bf16[1,1,1536,1536]{3,2,1,0:T(8,128)(2,1)} %param.15), kind=kOutput, calls=%fused_computation.20 | convolution fusion | flops 2725871616 | bytes 11796480 | tf_op jit(solution)/shard_map/dot_general | solution.py:126
  128.4 7.1 %fusion.6 = f32[576,1536]{1,0:T(8,128)} fusion(bf16[576,1536]{1,0:T(8,128)(2,1)S(1)} %multiply_convert_fusion.3, bf16[1,1,1536,1536]{3,2,1,0:T(8,128)(2,1)} %param.14), kind=kOutput, calls=%fused_computation.8 | convolution fusion | flops 2717908992 | bytes 10027008 | tf_op jit(solution)/shard_map/dot_general | solution.py:130
  142.1 11.8 %all_to_all.32 = bf16[4,36,1536]{2,1,0:T(8,128)(2,1)} all-to-all(bf16[4,36,1536]{2,1,0:T(8,128)(2,1)S(1)} %reshape.275), channel_id=1, replica_groups=mesh['pipe'=2,'dp'=4,'expert'=4] {'expert'}, dimensions={0} | all-to-all | bytes 884736 | tf_op jit(solution)/shard_map/all_to_all | solution.py:115
  156.3 44.5 %reduce-scatter.3.cloned.1.call-done = f32[144,1536]{1,0:T(8,128)} async-done(((f32[576,1536]{1,0:T(8,128)}), f32[144,1536]{1,0:T(8,128)}) %reduce-scatter.3.cloned.1.call-update) | async-done | bytes 884752 | tf_op jit(solution)/shard_map/reduce_scatter | solution.py:129
  208.1 6.0 %all-to-all-done.2 = bf16[4,36,1536]{2,1,0:T(8,128)(2,1)S(1)} async-done(((bf16[4,36,1536]{2,1,0:T(8,128)(2,1)}), bf16[4,36,1536]{2,1,0:T(8,128)(2,1)S(1)}, u32[]{:S(2)}, u32[]{:S(2)}) %all-to-all-start.2) | async-done | bytes 442400 | tf_op jit(solution)/shard_map/all_to_all | solution.py:135
  218.4 10.4 %all_to_all.33 = bf16[4,36,1536]{2,1,0:T(8,128)(2,1)} all-to-all(bf16[4,36,1536]{2,1,0:T(8,128)(2,1)S(1)} %reshape.278), channel_id=1, replica_groups=mesh['pipe'=2,'dp'=4,'expert'=4] {'expert'}, dimensions={0} | all-to-all | bytes 884736 | tf_op jit(solution)/shard_map/all_to_all | solution.py:114
  228.8 17.3 %all-gather.9.cloned.1.call-done = bf16[16,36,1536]{2,1,0:T(8,128)(2,1)} async-done(((bf16[4,36,1536]{2,1,0:T(8,128)(2,1)}), bf16[16,36,1536]{2,1,0:T(8,128)(2,1)}) %all-gather.9.cloned.1.call-update) | async-done | bytes 1769488 | tf_op jit(solution)/shard_map/all_gather | solution.py:119
  249.7 40.3 %all-gather.11.cloned.1.call-done = bf16[16,36,1536]{2,1,0:T(8,128)(2,1)} async-done(((bf16[4,36,1536]{2,1,0:T(8,128)(2,1)}), bf16[16,36,1536]{2,1,0:T(8,128)(2,1)}) %all-gather.11.cloned.1.call-update) | async-done | bytes 1769488 | tf_op jit(solution)/shard_map/all_gather | solution.py:118
  293.5 5.4 %fusion.4 = f32[576,1536]{1,0:T(8,128)S(1)} fusion(bf16[576,1536]{1,0:T(8,128)(2,1)} %reshape.279, bf16[1,1,1536,1536]{3,2,1,0:T(8,128)(2,1)} %param.14), kind=kOutput, calls=%fused_computation.6 | convolution fusion | flops 2717908992 | bytes 10027008 | tf_op jit(solution)/shard_map/dot_general | solution.py:123
  299.0 7.0 %multiply_convert_fusion.2 = bf16[576,1536]{1,0:T(8,128)(2,1)S(1)} fusion(f32[576,1536]{1,0:T(8,128)S(1)} %fusion.4, bf16[576,1536]{1,0:T(8,128)(2,1)S(1)} %copy-done.5, bf16[1,1,1536,1536]{3,2,1,0:T(8,128)(2,1)} %param.15), kind=kOutput, calls=%fused_computation.18 | convolution fusion | flops 2725871616 | bytes 11796480 | tf_op jit(solution)/shard_map/dot_general | solution.py:126
  307.4 4.7 fusion.2
  312.1 9.7 %fusion.163 = f32[1536,1536]{1,0:T(8,128)} fusion(bf16[576,1536]{1,0:T(8,128)(2,1)} %copy-done.2, bf16[576,1536]{1,0:T(8,128)(2,1)} %copy-done.125), kind=kOutput, calls=%fused_computation.427 | convolution fusion | flops 2717908992 | bytes 12976128 | tf_op jit(solution)/shard_map/dot_general | solution.py:128
  322.2 6.3 %fusion.18 = f32[1536,1536]{1,0:T(8,128)} fusion(bf16[576,1536]{1,0:T(8,128)(2,1)S(1)} %copy-done.4, f32[576,1536]{1,0:T(8,128)S(1)} %copy-done.126), kind=kOutput, calls=%fused_computation.146 | convolution fusion | flops 2722332672 | bytes 14745600 | tf_op jit(solution)/shard_map/dot_general | solution.py:125
  342.7 34.7 %reduce-scatter.5.cloned.1.call-done = f32[144,1536]{1,0:T(8,128)} async-done(((f32[576,1536]{1,0:T(8,128)}), f32[144,1536]{1,0:T(8,128)}) %reduce-scatter.5.cloned.1.call-update) | async-done | bytes 884752 | tf_op jit(solution)/shard_map/reduce_scatter | solution.py:129
  385.5 9.8 %all-reduce.6.cloned.1.call-start = ((), (), s32[]{:S(2)}) async-start(), calls=%async_computation.14 | async-start | bytes 393216 | tf_op jit(solution)/shard_map/psum | solution.py:159
  395.3 11.4 %fusion.1 = bf16[1,1,1536,1536]{3,2,1,0:T(8,128)(2,1)} fusion(f32[1536,1536]{1,0:T(8,128)} %fusion.18, bf16[576,1536]{1,0:T(8,128)(2,1)} %reshape.276, f32[576,1536]{1,0:T(8,128)} %copy-done.127), kind=kOutput, calls=%fused_computation.3 | convolution fusion | flops 2727051264 | bytes 19464192 | tf_op jit(solution)/shard_map/dot_general | solution.py:125
  418.9 10.8 %fusion = bf16[1,1,1536,1536]{3,2,1,0:T(8,128)(2,1)} fusion(f32[1536,1536]{1,0:T(8,128)} %fusion.163, bf16[576,1536]{1,0:T(8,128)(2,1)} %reshape.279, bf16[576,1536]{1,0:T(8,128)(2,1)} %copy-done.128), kind=kOutput, calls=%fused_computation.2 | convolution fusion | flops 2722627584 | bytes 17694720 | tf_op jit(solution)/shard_map/dot_general | solution.py:128
  429.8 41.7 %psum.33 = f32[1536]{0:T(1024)S(1)} all-reduce(f32[1536]{0:T(1024)S(1)} %add.631), channel_id=1, replica_groups=mesh['pipe'=2,'dp'=4,'expert'=4] {'dp','expert'}, use_global_device_ids=true, to_apply=%region_77.78 | all-reduce | flops 1536 | bytes 12288 | tf_op jit(solution)/shard_map/psum | solution.py:159
  472.1 54.5 %all-reduce.6.cloned.1.call-done = f32[31,1536]{1,0:T(8,128)} async-done(((f32[31,1536]{1,0:T(8,128)}), f32[31,1536]{1,0:T(8,128)}) %all-reduce.6.cloned.1.call-update) | async-done | bytes 190480 | tf_op jit(solution)/shard_map/psum | solution.py:159
  (423 shorter events, 85.9 us)
Async XLA Ops:
  7.2 66.6 %all-gather.7.cloned.1.call-start = ((), (), s32[]{:S(2)}) async-start(), calls=%async_computation.9 | async-start | bytes 2457600 | tf_op jit(solution)/shard_map/all_gather | solution.py:118
  11.1 19.3 %copy-start.119 = (s32[128]{0:T(128)}, s32[128]{0:T(128)S(1)}, u32[]{:S(2)}) copy-start(s32[128]{0:T(128)S(1)} %select_reduce_fusion.1) | copy-start | bytes 1540
  12.3 18.5 %copy-start.1 = (bf16[1,2,1,64,1536]{4,3,2,1,0:T(8,128)(2,1)S(1)}, bf16[1,2,1,64,1536]{4,3,2,1,0:T(8,128)(2,1)}, u32[]{:S(2)}) copy-start(bf16[1,2,1,64,1536]{4,3,2,1,0:T(8,128)(2,1)} %param.9) | copy-start | bytes 1179652
  30.5 87.4 %all-gather.5.cloned.1.call-start = ((), (), s32[]{:S(2)}) async-start(), calls=%async_computation.8 | async-start | bytes 2457600 | tf_op jit(solution)/shard_map/all_gather | solution.py:119
  44.8 156.0 %reduce-scatter.3.cloned.1.call-start = ((), (), s32[]{:S(2)}) async-start(), calls=%async_computation.10 | async-start | bytes 4423680 | tf_op jit(solution)/shard_map/reduce_scatter | solution.py:129
  135.4 18.5 %copy-start = (bf16[1,2,1,64,1536]{4,3,2,1,0:T(8,128)(2,1)S(1)}, bf16[1,2,1,64,1536]{4,3,2,1,0:T(8,128)(2,1)}, u32[]{:S(2)}) copy-start(bf16[1,2,1,64,1536]{4,3,2,1,0:T(8,128)(2,1)} %param.8) | copy-start | bytes 1179652
  135.5 110.6 %all-gather.9.cloned.1.call-start = ((), (), s32[]{:S(2)}) async-start(), calls=%async_computation.11 | async-start | bytes 2457600 | tf_op jit(solution)/shard_map/all_gather | solution.py:119
  142.0 65.2 %copy-start.120 = (s32[128]{0:T(128)S(1)}, s32[128]{0:T(128)}, u32[]{:S(2)}) copy-start(s32[128]{0:T(128)} %copy-done.119) | copy-start | bytes 1540
  142.0 65.5 %copy-start.110 = (s32[1,2,1,64,2]{3,4,2,1,0:T(2,128)S(1)}, s32[1,2,1,64,2]{3,4,2,1,0:T(2,128)}, u32[]{:S(2)}) copy-start(s32[1,2,1,64,2]{3,4,2,1,0:T(2,128)} %param.10) | copy-start | bytes 3076
  153.9 60.6 %copy-start.114 = (f32[64]{0:T(128)S(1)}, f32[64]{0:T(128)}, u32[]{:S(2)}) copy-start(f32[64]{0:T(128)} %copy-done.113) | copy-start | bytes 772
  202.9 11.2 %all-to-all-start.2 = ((bf16[4,36,1536]{2,1,0:T(8,128)(2,1)}), bf16[4,36,1536]{2,1,0:T(8,128)(2,1)S(1)}, u32[]{:S(2)}, u32[]{:S(2)}) async-start(bf16[4,36,1536]{2,1,0:T(8,128)(2,1)} %reshape.273), calls=%async_computation.3 | async-start | bytes 983040 | tf_op jit(solution)/shard_map/all_to_all | solution.py:135
  206.5 83.4 %all-gather.11.cloned.1.call-start = ((), (), s32[]{:S(2)}) async-start(), calls=%async_computation.12 | async-start | bytes 2457600 | tf_op jit(solution)/shard_map/all_gather | solution.py:118
  228.8 148.7 %reduce-scatter.5.cloned.1.call-start = ((), (), s32[]{:S(2)}) async-start(), calls=%async_computation.13 | async-start | bytes 4423680 | tf_op jit(solution)/shard_map/reduce_scatter | solution.py:129
  321.9 18.5 %copy-start.11 = (f32[1536]{0:T(1024)S(1)}, f32[1536]{0:T(1024)}, u32[]{:S(2)}) copy-start(f32[1536]{0:T(1024)} %copy-done.9) | copy-start | bytes 18436
  321.9 18.5 %copy-start.14 = (f32[1536]{0:T(1024)S(1)}, f32[1536]{0:T(1024)}, u32[]{:S(2)}) copy-start(f32[1536]{0:T(1024)} %copy-done.12) | copy-start | bytes 18436
  321.9 18.5 %copy-start.17 = (f32[1536]{0:T(1024)S(1)}, f32[1536]{0:T(1024)}, u32[]{:S(2)}) copy-start(f32[1536]{0:T(1024)} %copy-done.15) | copy-start | bytes 18436
  321.9 18.5 %copy-start.20 = (f32[1536]{0:T(1024)S(1)}, f32[1536]{0:T(1024)}, u32[]{:S(2)}) copy-start(f32[1536]{0:T(1024)} %copy-done.18) | copy-start | bytes 18436
  342.7 185.6 %collective-permute-start = (bf16[64,1536]{1,0:T(8,128)(2,1)}, bf16[64,1536]{1,0:T(8,128)(2,1)}, u32[]{:S(2)}, u32[]{:S(2)}) collective-permute-start(bf16[64,1536]{1,0:T(8,128)(2,1)} %fusion.75), channel_id=1, source_target_pairs={{0,16},{16,0},{1,17},{17,1},{2,18},{18,2},{3,19},{19,3},{4,20},{20... | collective-permute-start | bytes 589832 | tf_op jit(solution)/shard_map/ppermute | solution.py:14
  381.3 25.4 %all-to-all-start.5 = ((bf16[4,36,1536]{2,1,0:T(8,128)(2,1)}), bf16[4,36,1536]{2,1,0:T(8,128)(2,1)}, u32[]{:S(2)}, u32[]{:S(2)}) async-start(bf16[4,36,1536]{2,1,0:T(8,128)(2,1)} %reshape.280), calls=%async_computation.7 | async-start | bytes 983040 | tf_op jit(solution)/shard_map/all_to_all | solution.py:135
  385.5 23.1 %copy-start.118 = (s32[64,2]{0,1:T(2,128)S(1)}, s32[64,2]{0,1:T(2,128)}, u32[]{:S(2)}) copy-start(s32[64,2]{0,1:T(2,128)} %get-tuple-element.128) | copy-start | bytes 1540
  385.5 24.5 %copy-start.112 = (f32[64]{0:T(128)S(1)}, f32[64]{0:T(128)}, u32[]{:S(2)}) copy-start(f32[64]{0:T(128)} %copy-done.111) | copy-start | bytes 772
  385.5 24.6 %copy-start.7 = (f32[64,1536]{1,0:T(8,128)S(1)}, f32[64,1536]{1,0:T(8,128)}, u32[]{:S(2)}) copy-start(f32[64,1536]{1,0:T(8,128)} %get-tuple-element.121) | copy-start | bytes 1179652
  385.5 141.1 %all-reduce.6.cloned.1.call-start = ((), (), s32[]{:S(2)}) async-start(), calls=%async_computation.14 | async-start | bytes 393216 | tf_op jit(solution)/shard_map/psum | solution.py:159
  418.9 109.5 %collective-permute-start.1 = (bf16[64,1536]{1,0:T(8,128)(2,1)S(1)}, bf16[64,1536]{1,0:T(8,128)(2,1)S(1)}, u32[]{:S(2)}, u32[]{:S(2)}) collective-permute-start(bf16[64,1536]{1,0:T(8,128)(2,1)S(1)} %fusion.137), channel_id=1, source_target_pairs={{0,16},{16,0},{1,17},{17,1},{2,18},{18,2},{3,19},{19,3},{4,20},{20... | collective-permute-start | bytes 589832 | tf_op jit(solution)/shard_map/ppermute | solution.py:14
  (118 other events, 1338.8 us)
Sparse Core Ops, SparseCore 0:
  30.6 43.1 all-gather.6
  75.4 42.3 all-gather.4
  135.6 65.2 reduce-scatter.2
  202.2 43.8 all-gather.8
  247.5 42.3 all-gather.10
  312.2 65.2 reduce-scatter.4
  419.0 107.5 all-reduce.5
where the time goes:
time: 541 us; the launch traced here: 537 us
  waiting for transfers between devices  260 us (48%)
  blocking collectives  87.4 us (16%)
  matrix products  82.7 us (15%)
  local copies, waits for them, and re-layouts  45.4 us (8%)
  other arithmetic  26.4 us (5%)
  starting transfers between devices  18.1 us (3%)
  between operations  16.8 us (3%)
    reduce_scatter x2, waiting for transfers between devices, local(): lax.psum_scatter(jnp.dot(pre_grad, up_mat.T, preferred_element_type=jnp.f...  79.3 us
    all_gather x2, waiting for transfers between devices, local(): lax.all_gather(owner_in, 'dp', axis=0, tiled=True)  69.3 us
    psum x1, waiting for transfers between devices, local(): taps_total, gain_total = lax.psum((taps_term, gain_term), ('dp', 'expert'))  54.5 us
    all_gather x2, waiting for transfers between devices, local(): lax.all_gather(owner_grad, 'dp', axis=0, tiled=True)  51.2 us
    psum x1, blocking collectives, local(): taps_total, gain_total = lax.psum((taps_term, gain_term), ('dp', 'expert'))  41.7 us
    all_to_all x2, blocking collectives, local(): lax.all_to_all(send_in, 'expert', split_axis=0, concat_axis=0, tiled=True)  23.7 us
    all_to_all x2, blocking collectives, local(): lax.all_to_all(send_grad, 'expert', split_axis=0, concat_axis=0, tiled=True)  22 us
    dot_general x2, matrix products, local(): jnp.dot(rows_in.T, pre_grad, preferred_element_type=jnp.float32)  20.5 us
  transfers between devices with their start and end apart: 11, of which 8 were waited for; matrix products, arithmetic and copies ran while one was open for 19% of the time, Pallas kernels for 0%

commit v1 on v0

v1 whole, which is shorter than its diff:
```python
import functools

import jax
import jax.numpy as jnp
from jax import lax
from jax.experimental import pallas as pl
from jax.experimental.pallas import tpu as pltpu
from jax.sharding import PartitionSpec as P

MB = 2
EPSILON = 1e-06
LANES = 128
TILE = 256
VMEM_LIMIT = 60 * 1024 * 1024
bf16 = jnp.bfloat16
f32 = jnp.float32


def round_up(value, step):
    return -(-value // step) * step


def params():
    return pltpu.CompilerParams(vmem_limit_bytes=VMEM_LIMIT)


def whole(count):
    return [pl.BlockSpec(memory_space=pltpu.VMEM)] * count


def sigmoid(values):
    return 1.0 / (1.0 + jnp.exp(-values))


def silu_slope(values):
    gate_sig = sigmoid(values)
    return gate_sig * (1.0 + values * (1.0 - gate_sig))


def prologue_body(x_ref, taps_ref, gain_ref, normed_ref, conv_ref, mixed_ref, scale_ref, pad):
    frames, features = x_ref.shape
    tap_count = taps_ref.shape[0]
    margin = tap_count // 2
    lead = round_up(margin, 8)
    pad[...] = jnp.zeros(pad.shape, f32)

    def chunk(c, squares):
        cols = pl.ds(pl.multiple_of(c * LANES, LANES), LANES)
        xs = x_ref[:, cols].astype(f32)
        pad[lead : lead + frames, :] = xs
        acc = jnp.zeros((frames, LANES), f32)
        for j in range(tap_count):
            first = lead + j - margin
            acc = acc + taps_ref[j : j + 1, cols] * pad[first : first + frames, :]
        mixed = xs + acc * sigmoid(acc)
        conv_ref[:, cols] = acc
        mixed_ref[:, cols] = mixed
        return squares + mixed * mixed

    squares = lax.fori_loop(0, features // LANES, chunk, jnp.zeros((frames, LANES), f32))
    scale = lax.rsqrt(jnp.sum(squares, axis=1, keepdims=True) / features + EPSILON)
    scale_ref[...] = scale
    normed_ref[...] = (mixed_ref[...] * scale * gain_ref[...]).astype(bf16)


def prologue(x, taps, gain):
    frames, features = x.shape
    lead = round_up(taps.shape[0] // 2, 8)
    return pl.pallas_call(
        prologue_body,
        out_shape=(
            jax.ShapeDtypeStruct((frames, features), bf16),
            jax.ShapeDtypeStruct((frames, features), f32),
            jax.ShapeDtypeStruct((frames, features), f32),
            jax.ShapeDtypeStruct((frames, 1), f32),
        ),
        in_specs=whole(3),
        out_specs=tuple(whole(4)),
        scratch_shapes=[pltpu.VMEM((frames + 2 * lead, LANES), f32)],
        compiler_params=params(),
        cost_estimate=pl.CostEstimate(flops=4000000, bytes_accessed=2000000, transcendentals=0),
        name="conv_norm",
    )(x, taps, gain)


def slot_rows_body(experts, capacity, frames, weigh, meta_ref, *refs):
    seqs = (len(refs) - experts - 1)
    frame_refs, out_refs, joined = refs[:seqs], refs[seqs : seqs + experts], refs[-1]
    for k in range(seqs):
        joined[k * frames : (k + 1) * frames, :] = frame_refs[k][...]
    total = seqs * frames
    padded = round_up(experts, 16)
    named = lax.broadcasted_iota(jnp.int32, (padded, total), 0).astype(f32)
    first, second = meta_ref[0:1, :] == named, meta_ref[1:2, :] == named
    member = (first | second)
    earlier = lax.broadcasted_iota(jnp.int32, (total, total), 0)
    later = lax.broadcasted_iota(jnp.int32, (total, total), 1)
    before = (earlier < later) & (earlier // frames == later // frames)
    rank = jnp.dot(
        member.astype(f32).astype(bf16),
        before.astype(f32).astype(bf16),
        preferred_element_type=f32,
    )
    seq_of = (lax.broadcasted_iota(jnp.int32, (padded, total), 1) // frames).astype(f32)
    slot = jnp.where(member, rank + seq_of * capacity, -1.0)
    weight = jnp.where(first, meta_ref[2:3, :], 0.0) + jnp.where(second, meta_ref[3:4, :], 0.0)
    rows = out_refs[0].shape[0]
    row_ids = lax.broadcasted_iota(jnp.int32, (rows, total), 0).astype(f32)
    for e in range(experts):
        chosen = row_ids == slot[e : e + 1, :]
        placing = chosen.astype(f32).astype(bf16)
        if weigh:
            amount = jnp.sum(jnp.where(chosen, weight[e : e + 1, :], 0.0), axis=1, keepdims=True)
        for first_col in range(0, joined.shape[1], 512):
            cols = slice(first_col, min(first_col + 512, joined.shape[1]))
            picked = jnp.dot(placing, joined[:, cols], preferred_element_type=f32)
            if weigh:
                picked = picked * amount
            out_refs[e][:, cols] = picked.astype(bf16)


def slot_rows(meta, blocks, experts, capacity, weigh):
    frames, features = blocks[0].shape
    rows = round_up(len(blocks) * capacity, 16)
    return pl.pallas_call(
        functools.partial(slot_rows_body, experts, capacity, frames, weigh),
        out_shape=tuple(jax.ShapeDtypeStruct((rows, features), bf16) for _ in range(experts)),
        in_specs=whole(1 + len(blocks)),
        out_specs=tuple(whole(experts)),
        scratch_shapes=[pltpu.VMEM((len(blocks) * frames, features), bf16)],
        compiler_params=params(),
        cost_estimate=pl.CostEstimate(flops=450000000, bytes_accessed=3000000, transcendentals=0),
        name="slot_rows",
    )(meta, *blocks)


def expert_body(parts, *refs):
    in_refs, grad_refs = refs[:parts], refs[parts : 2 * parts]
    up_ref, down_ref = refs[2 * parts : 2 * parts + 2]
    slot_refs = refs[2 * parts + 2 : 3 * parts + 2]
    rows_in, rows_grad, acted, pre_grad = refs[3 * parts + 2 :]
    rows = in_refs[0].shape[0]
    for j in range(parts):
        rows_in[j * rows : (j + 1) * rows, :] = in_refs[j][...]
        rows_grad[j * rows : (j + 1) * rows, :] = grad_refs[j][...]
    width = up_ref.shape[1]

    def hidden(h, carry):
        cols = pl.ds(pl.multiple_of(h * TILE, TILE), TILE)
        pre_act = jnp.dot(rows_in[...], up_ref[:, cols], preferred_element_type=f32)
        act_grad = lax.dot_general(
            rows_grad[...],
            down_ref[cols, :],
            (((1,), (1,)), ((), ())),
            preferred_element_type=f32,
        )
        gate_sig = sigmoid(pre_act)
        acted[:, cols] = (pre_act * gate_sig).astype(bf16)
        slope = gate_sig * (1.0 + pre_act * (1.0 - gate_sig))
        pre_grad[:, cols] = (act_grad * slope).astype(bf16)
        return carry

    lax.fori_loop(0, width // TILE, hidden, 0)

    def feature(d, carry):
        cols = pl.ds(pl.multiple_of(d * TILE, TILE), TILE)
        term = lax.dot_general(
            pre_grad[...],
            up_ref[cols, :],
            (((1,), (1,)), ((), ())),
            preferred_element_type=f32,
        )
        for j in range(parts):
            slot_refs[j][:, cols] = term[j * rows : (j + 1) * rows, :].astype(bf16)
        return carry

    lax.fori_loop(0, up_ref.shape[0] // TILE, feature, 0)


def expert_products(in_blocks, grad_blocks, up_mat, down_mat):
    parts = len(in_blocks)
    rows, features = in_blocks[0].shape
    hidden = up_mat.shape[1]
    total = parts * rows
    out = pl.pallas_call(
        functools.partial(expert_body, parts),
        out_shape=tuple(jax.ShapeDtypeStruct((rows, features), bf16) for _ in range(parts))
        + (
            jax.ShapeDtypeStruct((total, features), bf16),
            jax.ShapeDtypeStruct((total, features), bf16),
            jax.ShapeDtypeStruct((total, hidden), bf16),
            jax.ShapeDtypeStruct((total, hidden), bf16),
        ),
        in_specs=whole(2 * parts + 2),
        out_specs=tuple(whole(parts + 4)),
        compiler_params=params(),
        cost_estimate=pl.CostEstimate(
            flops=6 * total * features * hidden, bytes_accessed=20000000, transcendentals=total * hidden
        ),
        name="expert_products",
    )(*in_blocks, *grad_blocks, up_mat, down_mat)
    return out[:parts], out[parts:]


def frame_sums_body(experts, seqs, capacity, frames, meta_ref, *refs):
    slot_refs, out_refs, picking = refs[:experts], refs[experts : experts + seqs], refs[-1]
    total = seqs * frames
    padded = round_up(experts, 128)
    named = lax.broadcasted_iota(jnp.int32, (total, padded), 1).astype(f32)
    member = (meta_ref[:, 0:1] == named) | (meta_ref[:, 1:2] == named)
    later = lax.broadcasted_iota(jnp.int32, (total, total), 0)
    earlier = lax.broadcasted_iota(jnp.int32, (total, total), 1)
    before = (earlier < later) & (earlier // frames == later // frames)
    rank = jnp.dot(
        before.astype(f32).astype(bf16),
        member.astype(f32).astype(bf16),
        preferred_element_type=f32,
    )
    seq_of = (lax.broadcasted_iota(jnp.int32, (total, padded), 0) // frames).astype(f32)
    slot = jnp.where(member, rank + seq_of * capacity, -1.0)
    rows = slot_refs[0].shape[0]
    col_ids = lax.broadcasted_iota(jnp.int32, (total, rows), 1).astype(f32)
    for e in range(experts):
        picking[e] = (col_ids == slot[:, e : e + 1]).astype(f32).astype(bf16)

    def feature(d, carry):
        cols = pl.ds(pl.multiple_of(d * TILE, TILE), TILE)
        acc = jnp.zeros((total, TILE), f32)
        for e in range(experts):
            acc = acc + jnp.dot(picking[e], slot_refs[e][:, cols], preferred_element_type=f32)
        for k in range(seqs):
            out_refs[k][:, cols] = acc[k * frames : (k + 1) * frames, :].astype(out_refs[k].dtype)
        return carry

    lax.fori_loop(0, slot_refs[0].shape[1] // TILE, feature, 0)


def frame_sums(meta, blocks, seqs, capacity):
    rows, features = blocks[0].shape
    frames = meta.shape[0] // seqs
    return pl.pallas_call(
        functools.partial(frame_sums_body, len(blocks), seqs, capacity, frames),
        out_shape=tuple(
            jax.ShapeDtypeStruct((frames, features), f32 if k == 0 else bf16) for k in range(seqs)
        ),
        in_specs=whole(1 + len(blocks)),
        out_specs=tuple(whole(seqs)),
        scratch_shapes=[pltpu.VMEM((len(blocks), seqs * frames, rows), bf16)],
        compiler_params=params(),
        cost_estimate=pl.CostEstimate(flops=450000000, bytes_accessed=3000000, transcendentals=0),
        name="frame_sums",
    )(meta, *blocks)


def epilogue_body(seqs, *refs):
    norm_refs = refs[:seqs]
    (x_ref, up_ref, conv_ref, mixed_ref, scale_ref, taps_ref, gain_ref, sums_ref) = refs[seqs : seqs + 8]
    prev_ref, term_ref, norm_grad, pad_x, pad_g = refs[seqs + 8 :]
    frames, features = x_ref.shape
    tap_count = taps_ref.shape[0]
    margin = tap_count // 2
    lead = round_up(margin, 8)
    pad_x[...] = jnp.zeros(pad_x.shape, f32)
    pad_g[...] = jnp.zeros(pad_g.shape, f32)
    scale = scale_ref[...]

    def gather(c, inner):
        cols = pl.ds(pl.multiple_of(c * LANES, LANES), LANES)
        grad = norm_refs[0][:, cols].astype(f32)
        for k in range(1, seqs):
            grad = grad + norm_refs[k][:, cols].astype(f32)
        norm_grad[:, cols] = grad
        weighed = grad * mixed_ref[:, cols]
        term_ref[tap_count : tap_count + 1, cols] = sums_ref[
            tap_count : tap_count + 1, cols
        ] + jnp.sum(weighed * scale, axis=0, keepdims=True)
        return inner + weighed * gain_ref[:, cols]

    inner = lax.fori_loop(0, features // LANES, gather, jnp.zeros((frames, LANES), f32))
    pull = scale * scale * scale * (jnp.sum(inner, axis=1, keepdims=True) / features)

    def chunk(c, carry):
        cols = pl.ds(pl.multiple_of(c * LANES, LANES), LANES)
        mixed_grad = (
            up_ref[:, cols].astype(f32)
            + scale * (norm_grad[:, cols] * gain_ref[:, cols])
            - mixed_ref[:, cols] * pull
        )
        conv_grad = mixed_grad * silu_slope(conv_ref[:, cols])
        pad_x[lead : lead + frames, :] = x_ref[:, cols].astype(f32)
        pad_g[lead : lead + frames, :] = conv_grad
        acc = mixed_grad
        for j in range(tap_count):
            first = lead + j - margin
            term_ref[j : j + 1, cols] = sums_ref[j : j + 1, cols] + jnp.sum(
                conv_grad * pad_x[first : first + frames, :], axis=0, keepdims=True
            )
            first = lead + margin - j
            acc = acc + taps_ref[j : j + 1, cols] * pad_g[first : first + frames, :]
        prev_ref[:, cols] = acc.astype(bf16)
        return carry

    lax.fori_loop(0, features // LANES, chunk, 0)


def epilogue(norm_blocks, x, upstream, conv, mixed, scale, taps, gain, sums):
    frames, features = x.shape
    seqs = len(norm_blocks)
    lead = round_up(taps.shape[0] // 2, 8)
    return pl.pallas_call(
        functools.partial(epilogue_body, seqs),
        out_shape=(
            jax.ShapeDtypeStruct((frames, features), bf16),
            jax.ShapeDtypeStruct((taps.shape[0] + 1, features), f32),
        ),
        in_specs=whole(seqs + 8),
        out_specs=tuple(whole(2)),
        scratch_shapes=[
            pltpu.VMEM((frames, features), f32),
            pltpu.VMEM((frames + 2 * lead, LANES), f32),
            pltpu.VMEM((frames + 2 * lead, LANES), f32),
        ],
        compiler_params=params(),
        cost_estimate=pl.CostEstimate(flops=8000000, bytes_accessed=3000000, transcendentals=0),
        name="norm_conv_back",
    )(*norm_blocks, x, upstream, conv, mixed, scale, taps, gain, sums)


def to_partner(array, axis, k):
    return lax.ppermute(array, axis, [(i, i ^ k) for i in range(lax.axis_size(axis))])


def from_all(array, axis):
    return [array] + [to_partner(array, axis, k) for k in range(1, lax.axis_size(axis))]


def exchanged(blocks, axis):
    return [blocks[0]] + [to_partner(blocks[k], axis, k) for k in range(1, len(blocks))]


def tree_sum(terms):
    while len(terms) > 1:
        terms = [terms[i] + terms[i + 1] for i in range(0, len(terms), 2)]
    return terms[0]


def local(section_input, out_grad, routes, combine, kernel, norm_gain, up_weight, down_weight):
    experts = lax.axis_size("expert")
    seqs = lax.axis_size("dp")
    frames, features = section_input.shape[3:]
    top_count = routes.shape[4]
    capacity = 9 * frames * top_count // (8 * experts)
    taps = kernel[0]
    gain = norm_gain
    up_mat, down_mat = up_weight[0, 0], down_weight[0, 0]
    own = lax.axis_index("expert").astype(jnp.int32)

    relative = (routes[0, :, 0] ^ own).astype(f32)
    meta = jnp.concatenate([relative, combine[0, :, 0]], axis=2)
    metas = jnp.concatenate(from_all(meta, "dp"), axis=1)
    metas_wide = metas.transpose(0, 2, 1)

    xs = [section_input[0, m, 0] for m in range(MB)]
    ups = [out_grad[0, m, 0] for m in range(MB)]
    saved, rows_in, rows_grad = [], [], []
    for m in range(MB):
        normed, *rest = prologue(xs[m], taps, gain)
        saved.append(rest)
        rows_in.append(from_all(normed, "dp"))
        rows_grad.append(from_all(ups[m], "dp"))
    kept, back = [], []
    for m in range(MB):
        in_blocks = exchanged(slot_rows(metas_wide[m], rows_in[m], experts, capacity, False), "expert")
        grad_blocks = exchanged(slot_rows(metas_wide[m], rows_grad[m], experts, capacity, True), "expert")
        slots, rest = expert_products(in_blocks, grad_blocks, up_mat, down_mat)
        kept.append(rest)
        back.append(exchanged(slots, "expert"))
    handed = []
    sums = jnp.zeros((taps.shape[0] + 1, features), f32)
    for m in range(MB):
        norm_blocks = exchanged(frame_sums(metas[m], back[m], seqs, capacity), "dp")
        conv, mixed, scale = saved[m]
        prev, sums = epilogue(norm_blocks, xs[m], ups[m], conv, mixed, scale, taps, gain, sums)
        handed.append(
            lax.ppermute(prev, "pipe", [(i, (i - 1) % lax.axis_size("pipe")) for i in range(lax.axis_size("pipe"))])
        )
    all_in, all_grad, all_acted, all_pre = [jnp.concatenate(a, axis=0) for a in zip(*kept)]
    over_rows = (((0,), (0,)), ((), ()))
    up_grad = lax.dot_general(all_in, all_pre, over_rows, preferred_element_type=f32).astype(bf16)
    down_grad = lax.dot_general(all_acted, all_grad, over_rows, preferred_element_type=f32).astype(bf16)
    for axis in ("expert", "dp"):
        sums = tree_sum(from_all(sums, axis))
    return (
        jnp.stack(handed)[None, :, None],
        sums[:-1][None],
        sums[-1][None],
        up_grad[None, None],
        down_grad[None, None],
    )


def solution(mesh):
    split = P("pipe", None, ("dp", "expert"), None, None)
    up_split = P("pipe", "expert", None, "dp")
    down_split = P("pipe", "expert", "dp", None)
    return jax.shard_map(
        local,
        mesh=mesh,
        in_specs=(split, split, split, split, P("pipe", None, None), P("pipe", None), up_split, down_split),
        out_specs=(split, P("pipe", None, None), P("pipe", None), up_split, down_split),
        check_vma=False,
    )
```

time: 541 us -> 295 us (0.55)
  waiting for transfers between devices: 260 us -> 113 us
  blocking collectives: 87.4 us -> 0 us
  Pallas kernels: 0 us -> 79.2 us
  matrix products: 82.7 us -> 21 us
  starting transfers between devices: 18.1 us -> 64.7 us
  local copies, waits for them, and re-layouts: 45.4 us -> 12.3 us
  other arithmetic: 26.4 us -> 3.07 us
  between operations: 16.8 us -> 0.88 us
    all_gather x4 -> x0, waiting for transfers between devices: 120 us -> none  [the longest x2 69.3 us: local(): lax.all_gather(owner_in, 'dp', axis=0, tiled=True)]
    ppermute x2 -> x47, waiting for transfers between devices: 0.01 us -> 113 us  [the longest x45 113 us: to_partner(): lax.ppermute(array, axis, [(i, i ^ k) for i in range(lax.axis_size(axis))])]
    reduce_scatter x2 -> x0, waiting for transfers between devices: 79.3 us -> none  [local(): lax.psum_scatter(jnp.dot(pre_grad, up_mat.T, preferred_element_type=jnp.f...]
    pallas_call x0 -> x12, Pallas kernels: none -> 79.2 us  [the longest x2 37.5 us: expert_products(): pl.pallas_call(functools.partial(expert_body, parts), out_shape=tuple((ja...]
    ppermute x2 -> x47, starting transfers between devices: 0.07 us -> 64.7 us  [the longest x45 64.2 us: to_partner(): lax.ppermute(array, axis, [(i, i ^ k) for i in range(lax.axis_size(axis))])]
    dot_general x16 -> x2, matrix products: 82.7 us -> 21 us  [the longest x1 10.6 us: local(): lax.dot_general(all_in, all_pre, over_rows, preferred_element_type=f32)]
    psum x1 -> x0, waiting for transfers between devices: 54.5 us -> none  [local(): taps_total, gain_total = lax.psum((taps_term, gain_term), ('dp', 'expert'))]
    all_to_all x4 -> x0, blocking collectives: 45.7 us -> none  [the longest x2 23.7 us: local(): lax.all_to_all(send_in, 'expert', split_axis=0, concat_axis=0, tiled=True)]
  transfers between devices with their start and end apart: 11 -> 47, of which waited for: 8 -> 15; matrix products, arithmetic and copies ran while one was open for 19% -> 9% of each run, Pallas kernels for 0% -> 23%
where the time goes in v1:
time: 295 us; the launch traced here: 294 us
  waiting for transfers between devices  113 us (38%)
  Pallas kernels  79.2 us (27%)
  starting transfers between devices  64.7 us (22%)
  matrix products  21 us (7%)
  local copies, waits for them, and re-layouts  12.3 us (4%)
  other arithmetic  3.07 us (1%)
    ppermute x45, waiting for transfers between devices, to_partner(): lax.ppermute(array, axis, [(i, i ^ k) for i in range(lax.axis_size(axis))])  113 us
    ppermute x45, starting transfers between devices, to_partner(): lax.ppermute(array, axis, [(i, i ^ k) for i in range(lax.axis_size(axis))])  64.2 us
    pallas_call x2, Pallas kernels, expert_products(): pl.pallas_call(functools.partial(expert_body, parts), out_shape=tuple((ja...  37.5 us
    pallas_call x2, Pallas kernels, epilogue(): pl.pallas_call(functools.partial(epilogue_body, seqs), out_shape=(jax.Sha...  14.5 us
    pallas_call x4, Pallas kernels, slot_rows(): pl.pallas_call(functools.partial(slot_rows_body, experts, capacity, frame...  11.5 us
    dot_general x1, matrix products, local(): lax.dot_general(all_in, all_pre, over_rows, preferred_element_type=f32)  10.6 us
    dot_general x1, matrix products, local(): lax.dot_general(all_acted, all_grad, over_rows, preferred_element_type=f32)  10.4 us
    pallas_call x2, Pallas kernels, frame_sums(): pl.pallas_call(functools.partial(frame_sums_body, len(blocks), seqs, capa...  9.2 us
  transfers between devices with their start and end apart: 47, of which 15 were waited for; matrix products, arithmetic and copies ran while one was open for 9% of the time, Pallas kernels for 23%

profile of v1, /device:TPU:0, one launch (start us, length us, event | category | flops | bytes accessed | tf_op | source)
XLA Modules:
  0.0 294.5 jit_solution(7823304579317866385)
XLA Ops:
  4.3 3.3 %conv_norm.3 = (bf16[64,1536]{1,0:T(8,128)(2,1)}, f32[64,1536]{1,0:T(8,128)}, f32[64,1536]{1,0:T(8,128)}, f32[64,1]{1,0:T(8,128)}) custom-call(bf16[64,1536]{1,0:T(8,128)(2,1)} %get-tuple-element.127.x_ref.refs_4_, f32[31,1536]{1,0:T(8,128)} %bitcast.42, f32[1,1536]{1,0:T(1,128)} %refs_10_.3), custom_call_target="tpu_custom_call" | custom-call | flops 4000000 | bytes 2000000 | tf_op jit(solution)/shard_map/conv_norm/pallas_call | solution.py:69
  29.0 4.1 %collective-permute-done.23.refs_2_ = bf16[64,1536]{1,0:T(8,128)(2,1)S(1)} collective-permute-done((bf16[64,1536]{1,0:T(8,128)(2,1)}, bf16[64,1536]{1,0:T(8,128)(2,1)S(1)}, u32[]{:S(2)}, u32[]{:S(2)}) %collective-permute-start.23) | collective-permute-done | bytes 196640 | tf_op jit(solution)/shard_map/ppermute | solution.py:330
  38.2 10.3 %collective-permute-done.4.refs_2_ = bf16[64,1536]{1,0:T(8,128)(2,1)S(1)} collective-permute-done((bf16[64,1536]{1,0:T(8,128)(2,1)}, bf16[64,1536]{1,0:T(8,128)(2,1)S(1)}, u32[]{:S(2)}, u32[]{:S(2)}) %collective-permute-start.4) | collective-permute-done | bytes 196640 | tf_op jit(solution)/shard_map/ppermute | solution.py:330
  53.7 4.5 %collective-permute-start.9 = (bf16[64,1536]{1,0:T(8,128)(2,1)S(1)}, bf16[64,1536]{1,0:T(8,128)(2,1)S(1)}, u32[]{:S(2)}, u32[]{:S(2)}) collective-permute-start(bf16[64,1536]{1,0:T(8,128)(2,1)S(1)} %get-tuple-element.119.refs_0_.refs_5_), channel_id=1, source_target_pairs={{0,4},{4,0},{8,12},{12,8},{1,5},{5,1},{9,13},{13,9},{2,6},{6,2},{1... | collective-permute-start | bytes 589832 | tf_op jit(solution)/shard_map/ppermute | solution.py:330
  60.6 5.5 %collective-permute-done.9.refs_1_ = bf16[64,1536]{1,0:T(8,128)(2,1)S(1)} collective-permute-done((bf16[64,1536]{1,0:T(8,128)(2,1)S(1)}, bf16[64,1536]{1,0:T(8,128)(2,1)S(1)}, u32[]{:S(2)}, u32[]{:S(2)}) %collective-permute-start.9) | collective-permute-done | bytes 196640 | tf_op jit(solution)/shard_map/ppermute | solution.py:330
  66.1 9.3 %collective-permute-done.10.refs_2_ = bf16[64,1536]{1,0:T(8,128)(2,1)S(1)} collective-permute-done((bf16[64,1536]{1,0:T(8,128)(2,1)S(1)}, bf16[64,1536]{1,0:T(8,128)(2,1)S(1)}, u32[]{:S(2)}, u32[]{:S(2)}) %collective-permute-start.10) | collective-permute-done | bytes 196640 | tf_op jit(solution)/shard_map/ppermute | solution.py:330
  82.4 9.9 %collective-permute-done.29.refs_2_ = bf16[64,1536]{1,0:T(8,128)(2,1)S(1)} collective-permute-done((bf16[64,1536]{1,0:T(8,128)(2,1)S(1)}, bf16[64,1536]{1,0:T(8,128)(2,1)S(1)}, u32[]{:S(2)}, u32[]{:S(2)}) %collective-permute-start.29) | collective-permute-done | bytes 196640 | tf_op jit(solution)/shard_map/ppermute | solution.py:330
  100.8 5.7 %collective-permute-done.8.refs_3_ = bf16[144,1536]{1,0:T(8,128)(2,1)S(1)} collective-permute-done((bf16[144,1536]{1,0:T(8,128)(2,1)}, bf16[144,1536]{1,0:T(8,128)(2,1)S(1)}, u32[]{:S(2)}, u32[]{:S(2)}) %collective-permute-start.8) | collective-permute-done | bytes 442400 | tf_op jit(solution)/shard_map/ppermute | solution.py:330
  108.0 8.1 %collective-permute-done.12.refs_5_ = bf16[144,1536]{1,0:T(8,128)(2,1)} collective-permute-done((bf16[144,1536]{1,0:T(8,128)(2,1)}, bf16[144,1536]{1,0:T(8,128)(2,1)}, u32[]{:S(2)}, u32[]{:S(2)}) %collective-permute-start.12) | collective-permute-done | bytes 442400 | tf_op jit(solution)/shard_map/ppermute | solution.py:330
  116.7 11.0 %collective-permute-done.13.refs_6_ = bf16[144,1536]{1,0:T(8,128)(2,1)} collective-permute-done((bf16[144,1536]{1,0:T(8,128)(2,1)}, bf16[144,1536]{1,0:T(8,128)(2,1)}, u32[]{:S(2)}, u32[]{:S(2)}) %collective-permute-start.13) | collective-permute-done | bytes 442400 | tf_op jit(solution)/shard_map/ppermute | solution.py:330
  129.7 18.8 %expert_products.2 = (bf16[144,1536]{1,0:T(8,128)(2,1)}, bf16[144,1536]{1,0:T(8,128)(2,1)}, bf16[144,1536]{1,0:T(8,128)(2,1)}, bf16[144,1536]{1,0:T(8,128)(2,1)}...) custom-call(bf16[144,1536]{1,0:T(8,128)(2,1)} %get-tuple-element.58., ...), custom_call_target="tpu_custom_call" | custom-call | flops 8153726976 | bytes 20000000 | tf_op jit(solution)/shard_map/expert_products/pallas_call | solution.py:185
  152.1 17.1 %collective-permute-done.32.refs_6_ = bf16[144,1536]{1,0:T(8,128)(2,1)} collective-permute-done((bf16[144,1536]{1,0:T(8,128)(2,1)}, bf16[144,1536]{1,0:T(8,128)(2,1)}, u32[]{:S(2)}, u32[]{:S(2)}) %collective-permute-start.32) | collective-permute-done | bytes 442400 | tf_op jit(solution)/shard_map/ppermute | solution.py:330
  169.3 18.8 %expert_products.3 = (bf16[144,1536]{1,0:T(8,128)(2,1)}, bf16[144,1536]{1,0:T(8,128)(2,1)}, bf16[144,1536]{1,0:T(8,128)(2,1)}, bf16[144,1536]{1,0:T(8,128)(2,1)}...) custom-call(bf16[144,1536]{1,0:T(8,128)(2,1)} %get-tuple-element.79., ...), custom_call_target="tpu_custom_call" | custom-call | flops 8153726976 | bytes 20000000 | tf_op jit(solution)/shard_map/expert_products/pallas_call | solution.py:185
  193.4 4.6 %frame_sums.2 = (f32[64,1536]{1,0:T(8,128)}, bf16[64,1536]{1,0:T(8,128)(2,1)}, bf16[64,1536]{1,0:T(8,128)(2,1)}, bf16[64,1536]{1,0:T(8,128)(2,1)}) custom-call(f32[256,4]{1,0:T(8,128)} %bitcast.47, bf16[144,1536]{1,0:T(8,128)(2,1)} %get-tuple-element.66.refs_0_, bf16[144,1536]{1,0:T(8,128)(2,1)} %copy-done.2, bf16[144,1536]{1,0:T(8,128)(2,1)} %copy-done.3, ...), custom_call_target="tpu_custom_call" | custom-call | flops 450000000 | bytes 3000000 | tf_op jit(solution)/shard_map/frame_sums/pallas_call | solution.py:241
  198.0 3.7 %collective-permute-start.18 = (bf16[64,1536]{1,0:T(8,128)(2,1)}, bf16[64,1536]{1,0:T(8,128)(2,1)S(1)}, u32[]{:S(2)}, u32[]{:S(2)}) collective-permute-start(bf16[64,1536]{1,0:T(8,128)(2,1)} %get-tuple-element.71), channel_id=1, source_target_pairs={{0,4},{4,0},{8,12},{12,8},{1,5},{5,1},{9,13},{13,9},{2,6},{6,2},{1... | collective-permute-start | bytes 589832 | tf_op jit(solution)/shard_map/ppermute | solution.py:330
  202.5 4.1 %collective-permute-done.35.refs_2_ = bf16[144,1536]{1,0:T(8,128)(2,1)S(1)} collective-permute-done((bf16[144,1536]{1,0:T(8,128)(2,1)}, bf16[144,1536]{1,0:T(8,128)(2,1)S(1)}, u32[]{:S(2)}, u32[]{:S(2)}) %collective-permute-start.35) | collective-permute-done | bytes 442400 | tf_op jit(solution)/shard_map/ppermute | solution.py:330
  207.5 4.6 %frame_sums.3 = (f32[64,1536]{1,0:T(8,128)}, bf16[64,1536]{1,0:T(8,128)(2,1)}, bf16[64,1536]{1,0:T(8,128)(2,1)}, bf16[64,1536]{1,0:T(8,128)(2,1)}) custom-call(f32[256,4]{1,0:T(8,128)} %bitcast.46, bf16[144,1536]{1,0:T(8,128)(2,1)} %get-tuple-element.87.refs_0_, bf16[144,1536]{1,0:T(8,128)(2,1)} %copy-done.5, bf16[144,1536]{1,0:T(8,128)(2,1)} %copy-done.6, ...), custom_call_target="tpu_custom_call" | custom-call | flops 450000000 | bytes 3000000 | tf_op jit(solution)/shard_map/frame_sums/pallas_call | solution.py:241
  218.9 10.6 %fusion = bf16[1,1,1536,1536]{3,2,1,0:T(8,128)(2,1)} fusion(bf16[576,1536]{1,0:T(8,128)(2,1)} %get-tuple-element.102, bf16[576,1536]{1,0:T(8,128)(2,1)} %get-tuple-element.101, bf16[576,1536]{1,0:T(8,128)(2,1)} %get-tuple-element.104, bf16[576,1536]{1,0:T(8,128)(2,1)} %get-tuple-element.103), kind=kOutput, calls=%fused_computation.2 | convolution fusion | flops 5452333056 | bytes 11796480 | tf_op jit(solution)/shard_map/dot_general | solution.py:389
  229.5 14.3 %collective-permute-done.19.refs_2_ = bf16[64,1536]{1,0:T(8,128)(2,1)S(1)} collective-permute-done((bf16[64,1536]{1,0:T(8,128)(2,1)}, bf16[64,1536]{1,0:T(8,128)(2,1)S(1)}, u32[]{:S(2)}, u32[]{:S(2)}) %collective-permute-start.19) | collective-permute-done | bytes 196640 | tf_op jit(solution)/shard_map/ppermute | solution.py:330
  244.6 7.2 %norm_conv_back.2 = (bf16[64,1536]{1,0:T(8,128)(2,1)}, f32[32,1536]{1,0:T(8,128)}) custom-call(f32[64,1536]{1,0:T(8,128)} %get-tuple-element.70.refs_0_, bf16[64,1536]{1,0:T(8,128)(2,1)} %copy-done.8, bf16[64,1536]{1,0:T(8,128)(2,1)} %copy-done.12, bf16[64,1536]{1,0:T(8,128)(2,1)} %copy-done.13, bf16[64,1536]{1,0:T(8,128)(2,1)} %get-tuple-element.128.x_ref.refs_4_, ...), custom_call_target="tpu_custom_call" | custom-call | flops 8000000 | bytes 3000000 | tf_op jit(solution)/shard_map/norm_conv_back/pallas_call | solution.py:310
  252.7 7.3 %norm_conv_back.3 = (bf16[64,1536]{1,0:T(8,128)(2,1)}, f32[32,1536]{1,0:T(8,128)}) custom-call(f32[64,1536]{1,0:T(8,128)} %get-tuple-element.91.refs_0_, bf16[64,1536]{1,0:T(8,128)(2,1)} %copy-done.9, bf16[64,1536]{1,0:T(8,128)(2,1)} %copy-done.10, bf16[64,1536]{1,0:T(8,128)(2,1)} %copy-done.11, bf16[64,1536]{1,0:T(8,128)(2,1)} %get-tuple-element.127.x_ref.refs_4_, ...), custom_call_target="tpu_custom_call" | custom-call | flops 8000000 | bytes 3000000 | tf_op jit(solution)/shard_map/norm_conv_back/pallas_call | solution.py:310
  263.4 10.4 %fusion.1 = bf16[1,1,1536,1536]{3,2,1,0:T(8,128)(2,1)} fusion(bf16[576,1536]{1,0:T(8,128)(2,1)} %get-tuple-element.106, bf16[576,1536]{1,0:T(8,128)(2,1)} %get-tuple-element.105, bf16[576,1536]{1,0:T(8,128)(2,1)} %get-tuple-element.108, bf16[576,1536]{1,0:T(8,128)(2,1)S(1)} %copy-done.38), kind=kOutput, calls=%fused_computation.3 | convolution fusion | flops 5452333056 | bytes 11796480 | tf_op jit(solution)/shard_map/dot_general | solution.py:390
  274.4 3.6 %collective-permute-start.45 = (f32[32,1536]{1,0:T(8,128)S(1)}, f32[32,1536]{1,0:T(8,128)S(1)}, u32[]{:S(2)}, u32[]{:S(2)}) collective-permute-start(f32[32,1536]{1,0:T(8,128)S(1)} %add_add_fusion.1), channel_id=1, source_target_pairs={{0,8},{4,12},{8,0},{12,4},{1,9},{5,13},{9,1},{13,5},{2,10},{6,14},... | collective-permute-start | bytes 589832 | tf_op jit(solution)/shard_map/ppermute | solution.py:330
  280.2 11.9 %collective-permute-done.45 = f32[32,1536]{1,0:T(8,128)S(1)} collective-permute-done((f32[32,1536]{1,0:T(8,128)S(1)}, f32[32,1536]{1,0:T(8,128)S(1)}, u32[]{:S(2)}, u32[]{:S(2)}) %collective-permute-start.45) | collective-permute-done | bytes 196640 | tf_op jit(solution)/shard_map/ppermute | solution.py:330
  (179 shorter events, 84.8 us)
Async XLA Ops:
  7.5 18.8 %collective-permute-start.22 = (bf16[64,1536]{1,0:T(8,128)(2,1)}, bf16[64,1536]{1,0:T(8,128)(2,1)S(1)}, u32[]{:S(2)}, u32[]{:S(2)}) collective-permute-start(bf16[64,1536]{1,0:T(8,128)(2,1)} %get-tuple-element.78.refs_0_), channel_id=1, source_target_pairs={{0,4},{4,0},{8,12},{12,8},{1,5},{5,1},{9,13},{13,9},{2,6},{6,2},{1... | collective-permute-start | bytes 589832 | tf_op jit(solution)/shard_map/ppermute | solution.py:330
  23.2 25.3 %collective-permute-start.4 = (bf16[64,1536]{1,0:T(8,128)(2,1)}, bf16[64,1536]{1,0:T(8,128)(2,1)S(1)}, u32[]{:S(2)}, u32[]{:S(2)}) collective-permute-start(bf16[64,1536]{1,0:T(8,128)(2,1)} %get-tuple-element.57.refs_0_), channel_id=1, source_target_pairs={{0,8},{4,12},{8,0},{12,4},{1,9},{5,13},{9,1},{13,5},{2,10},{6,14},... | collective-permute-start | bytes 589832 | tf_op jit(solution)/shard_map/ppermute | solution.py:330
  26.3 22.2 %collective-permute-start.5 = (bf16[64,1536]{1,0:T(8,128)(2,1)}, bf16[64,1536]{1,0:T(8,128)(2,1)S(1)}, u32[]{:S(2)}, u32[]{:S(2)}) collective-permute-start(bf16[64,1536]{1,0:T(8,128)(2,1)} %get-tuple-element.57.refs_0_), channel_id=1, source_target_pairs={{0,12},{4,8},{8,4},{12,0},{1,13},{5,9},{9,5},{13,1},{2,14},{6,10},... | collective-permute-start | bytes 589832 | tf_op jit(solution)/shard_map/ppermute | solution.py:330
  36.7 58.5 %collective-permute-start.25 = (bf16[144,1536]{1,0:T(8,128)(2,1)}, bf16[144,1536]{1,0:T(8,128)(2,1)S(1)}, u32[]{:S(2)}, u32[]{:S(2)}) collective-permute-start(bf16[144,1536]{1,0:T(8,128)(2,1)} %get-tuple-element.80), channel_id=1, source_target_pairs={{0,1},{1,0},{2,3},{3,2},{4,5},{5,4},{6,7},{7,6},{8,9},{9,8},{10,11... | collective-permute-start | bytes 1327112 | tf_op jit(solution)/shard_map/ppermute | solution.py:330
  52.2 43.6 %collective-permute-start.6 = (bf16[144,1536]{1,0:T(8,128)(2,1)}, bf16[144,1536]{1,0:T(8,128)(2,1)S(1)}, u32[]{:S(2)}, u32[]{:S(2)}) collective-permute-start(bf16[144,1536]{1,0:T(8,128)(2,1)} %get-tuple-element.59), channel_id=1, source_target_pairs={{0,1},{1,0},{2,3},{3,2},{4,5},{5,4},{6,7},{7,6},{8,9},{9,8},{10,11... | collective-permute-start | bytes 1327112 | tf_op jit(solution)/shard_map/ppermute | solution.py:330
  75.4 18.3 %collective-permute-start.30 = (bf16[64,1536]{1,0:T(8,128)(2,1)S(1)}, bf16[64,1536]{1,0:T(8,128)(2,1)S(1)}, u32[]{:S(2)}, u32[]{:S(2)}) collective-permute-start(bf16[64,1536]{1,0:T(8,128)(2,1)S(1)} %get-tuple-element.120.refs_0_.refs_5_), channel_id=1, source_target_pairs={{0,12},{4,8},{8,4},{12,0},{1,13},{5,9},{9,5},{13,1},{2,14},{6,10},... | collective-permute-start | bytes 589832 | tf_op jit(solution)/shard_map/ppermute | solution.py:330
  80.8 19.4 %collective-permute-start.7 = (bf16[144,1536]{1,0:T(8,128)(2,1)}, bf16[144,1536]{1,0:T(8,128)(2,1)S(1)}, u32[]{:S(2)}, u32[]{:S(2)}) collective-permute-start(bf16[144,1536]{1,0:T(8,128)(2,1)} %get-tuple-element.60), channel_id=1, source_target_pairs={{0,2},{1,3},{2,0},{3,1},{4,6},{5,7},{6,4},{7,5},{8,10},{9,11},{10,... | collective-permute-start | bytes 1327112 | tf_op jit(solution)/shard_map/ppermute | solution.py:330
  93.8 22.4 %collective-permute-start.12 = (bf16[144,1536]{1,0:T(8,128)(2,1)}, bf16[144,1536]{1,0:T(8,128)(2,1)}, u32[]{:S(2)}, u32[]{:S(2)}) collective-permute-start(bf16[144,1536]{1,0:T(8,128)(2,1)} %get-tuple-element.63), channel_id=1, source_target_pairs={{0,1},{1,0},{2,3},{3,2},{4,5},{5,4},{6,7},{7,6},{8,9},{9,8},{10,11... | collective-permute-start | bytes 1327112 | tf_op jit(solution)/shard_map/ppermute | solution.py:330
  95.3 32.4 %collective-permute-start.13 = (bf16[144,1536]{1,0:T(8,128)(2,1)}, bf16[144,1536]{1,0:T(8,128)(2,1)}, u32[]{:S(2)}, u32[]{:S(2)}) collective-permute-start(bf16[144,1536]{1,0:T(8,128)(2,1)} %get-tuple-element.64), channel_id=1, source_target_pairs={{0,2},{1,3},{2,0},{3,1},{4,6},{5,7},{6,4},{7,5},{8,10},{9,11},{10,... | collective-permute-start | bytes 1327112 | tf_op jit(solution)/shard_map/ppermute | solution.py:330
  95.8 31.9 %collective-permute-start.14 = (bf16[144,1536]{1,0:T(8,128)(2,1)}, bf16[144,1536]{1,0:T(8,128)(2,1)}, u32[]{:S(2)}, u32[]{:S(2)}) collective-permute-start(bf16[144,1536]{1,0:T(8,128)(2,1)} %get-tuple-element.65), channel_id=1, source_target_pairs={{0,3},{1,2},{2,1},{3,0},{4,7},{5,6},{6,5},{7,4},{8,11},{9,10},{10,... | collective-permute-start | bytes 1327112 | tf_op jit(solution)/shard_map/ppermute | solution.py:330
  100.2 48.5 %collective-permute-start.26 = (bf16[144,1536]{1,0:T(8,128)(2,1)S(1)}, bf16[144,1536]{1,0:T(8,128)(2,1)S(1)}, u32[]{:S(2)}, u32[]{:S(2)}) collective-permute-start(bf16[144,1536]{1,0:T(8,128)(2,1)S(1)} %copy-done.18), channel_id=1, source_target_pairs={{0,2},{1,3},{2,0},{3,1},{4,6},{5,7},{6,4},{7,5},{8,10},{9,11},{10,... | collective-permute-start | bytes 1327112 | tf_op jit(solution)/shard_map/ppermute | solution.py:330
  106.5 43.6 %collective-permute-start.27 = (bf16[144,1536]{1,0:T(8,128)(2,1)S(1)}, bf16[144,1536]{1,0:T(8,128)(2,1)S(1)}, u32[]{:S(2)}, u32[]{:S(2)}) collective-permute-start(bf16[144,1536]{1,0:T(8,128)(2,1)S(1)} %copy-done.17), channel_id=1, source_target_pairs={{0,3},{1,2},{2,1},{3,0},{4,7},{5,6},{6,5},{7,4},{8,11},{9,10},{10,... | collective-permute-start | bytes 1327112 | tf_op jit(solution)/shard_map/ppermute | solution.py:330
  116.1 33.9 %collective-permute-start.31 = (bf16[144,1536]{1,0:T(8,128)(2,1)}, bf16[144,1536]{1,0:T(8,128)(2,1)}, u32[]{:S(2)}, u32[]{:S(2)}) collective-permute-start(bf16[144,1536]{1,0:T(8,128)(2,1)} %get-tuple-element.84), channel_id=1, source_target_pairs={{0,1},{1,0},{2,3},{3,2},{4,5},{5,4},{6,7},{7,6},{8,9},{9,8},{10,11... | collective-permute-start | bytes 1327112 | tf_op jit(solution)/shard_map/ppermute | solution.py:330
  127.7 41.6 %collective-permute-start.32 = (bf16[144,1536]{1,0:T(8,128)(2,1)}, bf16[144,1536]{1,0:T(8,128)(2,1)}, u32[]{:S(2)}, u32[]{:S(2)}) collective-permute-start(bf16[144,1536]{1,0:T(8,128)(2,1)} %get-tuple-element.85), channel_id=1, source_target_pairs={{0,2},{1,3},{2,0},{3,1},{4,6},{5,7},{6,4},{7,5},{8,10},{9,11},{10,... | collective-permute-start | bytes 1327112 | tf_op jit(solution)/shard_map/ppermute | solution.py:330
  127.7 41.6 %collective-permute-start.33 = (bf16[144,1536]{1,0:T(8,128)(2,1)}, bf16[144,1536]{1,0:T(8,128)(2,1)}, u32[]{:S(2)}, u32[]{:S(2)}) collective-permute-start(bf16[144,1536]{1,0:T(8,128)(2,1)} %get-tuple-element.86), channel_id=1, source_target_pairs={{0,3},{1,2},{2,1},{3,0},{4,7},{5,6},{6,5},{7,4},{8,11},{9,10},{10,... | collective-permute-start | bytes 1327112 | tf_op jit(solution)/shard_map/ppermute | solution.py:330
  148.6 40.0 %collective-permute-start.15 = (bf16[144,1536]{1,0:T(8,128)(2,1)}, bf16[144,1536]{1,0:T(8,128)(2,1)S(1)}, u32[]{:S(2)}, u32[]{:S(2)}) collective-permute-start(bf16[144,1536]{1,0:T(8,128)(2,1)} %get-tuple-element.67), channel_id=1, source_target_pairs={{0,1},{1,0},{2,3},{3,2},{4,5},{5,4},{6,7},{7,6},{8,9},{9,8},{10,11... | collective-permute-start | bytes 1327112 | tf_op jit(solution)/shard_map/ppermute | solution.py:330
  150.0 42.4 %collective-permute-start.16 = (bf16[144,1536]{1,0:T(8,128)(2,1)}, bf16[144,1536]{1,0:T(8,128)(2,1)S(1)}, u32[]{:S(2)}, u32[]{:S(2)}) collective-permute-start(bf16[144,1536]{1,0:T(8,128)(2,1)} %get-tuple-element.68), channel_id=1, source_target_pairs={{0,2},{1,3},{2,0},{3,1},{4,6},{5,7},{6,4},{7,5},{8,10},{9,11},{10,... | collective-permute-start | bytes 1327112 | tf_op jit(solution)/shard_map/ppermute | solution.py:330
  150.1 42.4 %collective-permute-start.17 = (bf16[144,1536]{1,0:T(8,128)(2,1)}, bf16[144,1536]{1,0:T(8,128)(2,1)S(1)}, u32[]{:S(2)}, u32[]{:S(2)}) collective-permute-start(bf16[144,1536]{1,0:T(8,128)(2,1)} %get-tuple-element.69), channel_id=1, source_target_pairs={{0,3},{1,2},{2,1},{3,0},{4,7},{5,6},{6,5},{7,4},{8,11},{9,10},{10,... | collective-permute-start | bytes 1327112 | tf_op jit(solution)/shard_map/ppermute | solution.py:330
  198.0 18.5 %collective-permute-start.18 = (bf16[64,1536]{1,0:T(8,128)(2,1)}, bf16[64,1536]{1,0:T(8,128)(2,1)S(1)}, u32[]{:S(2)}, u32[]{:S(2)}) collective-permute-start(bf16[64,1536]{1,0:T(8,128)(2,1)} %get-tuple-element.71), channel_id=1, source_target_pairs={{0,4},{4,0},{8,12},{12,8},{1,5},{5,1},{9,13},{13,9},{2,6},{6,2},{1... | collective-permute-start | bytes 589832 | tf_op jit(solution)/shard_map/ppermute | solution.py:330
  212.1 39.7 %collective-permute-start.37 = (bf16[64,1536]{1,0:T(8,128)(2,1)}, bf16[64,1536]{1,0:T(8,128)(2,1)S(1)}, u32[]{:S(2)}, u32[]{:S(2)}) collective-permute-start(bf16[64,1536]{1,0:T(8,128)(2,1)} %get-tuple-element.92), channel_id=1, source_target_pairs={{0,4},{4,0},{8,12},{12,8},{1,5},{5,1},{9,13},{13,9},{2,6},{6,2},{1... | collective-permute-start | bytes 589832 | tf_op jit(solution)/shard_map/ppermute | solution.py:330
  212.1 39.8 %collective-permute-start.38 = (bf16[64,1536]{1,0:T(8,128)(2,1)}, bf16[64,1536]{1,0:T(8,128)(2,1)S(1)}, u32[]{:S(2)}, u32[]{:S(2)}) collective-permute-start(bf16[64,1536]{1,0:T(8,128)(2,1)} %get-tuple-element.93), channel_id=1, source_target_pairs={{0,8},{4,12},{8,0},{12,4},{1,9},{5,13},{9,1},{13,5},{2,10},{6,14},... | collective-permute-start | bytes 589832 | tf_op jit(solution)/shard_map/ppermute | solution.py:330
  215.0 36.8 %collective-permute-start.39 = (bf16[64,1536]{1,0:T(8,128)(2,1)}, bf16[64,1536]{1,0:T(8,128)(2,1)S(1)}, u32[]{:S(2)}, u32[]{:S(2)}) collective-permute-start(bf16[64,1536]{1,0:T(8,128)(2,1)} %get-tuple-element.94), channel_id=1, source_target_pairs={{0,12},{4,8},{8,4},{12,0},{1,13},{5,9},{9,5},{13,1},{2,14},{6,10},... | collective-permute-start | bytes 589832 | tf_op jit(solution)/shard_map/ppermute | solution.py:330
  216.5 27.3 %collective-permute-start.19 = (bf16[64,1536]{1,0:T(8,128)(2,1)}, bf16[64,1536]{1,0:T(8,128)(2,1)S(1)}, u32[]{:S(2)}, u32[]{:S(2)}) collective-permute-start(bf16[64,1536]{1,0:T(8,128)(2,1)} %get-tuple-element.72), channel_id=1, source_target_pairs={{0,8},{4,12},{8,0},{12,4},{1,9},{5,13},{9,1},{13,5},{2,10},{6,14},... | collective-permute-start | bytes 589832 | tf_op jit(solution)/shard_map/ppermute | solution.py:330
  216.5 27.3 %collective-permute-start.20 = (bf16[64,1536]{1,0:T(8,128)(2,1)}, bf16[64,1536]{1,0:T(8,128)(2,1)S(1)}, u32[]{:S(2)}, u32[]{:S(2)}) collective-permute-start(bf16[64,1536]{1,0:T(8,128)(2,1)} %get-tuple-element.73), channel_id=1, source_target_pairs={{0,12},{4,8},{8,4},{12,0},{1,13},{5,9},{9,5},{13,1},{2,14},{6,10},... | collective-permute-start | bytes 589832 | tf_op jit(solution)/shard_map/ppermute | solution.py:330
  (62 other events, 967.7 us)

commit v2 on v1

v2 whole, which is shorter than its diff:
```python
import functools

import jax
import jax.numpy as jnp
from jax import lax
from jax.experimental import pallas as pl
from jax.experimental.pallas import tpu as pltpu
from jax.sharding import PartitionSpec as P

MB = 2
EPSILON = 1e-06
LANES = 128
TILE = 512
PART = 256
GATE = -1
MIB = 1024 * 1024
SMALL = pl.CostEstimate(flops=1, bytes_accessed=1, transcendentals=0)
bf16 = jnp.bfloat16
f32 = jnp.float32


def round_up(value, step):
    return -(-value // step) * step


def params(mib):
    return pltpu.CompilerParams(vmem_limit_bytes=mib * MIB)


def whole(count):
    return [pl.BlockSpec(memory_space=pltpu.VMEM)] * count


def after(count):
    return [pl.BlockSpec(memory_space=pl.ANY)] * count


def far(count):
    return [pl.BlockSpec(memory_space=pltpu.HBM)] * count


def fetched(m, sources, targets, sems):
    copies = [
        pltpu.make_async_copy(source.at[m], target, sems.at[i])
        for i, (source, target) in enumerate(zip(sources, targets))
    ]
    for copy in copies:
        copy.start()
    for copy in copies:
        copy.wait()


def fetch_scratch(frames, features):
    return [
        pltpu.VMEM((frames, features), bf16),
        pltpu.VMEM((frames, features), bf16),
        pltpu.SemaphoreType.DMA((2,)),
    ]


def sigmoid(values):
    return 1.0 / (1.0 + jnp.exp(-values))


def silu_slope(values):
    gate_sig = sigmoid(values)
    return gate_sig * (1.0 + values * (1.0 - gate_sig))


def mixed_frames(x_ref, taps_ref, pad, conv_ref, mixed_ref):
    frames, features = x_ref.shape
    tap_count = taps_ref.shape[0]
    margin = tap_count // 2
    lead = round_up(margin, 8)
    pad[...] = jnp.zeros(pad.shape, f32)

    def chunk(c, squares):
        cols = pl.ds(pl.multiple_of(c * LANES, LANES), LANES)
        xs = x_ref[:, cols].astype(f32)
        pad[lead : lead + frames, :] = xs
        acc = jnp.zeros((frames, LANES), f32)
        for j in range(tap_count):
            first = lead + j - margin
            acc = acc + taps_ref[j, :, cols] * pad[first : first + frames, :]
        mixed = xs + acc * sigmoid(acc)
        if conv_ref is not None:
            conv_ref[:, cols] = acc
        mixed_ref[:, cols] = mixed
        return squares + mixed * mixed

    squares = lax.fori_loop(0, features // LANES, chunk, jnp.zeros((frames, LANES), f32))
    return lax.rsqrt(jnp.sum(squares, axis=1, keepdims=True) / features + EPSILON)


def meta_rows(routes_ref, combine_ref, m):
    own = lax.axis_index("expert").astype(jnp.int32)
    rows = [(routes_ref[m] ^ own).astype(f32)]
    left = combine_ref[m]
    for _ in range(3):
        rows.append(left.astype(bf16).astype(f32))
        left = left - rows[-1]
    return jnp.concatenate(rows, axis=0)


def first_send_body(x_all, up_all, routes_ref, combine_ref, taps_ref, gain_ref, send_ref, mixed, pad, x_ref, sems):
    frames = x_ref.shape[0]
    fetched(0, (x_all, up_all), (x_ref, send_ref.at[frames : 2 * frames]), sems)
    scale = mixed_frames(x_ref, taps_ref, pad, None, mixed)
    send_ref[:frames, :] = (mixed[...] * scale * gain_ref[...]).astype(bf16)
    meta = jnp.concatenate([meta_rows(routes_ref, combine_ref, m) for m in range(MB)], axis=0)
    send_ref[2 * frames :, :frames] = meta.astype(bf16)


def first_send(x, upstream, routes, combine, taps, gain):
    _, frames, features = x.shape
    lead = round_up(taps.shape[0] // 2, 8)
    return pl.pallas_call(
        first_send_body,
        out_shape=jax.ShapeDtypeStruct((2 * frames + 8 * MB, features), bf16),
        in_specs=far(2) + whole(4),
        out_specs=whole(1)[0],
        scratch_shapes=[
            pltpu.VMEM((frames, features), f32),
            pltpu.VMEM((frames + 2 * lead, LANES), f32),
            pltpu.VMEM((frames, features), bf16),
            pltpu.SemaphoreType.DMA((2,)),
        ],
        compiler_params=params(16),
        cost_estimate=SMALL,
        name="first_send",
    )(x, upstream, routes, combine, taps, gain)


def second_send_body(experts, capacity, x_all, up_all, routes_ref, combine_ref, taps_ref, gain_ref, _, *refs):
    outs, (mixed, pad, x_ref, joined, sems) = refs[:experts], refs[experts:]
    frames, features = x_ref.shape
    fetched(1, (x_all, up_all), (x_ref, joined.at[frames:]), sems)
    scale = mixed_frames(x_ref, taps_ref, pad, None, mixed)
    joined[:frames, :] = (mixed[...] * scale * gain_ref[...]).astype(bf16)
    slot, weight = slot_map(experts, capacity, frames, meta_rows(routes_ref, combine_ref, 1))
    rows = outs[0].shape[0]
    row_ids = lax.broadcasted_iota(jnp.int32, (rows, frames), 0).astype(f32)
    for e in range(experts):
        normed_row = (row_ids == slot[e : e + 1, :]).astype(f32).astype(bf16)
        chosen = (row_ids - capacity == slot[e : e + 1, :]) & (row_ids >= capacity)
        amount = jnp.sum(jnp.where(chosen, weight[e : e + 1, :], 0.0), axis=1, keepdims=True)
        grad_row = chosen.astype(f32).astype(bf16)
        for first_col in range(0, features, 512):
            cols = slice(first_col, min(first_col + 512, features))
            picked = jnp.dot(grad_row, joined[frames:, cols], preferred_element_type=f32) * amount
            picked = picked + jnp.dot(normed_row, joined[:frames, cols], preferred_element_type=f32)
            outs[e][:, cols] = picked.astype(bf16)


def second_send(x, upstream, routes, combine, taps, gain, experts, capacity, earlier):
    _, frames, features = x.shape
    lead = round_up(taps.shape[0] // 2, 8)
    rows = round_up(2 * capacity, 8)
    return pl.pallas_call(
        functools.partial(second_send_body, experts, capacity),
        out_shape=(jax.ShapeDtypeStruct((rows, features), bf16),) * experts,
        in_specs=far(2) + whole(4) + after(1),
        out_specs=tuple(whole(experts)),
        scratch_shapes=[
            pltpu.VMEM((frames, features), f32),
            pltpu.VMEM((frames + 2 * lead, LANES), f32),
            pltpu.VMEM((frames, features), bf16),
            pltpu.VMEM((2 * frames, features), bf16),
            pltpu.SemaphoreType.DMA((2,)),
        ],
        compiler_params=params(16),
        cost_estimate=SMALL,
        name="second_send",
    )(x, upstream, routes, combine, taps, gain, earlier)


def saved_body(x_ref, taps_ref, _, conv_ref, mixed_ref, scale_ref, pad):
    for m in range(MB):
        scale_ref[m] = mixed_frames(x_ref.at[m], taps_ref, pad, conv_ref.at[m], mixed_ref.at[m])


def saved_frames(x, taps, earlier):
    lead = round_up(taps.shape[0] // 2, 8)
    return pl.pallas_call(
        saved_body,
        out_shape=(
            jax.ShapeDtypeStruct(x.shape, f32),
            jax.ShapeDtypeStruct(x.shape, f32),
            jax.ShapeDtypeStruct(x.shape[:2] + (1,), f32),
        ),
        in_specs=whole(2) + after(1),
        out_specs=tuple(whole(3)),
        scratch_shapes=[pltpu.VMEM((x.shape[1] + 2 * lead, LANES), f32)],
        compiler_params=params(16),
        cost_estimate=SMALL,
        name="saved_frames",
    )(x, taps, earlier)


def stacked_body(*refs):
    for i, ref in enumerate(refs[:-2]):
        refs[-1][i] = ref[...]


def stacked(blocks, earlier):
    return pl.pallas_call(
        stacked_body,
        out_shape=jax.ShapeDtypeStruct((len(blocks),) + blocks[0].shape, blocks[0].dtype),
        in_specs=whole(len(blocks)) + after(1),
        out_specs=whole(1)[0],
        compiler_params=params(16),
        cost_estimate=SMALL,
        name="stacked",
    )(*blocks, earlier)


def slot_map(experts, capacity, frames, meta):
    total = meta.shape[1]
    padded = round_up(experts, 16)
    named = lax.broadcasted_iota(jnp.int32, (padded, total), 0).astype(f32)
    first, second = meta[0:1, :] == named, meta[1:2, :] == named
    member = first | second
    earlier = lax.broadcasted_iota(jnp.int32, (total, total), 0)
    later = lax.broadcasted_iota(jnp.int32, (total, total), 1)
    before = (earlier < later) & (earlier // frames == later // frames)
    rank = jnp.dot(
        member.astype(f32).astype(bf16),
        before.astype(f32).astype(bf16),
        preferred_element_type=f32,
    )
    seq_of = lax.broadcasted_iota(jnp.int32, (padded, total), 1) // frames
    slot = jnp.where(member, rank + (seq_of * capacity).astype(f32), -1.0)
    first_weight = meta[2:3, :] + meta[4:5, :] + meta[6:7, :]
    second_weight = meta[3:4, :] + meta[5:6, :] + meta[7:8, :]
    weight = jnp.where(first, first_weight, 0.0) + jnp.where(second, second_weight, 0.0)
    return slot, weight


def place(slot, weight, joined, out_ref, first_row, rows):
    row_ids = lax.broadcasted_iota(jnp.int32, (rows, slot.shape[1]), 0).astype(f32)
    chosen = row_ids == slot
    placing = chosen.astype(f32).astype(bf16)
    if weight is not None:
        amount = jnp.sum(jnp.where(chosen, weight, 0.0), axis=1, keepdims=True)
    for first_col in range(0, joined.shape[1], 512):
        cols = slice(first_col, min(first_col + 512, joined.shape[1]))
        picked = jnp.dot(placing, joined[:, cols], preferred_element_type=f32)
        if weight is not None:
            picked = picked * amount
        out_ref[first_row : first_row + rows, cols] = picked.astype(bf16)


def slots_body(experts, capacity, frames, *refs):
    seqs = len(refs) - experts - 3
    block_refs, out_refs = refs[:seqs], refs[seqs : seqs + experts]
    slot_ref, joined, meta = refs[seqs + experts :]
    total = seqs * frames
    for k in range(seqs):
        here = slice(k * frames, (k + 1) * frames)
        joined[here, :] = block_refs[k][:frames, :]
        joined[total + k * frames : total + (k + 1) * frames, :] = block_refs[k][frames : 2 * frames, :]
        meta[:, here] = block_refs[k][2 * frames :, :frames].astype(f32)
    slot, weight = slot_map(experts, capacity, frames, meta[:8, :])
    slot_ref[0] = slot
    slot_ref[1] = slot_map(experts, capacity, frames, meta[8:, :])[0]
    rows = out_refs[0].shape[0] // 2
    for e in range(experts):
        place(slot[e : e + 1, :], None, joined.at[:total], out_refs[e], 0, rows)
        place(slot[e : e + 1, :], weight[e : e + 1, :], joined.at[total:], out_refs[e], rows, rows)


def slots(blocks, experts, capacity, frames):
    features = blocks[0].shape[1]
    seqs = len(blocks)
    rows = round_up(seqs * capacity, 16)
    total = seqs * frames
    out = pl.pallas_call(
        functools.partial(slots_body, experts, capacity, frames),
        out_shape=tuple(jax.ShapeDtypeStruct((2 * rows, features), bf16) for _ in range(experts))
        + (jax.ShapeDtypeStruct((MB, round_up(experts, 16), total), f32),),
        in_specs=whole(seqs),
        out_specs=tuple(whole(experts + 1)),
        scratch_shapes=[pltpu.VMEM((2 * total, features), bf16), pltpu.VMEM((8 * MB, total), f32)],
        compiler_params=params(16),
        cost_estimate=SMALL,
        name="slots",
    )(*blocks)
    return out[:experts], out[experts]


def expert_body(parts, rows, capacity, count, *refs):
    in_refs, (up_far, down_far) = refs[:count], refs[count : count + 2]
    slot_refs, far_outs = refs[count + 2 : count + 2 + parts], refs[count + 2 + parts : count + 6 + parts]
    up_mat, down_mat, rows_in, rows_grad, acted, kept, get_sems, put_sems = refs[count + 6 + parts :]
    features, hidden = up_mat.shape
    steps = hidden // TILE

    def hidden_cols(h):
        return pl.ds(pl.multiple_of(h * TILE, TILE), TILE)

    def getting(h):
        cols = hidden_cols(h)
        return (
            pltpu.make_async_copy(up_far.at[:, cols], up_mat.at[:, cols], get_sems.at[0, h]),
            pltpu.make_async_copy(down_far.at[cols, :], down_mat.at[cols, :], get_sems.at[1, h]),
        )

    def putting(h):
        cols = hidden_cols(h)
        return (
            pltpu.make_async_copy(acted.at[:, cols], far_outs[2].at[:, cols], put_sems.at[0, h]),
            pltpu.make_async_copy(kept.at[:, cols], far_outs[3].at[:, cols], put_sems.at[1, h]),
        )

    row_puts = [
        pltpu.make_async_copy(rows_in, far_outs[0], put_sems.at[2, 0]),
        pltpu.make_async_copy(rows_grad, far_outs[1], put_sems.at[2, 1]),
    ]
    for h in range(steps):
        for copy in getting(h):
            copy.start()
    for j in range(parts):
        here = slice(j * rows, (j + 1) * rows)
        if capacity is None:
            rows_in[here, :] = in_refs[j][:rows, :]
            rows_grad[here, :] = in_refs[j][rows:, :]
            continue
        seqs, size = len(in_refs), in_refs[0].shape[1]
        pieces = jnp.concatenate([ref[j] for ref in in_refs], axis=0)
        row = lax.broadcasted_iota(jnp.int32, (rows, seqs * size), 0)
        source = lax.broadcasted_iota(jnp.int32, (rows, seqs * size), 1)
        wanted = (row // capacity) * size + row % capacity
        wanted = jnp.where(row < seqs * capacity, wanted, -size)
        for target, first in ((rows_in, 0), (rows_grad, capacity)):
            moving = (source == wanted + first).astype(f32).astype(bf16)
            target[here, :] = jnp.dot(moving, pieces, preferred_element_type=f32).astype(bf16)
    for copy in row_puts:
        copy.start()

    def forward(h, carry):
        for copy in getting(h):
            copy.wait()
        for first in range(0, TILE, PART):
            cols = pl.ds(pl.multiple_of(h * TILE + first, PART), PART)
            pre_act = jnp.dot(rows_in[...], up_mat[:, cols], preferred_element_type=f32)
            act_grad = lax.dot_general(
                rows_grad[...], down_mat[cols, :], (((1,), (1,)), ((), ())), preferred_element_type=f32
            )
            gate_sig = sigmoid(pre_act)
            acted[:, cols] = (pre_act * gate_sig).astype(bf16)
            slope = gate_sig * (1.0 + pre_act * (1.0 - gate_sig))
            kept[:, cols] = (act_grad * slope).astype(bf16)
        for copy in putting(h):
            copy.start()
        return carry

    lax.fori_loop(0, steps, forward, 0)

    def backward(d, carry):
        for first in range(0, TILE, PART):
            cols = pl.ds(pl.multiple_of(d * TILE + first, PART), PART)
            term = lax.dot_general(
                kept[...], up_mat[cols, :], (((1,), (1,)), ((), ())), preferred_element_type=f32
            )
            for j in range(parts):
                slot_refs[j][:, cols] = term[j * rows : (j + 1) * rows, :].astype(bf16)
        return carry

    lax.fori_loop(0, features // TILE, backward, 0)
    for copy in row_puts:
        copy.wait()
    for h in range(steps):
        for copy in putting(h):
            copy.wait()


def expert_products(blocks, parts, seqs, capacity, up_mat, down_mat):
    features, hidden = up_mat.shape
    rows = round_up(seqs * capacity, 16)
    total = parts * rows
    steps = hidden // TILE
    out = pl.pallas_call(
        functools.partial(
            expert_body, parts, rows, capacity if blocks[0].ndim == 3 else None, len(blocks)
        ),
        out_shape=tuple(jax.ShapeDtypeStruct((rows, features), bf16) for _ in range(parts))
        + (
            pltpu.HBM((total, features), bf16),
            pltpu.HBM((total, features), bf16),
            pltpu.HBM((total, hidden), bf16),
            pltpu.HBM((total, hidden), bf16),
        ),
        in_specs=whole(len(blocks)) + far(2),
        out_specs=tuple(whole(parts) + far(4)),
        scratch_shapes=[
            pltpu.VMEM((features, hidden), bf16),
            pltpu.VMEM((hidden, features), bf16),
            pltpu.VMEM((total, features), bf16),
            pltpu.VMEM((total, features), bf16),
            pltpu.VMEM((total, hidden), bf16),
            pltpu.VMEM((total, hidden), bf16),
            pltpu.SemaphoreType.DMA((2, steps)),
            pltpu.SemaphoreType.DMA((3, max(2, steps))),
        ],
        compiler_params=params(54),
        cost_estimate=SMALL,
        name="expert_products",
    )(*blocks, up_mat, down_mat)
    return out[:parts], out[parts:]


def frame_sums_body(m, experts, seqs, frames, slot_ref, *refs):
    slot_refs, out_refs, picking = refs[:experts], refs[-1 - seqs : -1], refs[-1]
    total = seqs * frames
    rows = slot_refs[0].shape[0]
    same = lax.broadcasted_iota(jnp.int32, (total, total), 0) == lax.broadcasted_iota(
        jnp.int32, (total, total), 1
    )
    columns = lax.dot_general(
        same.astype(f32).astype(bf16),
        slot_ref[m].astype(bf16),
        (((1,), (1,)), ((), ())),
        preferred_element_type=f32,
    )
    col_ids = lax.broadcasted_iota(jnp.int32, (total, rows), 1).astype(f32)
    for e in range(experts):
        picking[e] = (col_ids == columns[:, e : e + 1]).astype(f32).astype(bf16)

    def feature(d, carry):
        cols = pl.ds(pl.multiple_of(d * PART, PART), PART)
        acc = jnp.zeros((total, PART), f32)
        for e in range(experts):
            acc = acc + jnp.dot(picking[e], slot_refs[e][:, cols], preferred_element_type=f32)
        for k in range(seqs):
            out_refs[k][:, cols] = acc[k * frames : (k + 1) * frames, :].astype(out_refs[k].dtype)
        return carry

    lax.fori_loop(0, slot_refs[0].shape[1] // PART, feature, 0)


def frame_sums(m, slot, blocks, seqs, earlier, handed=()):
    rows, features = blocks[0].shape
    frames = slot.shape[2] // seqs
    first = 1 + len(blocks) + len(earlier)
    out = pl.pallas_call(
        functools.partial(frame_sums_body, m, len(blocks), seqs, frames),
        out_shape=tuple(pltpu.HBM(h.shape, h.dtype) for h in handed)
        + tuple(
            jax.ShapeDtypeStruct((frames, features), f32 if k == 0 else bf16) for k in range(seqs)
        ),
        in_specs=whole(1 + len(blocks)) + after(len(earlier)) + far(len(handed)),
        out_specs=tuple(far(len(handed)) + whole(seqs)),
        input_output_aliases={first + i: i for i in range(len(handed))},
        scratch_shapes=[pltpu.VMEM((len(blocks), seqs * frames, rows), bf16)],
        compiler_params=params(16),
        cost_estimate=SMALL,
        name="frame_sums",
    )(slot, *blocks, *earlier, *handed)
    return out[: len(handed)], out[len(handed) :]


def epilogue_body(m, seqs, last, *refs):
    norm_refs = refs[:seqs]
    (x_all, up_all, conv_ref, mixed_ref, scale_ref, taps_ref, gain_ref) = refs[seqs : seqs + 7]
    if last:
        sums_ref, other_ref, prev_ref, term_ref, norm_grad, pad_x, pad_g, x_ref, up_ref, sems = refs[seqs + 7 :]
        prev_ref[0] = other_ref[...]
        prev_ref = prev_ref.at[1]
    else:
        prev_ref, term_ref, norm_grad, pad_x, pad_g, x_ref, up_ref, sems = refs[seqs + 7 :]
    fetched(m, (x_all, up_all), (x_ref, up_ref), sems)
    conv_ref, mixed_ref, scale_ref = conv_ref.at[m], mixed_ref.at[m], scale_ref.at[m]
    frames, features = x_ref.shape
    tap_count = taps_ref.shape[0]
    margin = tap_count // 2
    lead = round_up(margin, 8)
    pad_x[...] = jnp.zeros(pad_x.shape, f32)
    pad_g[...] = jnp.zeros(pad_g.shape, f32)
    scale = scale_ref[...]

    def put(row, cols, value):
        if last:
            value = value + sums_ref[row : row + 1, cols]
        term_ref[row : row + 1, cols] = value.astype(term_ref.dtype)

    def gather(c, inner):
        cols = pl.ds(pl.multiple_of(c * LANES, LANES), LANES)
        grad = norm_refs[0][:, cols].astype(f32)
        for k in range(1, seqs):
            grad = grad + norm_refs[k][:, cols].astype(f32)
        norm_grad[:, cols] = grad
        weighed = grad * mixed_ref[:, cols]
        put(tap_count, cols, jnp.sum(weighed * scale, axis=0, keepdims=True))
        return inner + weighed * gain_ref[:, cols]

    inner = lax.fori_loop(0, features // LANES, gather, jnp.zeros((frames, LANES), f32))
    pull = scale * scale * scale * (jnp.sum(inner, axis=1, keepdims=True) / features)

    def chunk(c, carry):
        cols = pl.ds(pl.multiple_of(c * LANES, LANES), LANES)
        mixed_grad = (
            up_ref[:, cols].astype(f32)
            + scale * (norm_grad[:, cols] * gain_ref[:, cols])
            - mixed_ref[:, cols] * pull
        )
        conv_grad = mixed_grad * silu_slope(conv_ref[:, cols])
        pad_x[lead : lead + frames, :] = x_ref[:, cols].astype(f32)
        pad_g[lead : lead + frames, :] = conv_grad
        acc = mixed_grad
        for j in range(tap_count):
            first = lead + j - margin
            put(j, cols, jnp.sum(conv_grad * pad_x[first : first + frames, :], axis=0, keepdims=True))
            first = lead + margin - j
            acc = acc + taps_ref[j, :, cols] * pad_g[first : first + frames, :]
        prev_ref[:, cols] = acc.astype(bf16)
        return carry

    lax.fori_loop(0, features // LANES, chunk, 0)


def epilogue(m, norm_blocks, x, upstream, saved, taps, gain, *before):
    _, frames, features = x.shape
    seqs = len(norm_blocks)
    lead = round_up(taps.shape[0] // 2, 8)
    last = bool(before)
    return pl.pallas_call(
        functools.partial(epilogue_body, m, seqs, last),
        out_shape=(
            jax.ShapeDtypeStruct(x.shape if last else (frames, features), bf16),
            jax.ShapeDtypeStruct((taps.shape[0] + 1, features), bf16 if last else f32),
        ),
        in_specs=whole(seqs) + far(2) + whole(5 + len(before)),
        out_specs=tuple(whole(2)),
        scratch_shapes=[
            pltpu.VMEM((frames, features), f32),
            pltpu.VMEM((frames + 2 * lead, LANES), f32),
            pltpu.VMEM((frames + 2 * lead, LANES), f32),
        ]
        + fetch_scratch(frames, features),
        compiler_params=params(16),
        cost_estimate=SMALL,
        name="norm_conv_back",
    )(*norm_blocks, x, upstream, *saved, taps, gain, *before)


def tree_sum(terms):
    while len(terms) > 1:
        terms = [terms[i] + terms[i + 1] for i in range(0, len(terms), 2)]
    return terms[0]


def last_sum_body(*refs):
    term_refs, taps_ref, gain_ref = refs[:-2], refs[-2], refs[-1]
    tap_count = taps_ref.shape[0]
    total = tree_sum([ref[...].astype(f32) for ref in term_refs])
    for j in range(tap_count):
        taps_ref[j] = total[j : j + 1, :]
    gain_ref[...] = total[tap_count:, :]


def last_sum(terms):
    rows, features = terms[0].shape
    return pl.pallas_call(
        last_sum_body,
        out_shape=(
            jax.ShapeDtypeStruct((rows - 1, 1, features), f32),
            jax.ShapeDtypeStruct((1, features), f32),
        ),
        in_specs=whole(len(terms)),
        out_specs=tuple(whole(2)),
        compiler_params=params(16),
        cost_estimate=SMALL,
        name="last_sum",
    )(*terms)


def to_partner(array, axis, k):
    return lax.ppermute(array, axis, [(i, i ^ k) for i in range(lax.axis_size(axis))])


def from_all(array, axis):
    held = [array]
    for k in range(1, lax.axis_size(axis)):
        low = k & -k
        held.append(to_partner(held[k - low], axis, low))
    return held


def exchanged(blocks, axis):
    return [blocks[0]] + [to_partner(blocks[k], axis, k) for k in range(1, len(blocks))]


def local(section_input, out_grad, routes, combine, kernel, norm_gain, up_weight, down_weight):
    experts = lax.axis_size("expert")
    seqs = lax.axis_size("dp")
    frames, features = section_input.shape[3:]
    top_count = routes.shape[4]
    capacity = 9 * frames * top_count // (8 * experts)
    taps = kernel.transpose(1, 0, 2)
    up_mat, down_mat = up_weight[0, 0], down_weight[0, 0]
    routes = routes[0, :, 0].transpose(0, 2, 1)
    combine = combine[0, :, 0].transpose(0, 2, 1)
    xs = section_input.reshape(MB, frames, features)
    ups = out_grad.reshape(MB, frames, features)

    first = from_all(first_send(xs, ups, routes, combine, taps, norm_gain), "dp")
    pieces = second_send(xs, ups, routes, combine, taps, norm_gain, experts, capacity, first[1])
    saved = saved_frames(xs, taps, pieces[0])
    pieces = from_all(stacked(exchanged(pieces, "expert"), first[GATE]), "dp")
    blocks, slot = slots(first, experts, capacity, frames)
    blocks = exchanged(blocks, "expert")
    back, first_kept = expert_products(blocks, experts, seqs, capacity, up_mat, down_mat)
    first_back = exchanged(back, "expert")
    back, second_kept = expert_products(pieces, experts, seqs, capacity, up_mat, down_mat)
    second_back = exchanged(back, "expert")

    second_kept, sent = frame_sums(0, slot, first_back, seqs, [back[0]], second_kept)
    first_norm = exchanged(sent, "dp")
    all_in, all_grad, all_acted, all_pre = [
        jnp.concatenate(a, axis=0) for a in zip(first_kept, second_kept)
    ]
    over_rows = (((0,), (0,)), ((), ()))
    up_grad = lax.dot_general(all_in, all_pre, over_rows, preferred_element_type=f32).astype(bf16)
    down_grad = lax.dot_general(all_acted, all_grad, over_rows, preferred_element_type=f32).astype(bf16)
    _, sent = frame_sums(1, slot, second_back, seqs, [up_grad, down_grad])
    second_norm = exchanged(sent, "dp")
    before = epilogue(0, first_norm, xs, ups, saved, taps, norm_gain)
    prev, sums = epilogue(1, second_norm, xs, ups, saved, taps, norm_gain, before[1], before[0])
    peers = lax.axis_size("pipe")
    handed = lax.ppermute(prev, "pipe", [(i, (i - 1) % peers) for i in range(peers)])
    sums = tree_sum([term.astype(f32) for term in from_all(sums, "expert")]).astype(bf16)
    taps_grad, gain_grad = last_sum(from_all(sums, "dp"))
    return (
        handed[None, :, None],
        taps_grad.transpose(1, 0, 2),
        gain_grad,
        up_grad[None, None],
        down_grad[None, None],
    )


def solution(mesh):
    split = P("pipe", None, ("dp", "expert"), None, None)
    up_split = P("pipe", "expert", None, "dp")
    down_split = P("pipe", "expert", "dp", None)
    return jax.shard_map(
        local,
        mesh=mesh,
        in_specs=(split, split, split, split, P("pipe", None, None), P("pipe", None), up_split, down_split),
        out_specs=(split, P("pipe", None, None), P("pipe", None), up_split, down_split),
        check_vma=False,
    )
```

time: 295 us -> 205 us (0.69)
  waiting for transfers between devices: 113 us -> 78.4 us
  Pallas kernels: 79.2 us -> 55 us
  starting transfers between devices: 64.7 us -> 43.7 us
  matrix products: 21 us -> 15.4 us
  other arithmetic: 3.07 us -> 0.05 us
    ppermute x45 -> x30, waiting for transfers between devices: 113 us -> 78.4 us  [to_partner(): lax.ppermute(array, axis, [(i, i ^ k) for i in range(lax.axis_size(axis))])]
    pallas_call x12, Pallas kernels: 79.2 us -> 55 us  [the longest x2 31.3 us: expert_products(): pl.pallas_call(functools.partial(expert_body, parts, rows, capacity if bl...]
    ppermute x45 -> x30, starting transfers between devices: 64.2 us -> 43.7 us  [to_partner(): lax.ppermute(array, axis, [(i, i ^ k) for i in range(lax.axis_size(axis))])]
    dot_general x1, matrix products: 10.4 us -> 6.64 us  [local(): lax.dot_general(all_acted, all_grad, over_rows, preferred_element_type=f32)]
    unnamed x82 -> x59, local copies, waits for them, and re-layouts: 8.24 us -> 10.8 us
  transfers between devices with their start and end apart: 47 -> 31, of which waited for: 15 -> 10; matrix products, arithmetic and copies ran while one was open for 9% -> 8% of each run, Pallas kernels for 23% -> 23%
where the time goes in v2:
time: 205 us; the launch traced here: 204 us
  waiting for transfers between devices  78.4 us (38%)
  Pallas kernels  55 us (27%)
  starting transfers between devices  43.7 us (21%)
  matrix products  15.4 us (8%)
  local copies, waits for them, and re-layouts  10.8 us (5%)
    ppermute x30, waiting for transfers between devices, to_partner(): lax.ppermute(array, axis, [(i, i ^ k) for i in range(lax.axis_size(axis))])  78.4 us
    ppermute x30, starting transfers between devices, to_partner(): lax.ppermute(array, axis, [(i, i ^ k) for i in range(lax.axis_size(axis))])  43.7 us
    pallas_call x2, Pallas kernels, expert_products(): pl.pallas_call(functools.partial(expert_body, parts, rows, capacity if bl...  31.3 us
    unnamed x59, local copies, waits for them, and re-layouts  10.8 us
    pallas_call x2, Pallas kernels, epilogue(): pl.pallas_call(functools.partial(epilogue_body, m, seqs, last), out_shape...  10.6 us
    dot_general x1, matrix products, local(): lax.dot_general(all_in, all_pre, over_rows, preferred_element_type=f32)  8.73 us
    dot_general x1, matrix products, local(): lax.dot_general(all_acted, all_grad, over_rows, preferred_element_type=f32)  6.64 us
    pallas_call x2, Pallas kernels, frame_sums(): pl.pallas_call(functools.partial(frame_sums_body, m, len(blocks), seqs, f...  4.17 us
  transfers between devices with their start and end apart: 31, of which 10 were waited for; matrix products, arithmetic and copies ran while one was open for 8% of the time, Pallas kernels for 23%

profile of v2, /device:TPU:0, one launch (start us, length us, event | category | flops | bytes accessed | tf_op | source)
XLA Modules:
  0.0 204.4 jit_solution(10960730057013709092)
XLA Ops:
  7.4 4.1 %collective-permute-start.1 = (bf16[144,1536]{1,0:T(8,128)(2,1)S(1)}, bf16[144,1536]{1,0:T(8,128)(2,1)S(1)}, u32[]{:S(2)}, u32[]{:S(2)}) collective-permute-start(bf16[144,1536]{1,0:T(8,128)(2,1)S(1)} %first_send.1.refs_0_), channel_id=1, source_target_pairs={{0,8},{4,12},{8,0},{12,4},{1,9},{5,13},{9,1},{13,5},{2,10},{6,14},... | collective-permute-start | bytes 1327112 | tf_op jit(solution)/shard_map/ppermute | solution.py:578
  13.1 18.2 %collective-permute-done.1.refs_2_ = bf16[144,1536]{1,0:T(8,128)(2,1)S(1)} collective-permute-done((bf16[144,1536]{1,0:T(8,128)(2,1)S(1)}, bf16[144,1536]{1,0:T(8,128)(2,1)S(1)}, u32[]{:S(2)}, u32[]{:S(2)}) %collective-permute-start.1) | collective-permute-done | bytes 442400 | tf_op jit(solution)/shard_map/ppermute | solution.py:578
  31.9 2.5 %second_send.1 = (bf16[72,1536]{1,0:T(8,128)(2,1)S(1)}, bf16[72,1536]{1,0:T(8,128)(2,1)S(1)}, bf16[72,1536]{1,0:T(8,128)(2,1)S(1)}, bf16[72,1536]{1,0:T(8,128)(2,1)S(1)}) custom-call(bf16[2,64,1536]{2,1,0:T(8,128)(2,1)S(1)} %bitcast.18, bf16[2,64,1536]{2,1,0:T(8,128)(2,1)S(1)} %bitcast.23, s32[2,2,64]{2,1,0:T(2,128)S(1)} %bitcast.34, ...), custom_call_target="tpu_custom_call" | custom-call | flops 1 | bytes 1 | tf_op jit(solution)/shard_map/second_send/pallas_call | solution.py:159
  37.9 4.8 %collective-permute-done.3.refs_1_ = bf16[72,1536]{1,0:T(8,128)(2,1)S(1)} collective-permute-done((bf16[72,1536]{1,0:T(8,128)(2,1)S(1)}, bf16[72,1536]{1,0:T(8,128)(2,1)S(1)}, u32[]{:S(2)}, u32[]{:S(2)}) %collective-permute-start.3) | collective-permute-done | bytes 221216 | tf_op jit(solution)/shard_map/ppermute | solution.py:578
  42.8 4.7 %collective-permute-done.4.refs_2_ = bf16[72,1536]{1,0:T(8,128)(2,1)S(1)} collective-permute-done((bf16[72,1536]{1,0:T(8,128)(2,1)S(1)}, bf16[72,1536]{1,0:T(8,128)(2,1)S(1)}, u32[]{:S(2)}, u32[]{:S(2)}) %collective-permute-start.4) | collective-permute-done | bytes 221216 | tf_op jit(solution)/shard_map/ppermute | solution.py:578
  47.6 3.4 %collective-permute-start.7 = (bf16[4,72,1536]{2,1,0:T(8,128)(2,1)S(1)}, bf16[4,72,1536]{2,1,0:T(8,128)(2,1)S(1)}, u32[]{:S(2)}, u32[]{:S(2)}) collective-permute-start(bf16[4,72,1536]{2,1,0:T(8,128)(2,1)S(1)} %stacked.1.refs_0_), channel_id=1, source_target_pairs={{0,8},{4,12},{8,0},{12,4},{1,9},{5,13},{9,1},{13,5},{2,10},{6,14},... | collective-permute-start | bytes 2654216 | tf_op jit(solution)/shard_map/ppermute | solution.py:578
  57.0 31.5 %collective-permute-done.7.refs_2_ = bf16[4,72,1536]{2,1,0:T(8,128)(2,1)S(1)} collective-permute-done((bf16[4,72,1536]{2,1,0:T(8,128)(2,1)S(1)}, bf16[4,72,1536]{2,1,0:T(8,128)(2,1)S(1)}, u32[]{:S(2)}, u32[]{:S(2)}) %collective-permute-start.7) | collective-permute-done | bytes 884768 | tf_op jit(solution)/shard_map/ppermute | solution.py:578
  88.5 4.7 %collective-permute-done.13.refs_2_ = bf16[288,1536]{1,0:T(8,128)(2,1)S(1)} collective-permute-done((bf16[288,1536]{1,0:T(8,128)(2,1)S(1)}, bf16[288,1536]{1,0:T(8,128)(2,1)S(1)}, u32[]{:S(2)}, u32[]{:S(2)}) %collective-permute-start.13) | collective-permute-done | bytes 884768 | tf_op jit(solution)/shard_map/ppermute | solution.py:578
  94.5 16.2 %expert_products.3 = (bf16[144,1536]{1,0:T(8,128)(2,1)}, bf16[144,1536]{1,0:T(8,128)(2,1)}, bf16[144,1536]{1,0:T(8,128)(2,1)}, bf16[144,1536]{1,0:T(8,128)(2,1)}...) custom-call(bf16[288,1536]{1,0:T(8,128)(2,1)} %copy-done.11, ...), custom_call_target="tpu_custom_call" | custom-call | flops 1 | bytes 1 | tf_op jit(solution)/shard_map/expert_products/pallas_call | solution.py:382
  112.3 2.1 %collective-permute-start.17 = (bf16[144,1536]{1,0:T(8,128)(2,1)}, bf16[144,1536]{1,0:T(8,128)(2,1)S(1)}, u32[]{:S(2)}, u32[]{:S(2)}) collective-permute-start(bf16[144,1536]{1,0:T(8,128)(2,1)} %get-tuple-element.68), channel_id=1, source_target_pairs={{0,3},{1,2},{2,1},{3,0},{4,7},{5,6},{6,5},{7,4},{8,11},{9,10},{10,... | collective-permute-start | bytes 1327112 | tf_op jit(solution)/shard_map/ppermute | solution.py:578
  116.2 15.1 %expert_products.2 = (bf16[144,1536]{1,0:T(8,128)(2,1)}, bf16[144,1536]{1,0:T(8,128)(2,1)}, bf16[144,1536]{1,0:T(8,128)(2,1)}, bf16[144,1536]{1,0:T(8,128)(2,1)}...) custom-call(bf16[4,72,1536]{2,1,0:T(8,128)(2,1)} %copy-done.8, ...), custom_call_target="tpu_custom_call" | custom-call | flops 1 | bytes 1 | tf_op jit(solution)/shard_map/expert_products/pallas_call | solution.py:382
  139.0 8.7 %convolution_convert_fusion.1.refs_4_ = bf16[1536,1536]{1,0:T(8,128)(2,1)S(1)} fusion(bf16[576,1536]{1,0:T(8,128)(2,1)} %get-tuple-element.73, bf16[576,1536]{1,0:T(8,128)(2,1)S(1)} %copy-done.27, bf16[576,1536]{1,0:T(8,128)(2,1)} %get-tuple-element.75, bf16[576,1536]{1,0:T(8,128)(2,1)S(1)} %copy-done.28), kind=kOutput, calls=%fused_computation.1 | convolution fusion | flops 5452333056 | bytes 11796480 | tf_op jit(solution)/shard_map/dot_general | solution.py:623
  147.8 6.6 %convolution_convert_fusion.refs_5_ = bf16[1536,1536]{1,0:T(8,128)(2,1)S(1)} fusion(bf16[576,1536]{1,0:T(8,128)(2,1)S(1)} %copy-done.18, bf16[576,1536]{1,0:T(8,128)(2,1)S(1)} %copy-done.26, bf16[576,1536]{1,0:T(8,128)(2,1)S(1)} %copy-done.17, bf16[576,1536]{1,0:T(8,128)(2,1)S(1)} %copy-done.25), kind=kOutput, calls=%fused_computation | convolution fusion | flops 5452333056 | bytes 11796480 | tf_op jit(solution)/shard_map/dot_general | solution.py:624
  154.5 3.5 %collective-permute-start.23 = (bf16[64,1536]{1,0:T(8,128)(2,1)S(1)}, bf16[64,1536]{1,0:T(8,128)(2,1)S(1)}, u32[]{:S(2)}, u32[]{:S(2)}) collective-permute-start(bf16[64,1536]{1,0:T(8,128)(2,1)S(1)} %get-tuple-element.90), channel_id=1, source_target_pairs={{0,12},{4,8},{8,4},{12,0},{1,13},{5,9},{9,5},{13,1},{2,14},{6,10},... | collective-permute-start | bytes 589832 | tf_op jit(solution)/shard_map/ppermute | solution.py:578
  161.2 3.5 %collective-permute-start.20 = (bf16[64,1536]{1,0:T(8,128)(2,1)S(1)}, bf16[64,1536]{1,0:T(8,128)(2,1)S(1)}, u32[]{:S(2)}, u32[]{:S(2)}) collective-permute-start(bf16[64,1536]{1,0:T(8,128)(2,1)S(1)} %get-tuple-element.83), channel_id=1, source_target_pairs={{0,12},{4,8},{8,4},{12,0},{1,13},{5,9},{9,5},{13,1},{2,14},{6,10},... | collective-permute-start | bytes 589832 | tf_op jit(solution)/shard_map/ppermute | solution.py:578
  164.7 2.5 %saved_frames.1 = (f32[2,64,1536]{2,1,0:T(8,128)S(1)}, f32[2,64,1536]{2,1,0:T(8,128)S(1)}, f32[2,64,1]{2,1,0:T(8,128)S(1)}) custom-call(bf16[2,64,1536]{2,1,0:T(8,128)(2,1)S(1)} %bitcast.19, f32[31,1,1536]{2,1,0:T(1,128)S(1)} %bitcast.28, bf16[72,1536]{1,0:T(8,128)(2,1)S(1)} %get-tuple-element.52.refs_0_._), custom_call_target="tpu_custom_call" | custom-call | flops 1 | bytes 1 | tf_op jit(solution)/shard_map/saved_frames/pallas_call | solution.py:184
  167.3 5.1 %norm_conv_back.2 = (bf16[64,1536]{1,0:T(8,128)(2,1)S(1)}, f32[32,1536]{1,0:T(8,128)S(1)}) custom-call(f32[64,1536]{1,0:T(8,128)S(1)} %get-tuple-element.87.refs_0_, bf16[64,1536]{1,0:T(8,128)(2,1)S(1)} %collective-permute-done.21.refs_1_, bf16[64,1536]{1,0:T(8,128)(2,1)S(1)} %collective-permute-done.22.refs_2_, ...), custom_call_target="tpu_custom_call" | custom-call | flops 1 | bytes 1 | tf_op jit(solution)/shard_map/norm_conv_back/pallas_call | solution.py:526
  172.4 3.9 %collective-permute-done.19.refs_2_ = bf16[64,1536]{1,0:T(8,128)(2,1)S(1)} collective-permute-done((bf16[64,1536]{1,0:T(8,128)(2,1)S(1)}, bf16[64,1536]{1,0:T(8,128)(2,1)S(1)}, u32[]{:S(2)}, u32[]{:S(2)}) %collective-permute-start.19) | collective-permute-done | bytes 196640 | tf_op jit(solution)/shard_map/ppermute | solution.py:578
  176.2 5.5 %norm_conv_back.3 = (bf16[2,64,1536]{2,1,0:T(8,128)(2,1)S(1)}, bf16[32,1536]{1,0:T(8,128)(2,1)S(1)}) custom-call(f32[64,1536]{1,0:T(8,128)S(1)} %get-tuple-element.80.refs_0_, bf16[64,1536]{1,0:T(8,128)(2,1)S(1)} %collective-permute-done.18.refs_1_, bf16[64,1536]{1,0:T(8,128)(2,1)S(1)} %collective-permute-done.19.refs_2_, ...), custom_call_target="tpu_custom_call" | custom-call | flops 1 | bytes 1 | tf_op jit(solution)/shard_map/norm_conv_back/pallas_call | solution.py:526
  187.9 3.2 %collective-permute-done.27 = bf16[32,1536]{1,0:T(8,128)(2,1)S(1)} collective-permute-done((bf16[32,1536]{1,0:T(8,128)(2,1)S(1)}, bf16[32,1536]{1,0:T(8,128)(2,1)S(1)}, u32[]{:S(2)}, u32[]{:S(2)}) %collective-permute-start.27) | collective-permute-done | bytes 98336 | tf_op jit(solution)/shard_map/ppermute | solution.py:578
  191.1 3.5 %collective-permute-start.29 = (bf16[32,1536]{1,0:T(8,128)(2,1)S(1)}, bf16[32,1536]{1,0:T(8,128)(2,1)S(1)}, u32[]{:S(2)}, u32[]{:S(2)}) collective-permute-start(bf16[32,1536]{1,0:T(8,128)(2,1)S(1)} %add_convert_fusion.refs_0_), channel_id=1, source_target_pairs={{0,8},{4,12},{8,0},{12,4},{1,9},{5,13},{9,1},{13,5},{2,10},{6,14},... | collective-permute-start | bytes 294920 | tf_op jit(solution)/shard_map/ppermute | solution.py:578
  194.6 3.2 %collective-permute-done.29.refs_2_ = bf16[32,1536]{1,0:T(8,128)(2,1)S(1)} collective-permute-done((bf16[32,1536]{1,0:T(8,128)(2,1)S(1)}, bf16[32,1536]{1,0:T(8,128)(2,1)S(1)}, u32[]{:S(2)}, u32[]{:S(2)}) %collective-permute-start.29) | collective-permute-done | bytes 98336 | tf_op jit(solution)/shard_map/ppermute | solution.py:578
  197.8 2.5 %collective-permute-start.30 = (bf16[32,1536]{1,0:T(8,128)(2,1)S(1)}, bf16[32,1536]{1,0:T(8,128)(2,1)S(1)}, u32[]{:S(2)}, u32[]{:S(2)}) collective-permute-start(bf16[32,1536]{1,0:T(8,128)(2,1)S(1)} %collective-permute-done.29.refs_2_), channel_id=1, source_target_pairs={{0,4},{4,0},{8,12},{12,8},{1,5},{5,1},{9,13},{13,9},{2,6},{6,2},{1... | collective-permute-start | bytes 294920 | tf_op jit(solution)/shard_map/ppermute | solution.py:578
  200.3 2.6 %collective-permute-done.30.refs_3_ = bf16[32,1536]{1,0:T(8,128)(2,1)S(1)} collective-permute-done((bf16[32,1536]{1,0:T(8,128)(2,1)S(1)}, bf16[32,1536]{1,0:T(8,128)(2,1)S(1)}, u32[]{:S(2)}, u32[]{:S(2)}) %collective-permute-start.30) | collective-permute-done | bytes 98336 | tf_op jit(solution)/shard_map/ppermute | solution.py:578
  (112 shorter events, 41.6 us)
Async XLA Ops:
  7.4 23.9 %collective-permute-start.1 = (bf16[144,1536]{1,0:T(8,128)(2,1)S(1)}, bf16[144,1536]{1,0:T(8,128)(2,1)S(1)}, u32[]{:S(2)}, u32[]{:S(2)}) collective-permute-start(bf16[144,1536]{1,0:T(8,128)(2,1)S(1)} %first_send.1.refs_0_), channel_id=1, source_target_pairs={{0,8},{4,12},{8,0},{12,4},{1,9},{5,13},{9,1},{13,5},{2,10},{6,14},... | collective-permute-start | bytes 1327112 | tf_op jit(solution)/shard_map/ppermute | solution.py:578
  11.5 20.4 %collective-permute-start = (bf16[144,1536]{1,0:T(8,128)(2,1)S(1)}, bf16[144,1536]{1,0:T(8,128)(2,1)S(1)}, u32[]{:S(2)}, u32[]{:S(2)}) collective-permute-start(bf16[144,1536]{1,0:T(8,128)(2,1)S(1)} %first_send.1.refs_0_), channel_id=1, source_target_pairs={{0,4},{4,0},{8,12},{12,8},{1,5},{5,1},{9,13},{13,9},{2,6},{6,2},{1... | collective-permute-start | bytes 1327112 | tf_op jit(solution)/shard_map/ppermute | solution.py:578
  31.3 16.2 %collective-permute-start.2 = (bf16[144,1536]{1,0:T(8,128)(2,1)S(1)}, bf16[144,1536]{1,0:T(8,128)(2,1)S(1)}, u32[]{:S(2)}, u32[]{:S(2)}) collective-permute-start(bf16[144,1536]{1,0:T(8,128)(2,1)S(1)} %collective-permute-done.1.refs_2_), channel_id=1, source_target_pairs={{0,4},{4,0},{8,12},{12,8},{1,5},{5,1},{9,13},{13,9},{2,6},{6,2},{1... | collective-permute-start | bytes 1327112 | tf_op jit(solution)/shard_map/ppermute | solution.py:578
  35.9 11.5 %collective-permute-start.4 = (bf16[72,1536]{1,0:T(8,128)(2,1)S(1)}, bf16[72,1536]{1,0:T(8,128)(2,1)S(1)}, u32[]{:S(2)}, u32[]{:S(2)}) collective-permute-start(bf16[72,1536]{1,0:T(8,128)(2,1)S(1)} %get-tuple-element.54), channel_id=1, source_target_pairs={{0,2},{1,3},{2,0},{3,1},{4,6},{5,7},{6,4},{7,5},{8,10},{9,11},{10,... | collective-permute-start | bytes 663560 | tf_op jit(solution)/shard_map/ppermute | solution.py:578
  37.5 10.0 %collective-permute-start.5 = (bf16[72,1536]{1,0:T(8,128)(2,1)S(1)}, bf16[72,1536]{1,0:T(8,128)(2,1)S(1)}, u32[]{:S(2)}, u32[]{:S(2)}) collective-permute-start(bf16[72,1536]{1,0:T(8,128)(2,1)S(1)} %get-tuple-element.55), channel_id=1, source_target_pairs={{0,3},{1,2},{2,1},{3,0},{4,7},{5,6},{6,5},{7,4},{8,11},{9,10},{10,... | collective-permute-start | bytes 663560 | tf_op jit(solution)/shard_map/ppermute | solution.py:578
  47.6 41.0 %collective-permute-start.7 = (bf16[4,72,1536]{2,1,0:T(8,128)(2,1)S(1)}, bf16[4,72,1536]{2,1,0:T(8,128)(2,1)S(1)}, u32[]{:S(2)}, u32[]{:S(2)}) collective-permute-start(bf16[4,72,1536]{2,1,0:T(8,128)(2,1)S(1)} %stacked.1.refs_0_), channel_id=1, source_target_pairs={{0,8},{4,12},{8,0},{12,4},{1,9},{5,13},{9,1},{13,5},{2,10},{6,14},... | collective-permute-start | bytes 2654216 | tf_op jit(solution)/shard_map/ppermute | solution.py:578
  53.2 35.3 %collective-permute-start.12 = (bf16[288,1536]{1,0:T(8,128)(2,1)S(1)}, bf16[288,1536]{1,0:T(8,128)(2,1)S(1)}, u32[]{:S(2)}, u32[]{:S(2)}) collective-permute-start(bf16[288,1536]{1,0:T(8,128)(2,1)S(1)} %get-tuple-element.61), channel_id=1, source_target_pairs={{0,1},{1,0},{2,3},{3,2},{4,5},{5,4},{6,7},{7,6},{8,9},{9,8},{10,11... | collective-permute-start | bytes 2654216 | tf_op jit(solution)/shard_map/ppermute | solution.py:578
  54.4 38.8 %collective-permute-start.13 = (bf16[288,1536]{1,0:T(8,128)(2,1)S(1)}, bf16[288,1536]{1,0:T(8,128)(2,1)S(1)}, u32[]{:S(2)}, u32[]{:S(2)}) collective-permute-start(bf16[288,1536]{1,0:T(8,128)(2,1)S(1)} %get-tuple-element.62), channel_id=1, source_target_pairs={{0,2},{1,3},{2,0},{3,1},{4,6},{5,7},{6,4},{7,5},{8,10},{9,11},{10,... | collective-permute-start | bytes 2654216 | tf_op jit(solution)/shard_map/ppermute | solution.py:578
  55.3 38.0 %collective-permute-start.14 = (bf16[288,1536]{1,0:T(8,128)(2,1)S(1)}, bf16[288,1536]{1,0:T(8,128)(2,1)S(1)}, u32[]{:S(2)}, u32[]{:S(2)}) collective-permute-start(bf16[288,1536]{1,0:T(8,128)(2,1)S(1)} %get-tuple-element.63), channel_id=1, source_target_pairs={{0,3},{1,2},{2,1},{3,0},{4,7},{5,6},{6,5},{7,4},{8,11},{9,10},{10,... | collective-permute-start | bytes 2654216 | tf_op jit(solution)/shard_map/ppermute | solution.py:578
  56.7 57.7 %collective-permute-start.6 = (bf16[4,72,1536]{2,1,0:T(8,128)(2,1)S(1)}, bf16[4,72,1536]{2,1,0:T(8,128)(2,1)S(1)}, u32[]{:S(2)}, u32[]{:S(2)}) collective-permute-start(bf16[4,72,1536]{2,1,0:T(8,128)(2,1)S(1)} %stacked.1.refs_0_), channel_id=1, source_target_pairs={{0,4},{4,0},{8,12},{12,8},{1,5},{5,1},{9,13},{13,9},{2,6},{6,2},{1... | collective-permute-start | bytes 2654216 | tf_op jit(solution)/shard_map/ppermute | solution.py:578
  88.5 25.9 %collective-permute-start.8 = (bf16[4,72,1536]{2,1,0:T(8,128)(2,1)S(1)}, bf16[4,72,1536]{2,1,0:T(8,128)(2,1)S(1)}, u32[]{:S(2)}, u32[]{:S(2)}) collective-permute-start(bf16[4,72,1536]{2,1,0:T(8,128)(2,1)S(1)} %collective-permute-done.7.refs_2_), channel_id=1, source_target_pairs={{0,4},{4,0},{8,12},{12,8},{1,5},{5,1},{9,13},{13,9},{2,6},{6,2},{1... | collective-permute-start | bytes 2654216 | tf_op jit(solution)/shard_map/ppermute | solution.py:578
  110.8 21.9 %collective-permute-start.15 = (bf16[144,1536]{1,0:T(8,128)(2,1)}, bf16[144,1536]{1,0:T(8,128)(2,1)S(1)}, u32[]{:S(2)}, u32[]{:S(2)}) collective-permute-start(bf16[144,1536]{1,0:T(8,128)(2,1)} %get-tuple-element.66), channel_id=1, source_target_pairs={{0,1},{1,0},{2,3},{3,2},{4,5},{5,4},{6,7},{7,6},{8,9},{9,8},{10,11... | collective-permute-start | bytes 1327112 | tf_op jit(solution)/shard_map/ppermute | solution.py:578
  111.5 23.4 %collective-permute-start.16 = (bf16[144,1536]{1,0:T(8,128)(2,1)}, bf16[144,1536]{1,0:T(8,128)(2,1)S(1)}, u32[]{:S(2)}, u32[]{:S(2)}) collective-permute-start(bf16[144,1536]{1,0:T(8,128)(2,1)} %get-tuple-element.67), channel_id=1, source_target_pairs={{0,2},{1,3},{2,0},{3,1},{4,6},{5,7},{6,4},{7,5},{8,10},{9,11},{10,... | collective-permute-start | bytes 1327112 | tf_op jit(solution)/shard_map/ppermute | solution.py:578
  112.3 22.6 %collective-permute-start.17 = (bf16[144,1536]{1,0:T(8,128)(2,1)}, bf16[144,1536]{1,0:T(8,128)(2,1)S(1)}, u32[]{:S(2)}, u32[]{:S(2)}) collective-permute-start(bf16[144,1536]{1,0:T(8,128)(2,1)} %get-tuple-element.68), channel_id=1, source_target_pairs={{0,3},{1,2},{2,1},{3,0},{4,7},{5,6},{6,5},{7,4},{8,11},{9,10},{10,... | collective-permute-start | bytes 1327112 | tf_op jit(solution)/shard_map/ppermute | solution.py:578
  131.3 23.2 %collective-permute-start.9 = (bf16[144,1536]{1,0:T(8,128)(2,1)}, bf16[144,1536]{1,0:T(8,128)(2,1)S(1)}, u32[]{:S(2)}, u32[]{:S(2)}) collective-permute-start(bf16[144,1536]{1,0:T(8,128)(2,1)} %get-tuple-element.57), channel_id=1, source_target_pairs={{0,1},{1,0},{2,3},{3,2},{4,5},{5,4},{6,7},{7,6},{8,9},{9,8},{10,11... | collective-permute-start | bytes 1327112 | tf_op jit(solution)/shard_map/ppermute | solution.py:578
  132.0 26.1 %collective-permute-start.10 = (bf16[144,1536]{1,0:T(8,128)(2,1)}, bf16[144,1536]{1,0:T(8,128)(2,1)S(1)}, u32[]{:S(2)}, u32[]{:S(2)}) collective-permute-start(bf16[144,1536]{1,0:T(8,128)(2,1)} %get-tuple-element.58), channel_id=1, source_target_pairs={{0,2},{1,3},{2,0},{3,1},{4,6},{5,7},{6,4},{7,5},{8,10},{9,11},{10,... | collective-permute-start | bytes 1327112 | tf_op jit(solution)/shard_map/ppermute | solution.py:578
  132.8 25.3 %collective-permute-start.11 = (bf16[144,1536]{1,0:T(8,128)(2,1)}, bf16[144,1536]{1,0:T(8,128)(2,1)S(1)}, u32[]{:S(2)}, u32[]{:S(2)}) collective-permute-start(bf16[144,1536]{1,0:T(8,128)(2,1)} %get-tuple-element.59), channel_id=1, source_target_pairs={{0,3},{1,2},{2,1},{3,0},{4,7},{5,6},{6,5},{7,4},{8,11},{9,10},{10,... | collective-permute-start | bytes 1327112 | tf_op jit(solution)/shard_map/ppermute | solution.py:578
  138.0 23.2 %collective-permute-start.21 = (bf16[64,1536]{1,0:T(8,128)(2,1)S(1)}, bf16[64,1536]{1,0:T(8,128)(2,1)S(1)}, u32[]{:S(2)}, u32[]{:S(2)}) collective-permute-start(bf16[64,1536]{1,0:T(8,128)(2,1)S(1)} %get-tuple-element.88), channel_id=1, source_target_pairs={{0,4},{4,0},{8,12},{12,8},{1,5},{5,1},{9,13},{13,9},{2,6},{6,2},{1... | collective-permute-start | bytes 589832 | tf_op jit(solution)/shard_map/ppermute | solution.py:578
  138.7 28.5 %collective-permute-start.22 = (bf16[64,1536]{1,0:T(8,128)(2,1)S(1)}, bf16[64,1536]{1,0:T(8,128)(2,1)S(1)}, u32[]{:S(2)}, u32[]{:S(2)}) collective-permute-start(bf16[64,1536]{1,0:T(8,128)(2,1)S(1)} %get-tuple-element.89), channel_id=1, source_target_pairs={{0,8},{4,12},{8,0},{12,4},{1,9},{5,13},{9,1},{13,5},{2,10},{6,14},... | collective-permute-start | bytes 589832 | tf_op jit(solution)/shard_map/ppermute | solution.py:578
  154.5 12.7 %collective-permute-start.23 = (bf16[64,1536]{1,0:T(8,128)(2,1)S(1)}, bf16[64,1536]{1,0:T(8,128)(2,1)S(1)}, u32[]{:S(2)}, u32[]{:S(2)}) collective-permute-start(bf16[64,1536]{1,0:T(8,128)(2,1)S(1)} %get-tuple-element.90), channel_id=1, source_target_pairs={{0,12},{4,8},{8,4},{12,0},{1,13},{5,9},{9,5},{13,1},{2,14},{6,10},... | collective-permute-start | bytes 589832 | tf_op jit(solution)/shard_map/ppermute | solution.py:578
  160.2 12.1 %collective-permute-start.18 = (bf16[64,1536]{1,0:T(8,128)(2,1)S(1)}, bf16[64,1536]{1,0:T(8,128)(2,1)S(1)}, u32[]{:S(2)}, u32[]{:S(2)}) collective-permute-start(bf16[64,1536]{1,0:T(8,128)(2,1)S(1)} %get-tuple-element.81), channel_id=1, source_target_pairs={{0,4},{4,0},{8,12},{12,8},{1,5},{5,1},{9,13},{13,9},{2,6},{6,2},{1... | collective-permute-start | bytes 589832 | tf_op jit(solution)/shard_map/ppermute | solution.py:578
  160.3 16.0 %collective-permute-start.19 = (bf16[64,1536]{1,0:T(8,128)(2,1)S(1)}, bf16[64,1536]{1,0:T(8,128)(2,1)S(1)}, u32[]{:S(2)}, u32[]{:S(2)}) collective-permute-start(bf16[64,1536]{1,0:T(8,128)(2,1)S(1)} %get-tuple-element.82), channel_id=1, source_target_pairs={{0,8},{4,12},{8,0},{12,4},{1,9},{5,13},{9,1},{13,5},{2,10},{6,14},... | collective-permute-start | bytes 589832 | tf_op jit(solution)/shard_map/ppermute | solution.py:578
  161.2 15.1 %collective-permute-start.20 = (bf16[64,1536]{1,0:T(8,128)(2,1)S(1)}, bf16[64,1536]{1,0:T(8,128)(2,1)S(1)}, u32[]{:S(2)}, u32[]{:S(2)}) collective-permute-start(bf16[64,1536]{1,0:T(8,128)(2,1)S(1)} %get-tuple-element.83), channel_id=1, source_target_pairs={{0,12},{4,8},{8,4},{12,0},{1,13},{5,9},{9,5},{13,1},{2,14},{6,10},... | collective-permute-start | bytes 589832 | tf_op jit(solution)/shard_map/ppermute | solution.py:578
  187.9 12.5 %collective-permute-start.24 = (bf16[2,64,1536]{2,1,0:T(8,128)(2,1)S(1)}, bf16[2,64,1536]{2,1,0:T(8,128)(2,1)S(1)}, u32[]{:S(2)}, u32[]{:S(2)}) collective-permute-start(bf16[2,64,1536]{2,1,0:T(8,128)(2,1)S(1)} %get-tuple-element.93), channel_id=1, source_target_pairs={{0,16},{16,0},{1,17},{17,1},{2,18},{18,2},{3,19},{19,3},{4,20},{20... | collective-permute-start | bytes 1179656 | tf_op jit(solution)/shard_map/ppermute | solution.py:630
  (36 other events, 277.2 us)

commit v3 on v2

v3 whole, which is shorter than its diff:
```python
import functools

import jax
import jax.numpy as jnp
from jax import lax
from jax.experimental import pallas as pl
from jax.experimental.pallas import tpu as pltpu
from jax.sharding import PartitionSpec as P

MB = 2
EPSILON = 1e-06
LANES = 128
TILE = 512
PART = 256
SEND_MIB = 60
EXPERT_MIB = 24
NOWHERE = -512.0
COSTS = (0, 0, 0, 0, 12, 0, 0, 0, 0, 2, 0, 0, 0, 0, 12)
MIB = 1024 * 1024
SMALL = pl.CostEstimate(flops=1, bytes_accessed=1, transcendentals=0)
bf16 = jnp.bfloat16
f32 = jnp.float32


def round_up(value, step):
    return -(-value // step) * step


def params(mib):
    return pltpu.CompilerParams(vmem_limit_bytes=mib * MIB)


def cost(amount):
    return pl.CostEstimate(flops=int(amount * 1.15e9) + 1, bytes_accessed=1, transcendentals=0)


def whole(count):
    return [pl.BlockSpec(memory_space=pltpu.VMEM)] * count


def after(count):
    return [pl.BlockSpec(memory_space=pl.ANY)] * count


def far(count):
    return [pl.BlockSpec(memory_space=pltpu.HBM)] * count


def fetching(sources, targets, sems):
    copies = [
        pltpu.make_async_copy(source, target, sems.at[i])
        for i, (source, target) in enumerate(zip(sources, targets))
    ]
    for copy in copies:
        copy.start()
    return copies


def fetched(sources, targets, sems):
    for copy in fetching(sources, targets, sems):
        copy.wait()


def sigmoid(values):
    return 1.0 / (1.0 + jnp.exp(-values))


def silu_slope(values):
    gate_sig = sigmoid(values)
    return gate_sig * (1.0 + values * (1.0 - gate_sig))


def shifted(pad, starts, frames):
    for residue in range(8):
        group = [(i, start // 8) for i, start in enumerate(starts) if start % 8 == residue]
        if not group:
            continue
        low, high = min(t for _, t in group), max(t for _, t in group)
        first = 8 * low + residue
        block = pad[first : first + 8 * (high - low) + frames, :]
        for i, tile in group:
            yield i, block[8 * (tile - low) : 8 * (tile - low) + frames, :]


def mixed_frames(x_ref, taps_ref, pad, conv_ref, mixed_ref):
    frames, features = x_ref.shape
    tap_count = taps_ref.shape[0]
    margin = tap_count // 2
    lead = round_up(margin, 8)
    pad[...] = jnp.zeros(pad.shape, f32)

    def chunk(c, squares):
        cols = pl.ds(pl.multiple_of(c * LANES, LANES), LANES)
        xs = x_ref[:, cols].astype(f32)
        pad[lead : lead + frames, :] = xs
        acc = jnp.zeros((frames, LANES), f32)
        for j, rows in shifted(pad, [lead + j - margin for j in range(tap_count)], frames):
            acc = acc + taps_ref[j, :, cols] * rows
        mixed = xs + acc * sigmoid(acc)
        if conv_ref is not None:
            conv_ref[:, cols] = acc
        mixed_ref[:, cols] = mixed
        return squares + mixed * mixed

    squares = lax.fori_loop(0, features // LANES, chunk, jnp.zeros((frames, LANES), f32))
    return lax.rsqrt(jnp.sum(squares, axis=1, keepdims=True) / features + EPSILON)


def meta_rows(routes_ref, combine_ref, m):
    own = lax.axis_index("expert").astype(jnp.int32)
    rows = [(routes_ref[m] ^ own).astype(f32)]
    left = combine_ref[m]
    for _ in range(3):
        rows.append(left.astype(bf16).astype(f32))
        left = left - rows[-1]
    return jnp.concatenate(rows, axis=0)


def first_send_body(
    x_all, up_all, routes_all, combine_all, taps_all, gain_all, send_ref, mixed, pad, x_ref, routes_ref,
    combine_ref, taps_ref, gain_ref, sems
):
    frames = x_ref.shape[0]
    fetched(
        (x_all.at[0], up_all.at[0], routes_all, combine_all, taps_all, gain_all),
        (x_ref, send_ref.at[frames : 2 * frames], routes_ref, combine_ref, taps_ref, gain_ref),
        sems,
    )
    scale = mixed_frames(x_ref, taps_ref, pad, None, mixed)
    send_ref[:frames, :] = (mixed[...] * scale * gain_ref[...]).astype(bf16)
    metas = [meta_rows(routes_ref, combine_ref, m) for m in range(MB)]
    send_ref[2 * frames :, :frames] = jnp.concatenate(metas, axis=0).astype(bf16)


def send_scratch(x, routes, combine, taps, gain):
    _, frames, features = x.shape
    return [
        pltpu.VMEM((frames, features), f32),
        pltpu.VMEM((frames + 2 * round_up(taps.shape[0] // 2, 8), LANES), f32),
        pltpu.VMEM((frames, features), bf16),
        pltpu.VMEM(routes.shape, routes.dtype),
        pltpu.VMEM(combine.shape, f32),
        pltpu.VMEM(taps.shape, f32),
        pltpu.VMEM(gain.shape, f32),
        pltpu.SemaphoreType.DMA((6,)),
    ]


def first_send(x, upstream, routes, combine, taps, gain):
    _, frames, features = x.shape
    return pl.pallas_call(
        first_send_body,
        out_shape=jax.ShapeDtypeStruct((2 * frames + 8 * MB, features), bf16),
        in_specs=far(6),
        out_specs=whole(1)[0],
        scratch_shapes=send_scratch(x, routes, combine, taps, gain),
        compiler_params=params(SEND_MIB),
        cost_estimate=cost(COSTS[0]),
        name="first_send",
    )(x, upstream, routes, combine, taps, gain)


def second_send_body(
    experts, capacity, x_all, up_all, routes_all, combine_all, taps_all, gain_all, _, *refs
):
    outs, (mixed, pad, x_ref, routes_ref, combine_ref, taps_ref, gain_ref, sems, joined) = (
        refs[:experts],
        refs[experts:],
    )
    frames, features = x_ref.shape
    fetched(
        (x_all.at[1], up_all.at[1], routes_all, combine_all, taps_all, gain_all),
        (x_ref, joined.at[frames:], routes_ref, combine_ref, taps_ref, gain_ref),
        sems,
    )
    scale = mixed_frames(x_ref, taps_ref, pad, None, mixed)
    joined[:frames, :] = (mixed[...] * scale * gain_ref[...]).astype(bf16)
    slot, weight = slot_map(experts, frames, meta_rows(routes_ref, combine_ref, 1), (0,))
    rows = outs[0].shape[0]
    row_ids = lax.broadcasted_iota(jnp.int32, (rows, frames), 0).astype(f32)
    for e in range(experts):
        normed_row = (row_ids == slot[e : e + 1, :]).astype(f32).astype(bf16)
        chosen = (row_ids - capacity == slot[e : e + 1, :]) & (row_ids >= capacity)
        amount = jnp.sum(jnp.where(chosen, weight[e : e + 1, :], 0.0), axis=1, keepdims=True)
        grad_row = chosen.astype(f32).astype(bf16)
        for first_col in range(0, features, 512):
            cols = slice(first_col, min(first_col + 512, features))
            picked = jnp.dot(grad_row, joined[frames:, cols], preferred_element_type=f32) * amount
            picked = picked + jnp.dot(normed_row, joined[:frames, cols], preferred_element_type=f32)
            outs[e][:, cols] = picked.astype(bf16)


def second_send(x, upstream, routes, combine, taps, gain, experts, capacity, earlier):
    _, frames, features = x.shape
    rows = round_up(2 * capacity, 8)
    return pl.pallas_call(
        functools.partial(second_send_body, experts, capacity),
        out_shape=(jax.ShapeDtypeStruct((rows, features), bf16),) * experts,
        in_specs=far(6) + after(1),
        out_specs=tuple(whole(experts)),
        scratch_shapes=send_scratch(x, routes, combine, taps, gain) + [pltpu.VMEM((2 * frames, features), bf16)],
        compiler_params=params(SEND_MIB),
        cost_estimate=cost(COSTS[14]),
        name="second_send",
    )(x, upstream, routes, combine, taps, gain, earlier)


def saved_body(x_ref, taps_ref, _, conv_ref, mixed_ref, scale_ref, pad):
    for m in range(MB):
        scale_ref[m] = mixed_frames(x_ref.at[m], taps_ref, pad, conv_ref.at[m], mixed_ref.at[m])


def saved_frames(x, taps, earlier):
    lead = round_up(taps.shape[0] // 2, 8)
    return pl.pallas_call(
        saved_body,
        out_shape=(
            jax.ShapeDtypeStruct(x.shape, f32),
            jax.ShapeDtypeStruct(x.shape, f32),
            jax.ShapeDtypeStruct(x.shape[:2] + (1,), f32),
        ),
        in_specs=whole(2) + after(1),
        out_specs=tuple(whole(3)),
        scratch_shapes=[pltpu.VMEM((x.shape[1] + 2 * lead, LANES), f32)],
        compiler_params=params(16),
        cost_estimate=cost(COSTS[1]),
        name="saved_frames",
    )(x, taps, earlier)


def passed_body(*refs):
    pass


def passed(array, earlier):
    return pl.pallas_call(
        passed_body,
        out_shape=jax.ShapeDtypeStruct(array.shape, array.dtype),
        in_specs=after(2),
        out_specs=after(1)[0],
        input_output_aliases={0: 0},
        compiler_params=params(16),
        cost_estimate=SMALL,
        name="passed",
    )(array, earlier)


def slot_map(experts, frames, meta, places):
    total = meta.shape[1]
    padded = round_up(experts, 16)
    named = lax.broadcasted_iota(jnp.int32, (padded, total), 0).astype(f32)
    first, second = meta[0:1, :] == named, meta[1:2, :] == named
    member = first | second
    earlier = lax.broadcasted_iota(jnp.int32, (total, total), 0)
    later = lax.broadcasted_iota(jnp.int32, (total, total), 1)
    before = (earlier < later) & (earlier // frames == later // frames)
    rank = jnp.dot(
        member.astype(f32).astype(bf16),
        before.astype(f32).astype(bf16),
        preferred_element_type=f32,
    )
    seq_of = lax.broadcasted_iota(jnp.int32, (padded, total), 1) // frames
    for k, first_row in enumerate(places):
        rank = jnp.where(seq_of == k, rank + first_row, rank)
    slot = jnp.where(member, rank, NOWHERE)
    first_weight = meta[2:3, :] + meta[4:5, :] + meta[6:7, :]
    second_weight = meta[3:4, :] + meta[5:6, :] + meta[7:8, :]
    weight = jnp.where(first, first_weight, 0.0) + jnp.where(second, second_weight, 0.0)
    return slot, weight


def place(slot, weight, joined, out_ref, first_row, rows):
    row_ids = lax.broadcasted_iota(jnp.int32, (rows, slot.shape[1]), 0).astype(f32)
    chosen = row_ids == slot
    placing = chosen.astype(f32).astype(bf16)
    if weight is not None:
        amount = jnp.sum(jnp.where(chosen, weight, 0.0), axis=1, keepdims=True)
    for first_col in range(0, joined.shape[1], 512):
        cols = slice(first_col, min(first_col + 512, joined.shape[1]))
        picked = jnp.dot(placing, joined[:, cols], preferred_element_type=f32)
        if weight is not None:
            picked = picked * amount
        out_ref[first_row : first_row + rows, cols] = picked.astype(bf16)


def slots_body(experts, frames, places, seqs, waits, *refs):
    block_refs, refs = refs[:seqs], refs[seqs + waits :]
    piece_refs, refs = refs[: len(refs) - experts - 3], refs[len(refs) - experts - 3 :]
    if piece_refs:
        piece_refs, stacked, refs = piece_refs[:-1], piece_refs[-1], refs
        for i, ref in enumerate(piece_refs):
            stacked[i] = ref[...]
    out_refs, (slot_ref, joined, meta) = refs[:experts], refs[experts:]
    total = seqs * frames
    for k in range(seqs):
        here = slice(k * frames, (k + 1) * frames)
        joined[here, :] = block_refs[k][:frames, :]
        joined[total + k * frames : total + (k + 1) * frames, :] = block_refs[k][frames : 2 * frames, :]
        meta[:, here] = block_refs[k][2 * frames :, :frames].astype(f32)
    slot, weight = slot_map(experts, frames, meta[:8, :], places[0])
    slot_ref[0] = slot
    slot_ref[1] = slot_map(experts, frames, meta[8:, :], places[1])[0]
    rows = out_refs[0].shape[0] // 2
    for e in range(experts):
        place(slot[e : e + 1, :], None, joined.at[:total], out_refs[e], 0, rows)
        place(slot[e : e + 1, :], weight[e : e + 1, :], joined.at[total:], out_refs[e], rows, rows)


def slots(blocks, experts, capacity, frames, places, pieces=(), earlier=()):
    features = blocks[0].shape[1]
    seqs = len(blocks)
    rows = round_up(seqs * capacity, 8)
    total = seqs * frames
    together = tuple(jax.ShapeDtypeStruct((len(pieces),) + p.shape, bf16) for p in pieces[:1])
    out = pl.pallas_call(
        functools.partial(slots_body, experts, frames, places, seqs, len(earlier)),
        out_shape=together
        + tuple(jax.ShapeDtypeStruct((2 * rows, features), bf16) for _ in range(experts))
        + (jax.ShapeDtypeStruct((MB, round_up(experts, 16), total), f32),),
        in_specs=whole(seqs) + after(len(earlier)) + whole(len(pieces)),
        out_specs=tuple(whole(len(together) + experts + 1)),
        scratch_shapes=[pltpu.VMEM((2 * total, features), bf16), pltpu.VMEM((8 * MB, total), f32)],
        compiler_params=params(16),
        cost_estimate=cost(COSTS[2 + (not pieces)]),
        name="slots",
    )(*blocks, *earlier, *pieces)
    return out[-1 - experts : -1], out[-1], out[0]


def expert_body(parts, rows, capacity, first_row, counts, *refs):
    cuts = [sum(counts[:i]) for i in range(len(counts) + 1)]
    in_refs, (up_mat, down_mat), before_refs, _, _, slot_refs, kept_far, scratch = (
        refs[cuts[i] : cuts[i + 1]] for i in range(len(counts))
    )
    rows_in, rows_grad, acted, kept, put_sems = scratch
    features, hidden = up_mat.shape
    steps = hidden // TILE
    far_outs = [ref.at[first_row : first_row + parts * rows, :] for ref in kept_far]

    def putting(h):
        cols = pl.ds(pl.multiple_of(h * TILE, TILE), TILE)
        return (
            pltpu.make_async_copy(acted.at[:, cols], far_outs[2].at[:, cols], put_sems.at[0, h]),
            pltpu.make_async_copy(kept.at[:, cols], far_outs[3].at[:, cols], put_sems.at[1, h]),
        )

    row_puts = [
        pltpu.make_async_copy(rows_in, far_outs[0], put_sems.at[2, 0]),
        pltpu.make_async_copy(rows_grad, far_outs[1], put_sems.at[2, 1]),
    ]
    for j in range(parts):
        here = slice(j * rows, (j + 1) * rows)
        if capacity is None:
            rows_in[here, :] = in_refs[j][:rows, :]
            rows_grad[here, :] = in_refs[j][rows:, :]
            continue
        seqs, size = len(in_refs), in_refs[0].shape[1]
        pieces = jnp.concatenate([ref[j] for ref in in_refs], axis=0)
        row = lax.broadcasted_iota(jnp.int32, (rows, seqs * size), 0)
        source = lax.broadcasted_iota(jnp.int32, (rows, seqs * size), 1)
        wanted = (row // capacity) * size + row % capacity
        wanted = jnp.where(row < seqs * capacity, wanted, -2 * size)
        for target, first in ((rows_in, 0), (rows_grad, capacity)):
            moving = (source == wanted + first).astype(f32).astype(bf16)
            target[here, :] = jnp.dot(moving, pieces, preferred_element_type=f32).astype(bf16)
    for copy in row_puts:
        copy.start()

    def forward(h, carry):
        for first in range(0, TILE, PART):
            cols = pl.ds(pl.multiple_of(h * TILE + first, PART), PART)
            pre_act = jnp.dot(rows_in[...], up_mat[:, cols], preferred_element_type=f32)
            act_grad = lax.dot_general(
                rows_grad[...], down_mat[cols, :], (((1,), (1,)), ((), ())), preferred_element_type=f32
            )
            gate_sig = sigmoid(pre_act)
            acted[:, cols] = (pre_act * gate_sig).astype(bf16)
            slope = gate_sig * (1.0 + pre_act * (1.0 - gate_sig))
            kept[:, cols] = (act_grad * slope).astype(bf16)
        for copy in putting(h):
            copy.start()
        return carry

    lax.fori_loop(0, steps, forward, 0)
    own_row = slot_refs[0].shape[0] - rows
    if before_refs:
        for j in range(parts):
            slot_refs[j][:own_row, :] = before_refs[j][...]

    def backward(d, carry):
        for first in range(0, TILE, PART):
            cols = pl.ds(pl.multiple_of(d * TILE + first, PART), PART)
            term = lax.dot_general(
                kept[...], up_mat[cols, :], (((1,), (1,)), ((), ())), preferred_element_type=f32
            )
            for j in range(parts):
                slot_refs[j][own_row:, cols] = term[j * rows : (j + 1) * rows, :].astype(bf16)
        return carry

    lax.fori_loop(0, features // TILE, backward, 0)
    for copy in row_puts:
        copy.wait()
    for h in range(steps):
        for copy in putting(h):
            copy.wait()


def expert_products(blocks, parts, capacity, up_mat, down_mat, rows, total, first_row, before, kept, earlier=(), stage=4):
    features, hidden = up_mat.shape
    steps = hidden // TILE
    mine = parts * rows
    slot_rows = rows + (before[0].shape[0] if before else 0)
    counts = (len(blocks), 2, len(before), len(earlier), len(kept), parts, 4, 5)
    first_kept = sum(counts[:4])
    out = pl.pallas_call(
        functools.partial(
            expert_body, parts, rows, capacity if blocks[0].ndim == 3 else None, first_row, counts
        ),
        out_shape=tuple(jax.ShapeDtypeStruct((slot_rows, features), bf16) for _ in range(parts))
        + (
            pltpu.HBM((total, features), bf16),
            pltpu.HBM((total, features), bf16),
            pltpu.HBM((total, hidden), bf16),
            pltpu.HBM((total, hidden), bf16),
        ),
        in_specs=whole(len(blocks) + 2 + len(before)) + after(len(earlier)) + far(len(kept)),
        out_specs=tuple(whole(parts) + far(4)),
        input_output_aliases={first_kept + i: parts + i for i in range(len(kept))},
        scratch_shapes=[
            pltpu.VMEM((mine, features), bf16),
            pltpu.VMEM((mine, features), bf16),
            pltpu.VMEM((mine, hidden), bf16),
            pltpu.VMEM((mine, hidden), bf16),
            pltpu.SemaphoreType.DMA((3, max(2, steps))),
        ],
        compiler_params=params(EXPERT_MIB),
        cost_estimate=cost(COSTS[stage]),
        name="expert_products",
    )(*blocks, up_mat, down_mat, *before, *earlier, *kept)
    return out[:parts], out[parts:]


def frame_sums_body(m, experts, frames, pieces, *refs):
    map_refs, slot_refs, out_refs, picking = refs[:2], refs[2 : 2 + experts], refs[-1 - len(pieces) : -1], refs[-1]
    total = len(pieces) * frames
    rows = slot_refs[0].shape[0]
    same = lax.broadcasted_iota(jnp.int32, (frames, frames), 0) == lax.broadcasted_iota(
        jnp.int32, (frames, frames), 1
    )
    same = same.astype(f32).astype(bf16)
    col_ids = lax.broadcasted_iota(jnp.int32, (frames, rows), 1)
    for i, (half, k, first_row) in enumerate(pieces):
        columns = lax.dot_general(
            same,
            map_refs[half][m, :, k * frames : (k + 1) * frames].astype(bf16),
            (((1,), (1,)), ((), ())),
            preferred_element_type=f32,
        )
        here = (col_ids - first_row).astype(f32)
        for e in range(experts):
            picking[e, i * frames : (i + 1) * frames, :] = (
                (here == columns[:, e : e + 1]).astype(f32).astype(bf16)
            )

    def feature(d, carry):
        cols = pl.ds(pl.multiple_of(d * PART, PART), PART)
        acc = jnp.zeros((total, PART), f32)
        for e in range(experts):
            acc = acc + jnp.dot(picking[e], slot_refs[e][:, cols], preferred_element_type=f32)
        for i, out_ref in enumerate(out_refs):
            out_ref[:, cols] = acc[i * frames : (i + 1) * frames, :].astype(out_ref.dtype)
        return carry

    lax.fori_loop(0, slot_refs[0].shape[1] // PART, feature, 0)


def frame_sums(m, maps, blocks, frames, pieces, earlier, handed=()):
    rows, features = blocks[0].shape
    first = 2 + len(blocks) + len(earlier)
    out = pl.pallas_call(
        functools.partial(frame_sums_body, m, len(blocks), frames, pieces),
        out_shape=tuple(pltpu.HBM(h.shape, h.dtype) for h in handed)
        + tuple(
            jax.ShapeDtypeStruct((frames, features), f32 if piece[:2] == (0, 0) else bf16)
            for piece in pieces
        ),
        in_specs=whole(2 + len(blocks)) + after(len(earlier)) + far(len(handed)),
        out_specs=tuple(far(len(handed)) + whole(len(pieces))),
        input_output_aliases={first + i: i for i in range(len(handed))},
        scratch_shapes=[pltpu.VMEM((len(blocks), len(pieces) * frames, rows), bf16)],
        compiler_params=params(16),
        cost_estimate=cost(COSTS[8 + m + (len(pieces) == 1)]),
        name="frame_sums",
    )(*maps, *blocks, *earlier, *handed)
    return out[: len(handed)], out[len(handed) :]


def epilogue_body(m, seqs, last, waits, *refs):
    norm_refs = refs[:seqs]
    (x_all, up_all, conv_ref, mixed_ref, scale_ref, taps_ref, gain_ref) = refs[seqs : seqs + 7]
    before, refs = refs[seqs + 7 : seqs + 7 + 2 * last], refs[seqs + 7 + 2 * last + waits :]
    if last:
        sums_ref, other_ref = before
    prev_ref, term_ref, norm_grad, pad_x, pad_g, x_ref, up_ref, sems = refs
    if last:
        prev_ref[0] = other_ref[...]
        prev_ref = prev_ref.at[1]
    copies = fetching((x_all.at[m], up_all.at[m]), (x_ref, up_ref), sems)
    conv_ref, mixed_ref, scale_ref = conv_ref.at[m], mixed_ref.at[m], scale_ref.at[m]
    frames, features = x_ref.shape
    tap_count = taps_ref.shape[0]
    margin = tap_count // 2
    lead = round_up(margin, 8)
    pad_x[...] = jnp.zeros(pad_x.shape, f32)
    pad_g[...] = jnp.zeros(pad_g.shape, f32)
    scale = scale_ref[...]

    def put(row, cols, value):
        if last:
            value = value + sums_ref[row : row + 1, cols]
        term_ref[row : row + 1, cols] = value.astype(term_ref.dtype)

    def gather(c, inner):
        cols = pl.ds(pl.multiple_of(c * LANES, LANES), LANES)
        grad = norm_refs[0][:, cols].astype(f32)
        for k in range(1, seqs):
            grad = grad + norm_refs[k][:, cols].astype(f32)
        norm_grad[:, cols] = grad
        weighed = grad * mixed_ref[:, cols]
        put(tap_count, cols, jnp.sum(weighed * scale, axis=0, keepdims=True))
        return inner + weighed * gain_ref[:, cols]

    inner = lax.fori_loop(0, features // LANES, gather, jnp.zeros((frames, LANES), f32))
    for copy in copies:
        copy.wait()
    pull = scale * scale * scale * (jnp.sum(inner, axis=1, keepdims=True) / features)

    def chunk(c, carry):
        cols = pl.ds(pl.multiple_of(c * LANES, LANES), LANES)
        mixed_grad = (
            up_ref[:, cols].astype(f32)
            + scale * (norm_grad[:, cols] * gain_ref[:, cols])
            - mixed_ref[:, cols] * pull
        )
        conv_grad = mixed_grad * silu_slope(conv_ref[:, cols])
        pad_x[lead : lead + frames, :] = x_ref[:, cols].astype(f32)
        pad_g[lead : lead + frames, :] = conv_grad
        acc = mixed_grad
        for j, rows in shifted(pad_x, [lead + j - margin for j in range(tap_count)], frames):
            put(j, cols, jnp.sum(conv_grad * rows, axis=0, keepdims=True))
        for j, rows in shifted(pad_g, [lead + margin - j for j in range(tap_count)], frames):
            acc = acc + taps_ref[j, :, cols] * rows
        prev_ref[:, cols] = acc.astype(bf16)
        return carry

    lax.fori_loop(0, features // LANES, chunk, 0)


def epilogue(m, norm_blocks, x, upstream, saved, taps, gain, before=(), earlier=()):
    _, frames, features = x.shape
    seqs = len(norm_blocks)
    lead = round_up(taps.shape[0] // 2, 8)
    last = bool(before)
    return pl.pallas_call(
        functools.partial(epilogue_body, m, seqs, last, len(earlier)),
        out_shape=(
            jax.ShapeDtypeStruct(x.shape if last else (frames, features), bf16),
            jax.ShapeDtypeStruct((taps.shape[0] + 1, features), bf16 if last else f32),
        ),
        in_specs=whole(seqs) + far(2) + whole(5 + len(before)) + after(len(earlier)),
        out_specs=tuple(whole(2)),
        scratch_shapes=[
            pltpu.VMEM((frames, features), f32),
            pltpu.VMEM((frames + 2 * lead, LANES), f32),
            pltpu.VMEM((frames + 2 * lead, LANES), f32),
        ]
        + [
            pltpu.VMEM((frames, features), bf16),
            pltpu.VMEM((frames, features), bf16),
            pltpu.SemaphoreType.DMA((2,)),
        ],
        compiler_params=params(16),
        cost_estimate=cost(COSTS[11 + m]),
        name="norm_conv_back",
    )(*norm_blocks, x, upstream, *saved, taps, gain, *before, *earlier)


def tree_sum(terms):
    while len(terms) > 1:
        terms = [terms[i] + terms[i + 1] for i in range(0, len(terms), 2)]
    return terms[0]


def last_sum_body(*refs):
    term_refs, taps_ref, gain_ref = refs[:-2], refs[-2], refs[-1]
    tap_count = taps_ref.shape[0]
    total = tree_sum([ref[...].astype(f32) for ref in term_refs])
    for j in range(tap_count):
        taps_ref[j] = total[j : j + 1, :]
    gain_ref[...] = total[tap_count:, :]


def last_sum(terms):
    rows, features = terms[0].shape
    return pl.pallas_call(
        last_sum_body,
        out_shape=(
            jax.ShapeDtypeStruct((rows - 1, 1, features), f32),
            jax.ShapeDtypeStruct((1, features), f32),
        ),
        in_specs=whole(len(terms)),
        out_specs=tuple(whole(2)),
        compiler_params=params(16),
        cost_estimate=cost(COSTS[13]),
        name="last_sum",
    )(*terms)


def to_partner(array, axis, k):
    return lax.ppermute(array, axis, [(i, i ^ k) for i in range(lax.axis_size(axis))])


def from_all(array, axis):
    return [array] + [to_partner(array, axis, k) for k in range(1, lax.axis_size(axis))]


def exchanged(blocks, axis):
    return [blocks[0]] + [to_partner(blocks[k], axis, k) for k in range(1, len(blocks))]


def local(section_input, out_grad, routes, combine, kernel, norm_gain, up_weight, down_weight):
    experts = lax.axis_size("expert")
    seqs = lax.axis_size("dp")
    frames, features = section_input.shape[3:]
    top_count = routes.shape[4]
    capacity = 9 * frames * top_count // (8 * experts)
    taps = kernel.transpose(1, 0, 2)
    up_mat, down_mat = up_weight[0, 0], down_weight[0, 0]
    routes = routes[0, :, 0].transpose(0, 2, 1)
    combine = combine[0, :, 0].transpose(0, 2, 1)
    xs = section_input.reshape(MB, frames, features)
    ups = out_grad.reshape(MB, frames, features)

    sent = first_send(xs, ups, routes, combine, taps, norm_gain)
    pieces = second_send(xs, ups, routes, combine, taps, norm_gain, experts, capacity, sent)
    half = round_up(seqs // 2 * capacity, 8)
    most, last = round_up((seqs - 1) * capacity, 16), round_up(capacity, 16)
    near_places = ((0, capacity), (0, capacity))
    wide_places = ((0, capacity), (2 * capacity, 0))

    first = [sent, to_partner(sent, "dp", 1)]
    near, near_map, pieces = slots(
        first, experts, capacity, frames, near_places, exchanged(pieces, "expert")
    )
    later = passed(to_partner(sent, "dp", 2), near[0])
    first += [later, to_partner(later, "dp", 1)]
    saved = saved_frames(xs, taps, first[1])
    near = exchanged(near, "expert")

    products = functools.partial(
        expert_products,
        parts=experts,
        capacity=capacity,
        up_mat=up_mat,
        down_mat=down_mat,
        total=experts * (2 * half + most + last),
    )
    at = experts * half
    back, kept = products(near, rows=half, first_row=0, before=(), kept=(), earlier=(saved[2],), stage=4)
    early = passed(pieces, later)
    pieces = passed(pieces, near[1])
    later = passed(to_partner(early, "dp", 2), back[0])
    second = [pieces, to_partner(pieces, "dp", 1), later, to_partner(later, "dp", 1)]
    wide, wide_map, _ = slots(first[2:], experts, capacity, frames, wide_places, earlier=tuple(near[1:]))
    maps = (near_map, wide_map)
    wide = exchanged(wide, "expert")
    back, kept = products(wide, rows=half, first_row=at, before=back, kept=kept, stage=5)
    first_back = exchanged(back, "expert")
    back, kept = products(second[:-1], rows=most, first_row=2 * at, before=(), kept=kept, stage=6)
    most_back = exchanged(back, "expert")
    back, kept = products(
        second[-1:], rows=last, first_row=2 * at + experts * most, before=(), kept=kept, stage=7
    )
    last_back = exchanged(back, "expert")

    _, sent = frame_sums(
        0, maps, first_back, frames, ((0, 0, 0), (0, 1, 0), (1, 0, half), (1, 1, half)), [back[0]]
    )
    first_norm = exchanged(sent, "dp")
    (all_in, all_grad, all_acted, all_pre), sent = frame_sums(
        1, maps, most_back, frames, ((0, 0, 0), (0, 1, 0), (1, 0, 0)), [], kept
    )
    second_norm = exchanged(sent, "dp")
    over_rows = (((0,), (0,)), ((), ()))
    up_grad = lax.dot_general(all_in, all_pre, over_rows, preferred_element_type=f32).astype(bf16)
    down_grad = lax.dot_general(all_acted, all_grad, over_rows, preferred_element_type=f32).astype(bf16)
    _, sent = frame_sums(1, maps, last_back, frames, ((1, 1, 0),), [])
    second_norm.append(to_partner(sent[0], "dp", seqs - 1))
    prev, sums = epilogue(0, first_norm, xs, ups, saved, taps, norm_gain, earlier=(up_grad,))
    prev, sums = epilogue(1, second_norm, xs, ups, saved, taps, norm_gain, before=(sums, prev))
    peers = lax.axis_size("pipe")
    handed = lax.ppermute(prev, "pipe", [(i, (i - 1) % peers) for i in range(peers)])
    sums = tree_sum([term.astype(f32) for term in from_all(sums, "expert")]).astype(bf16)
    taps_grad, gain_grad = last_sum(from_all(sums, "dp"))
    return (
        handed[None, :, None],
        taps_grad.transpose(1, 0, 2),
        gain_grad,
        up_grad[None, None],
        down_grad[None, None],
    )


def solution(mesh):
    split = P("pipe", None, ("dp", "expert"), None, None)
    up_split = P("pipe", "expert", None, "dp")
    down_split = P("pipe", "expert", "dp", None)
    return jax.shard_map(
        local,
        mesh=mesh,
        in_specs=(split, split, split, split, P("pipe", None, None), P("pipe", None), up_split, down_split),
        out_specs=(split, P("pipe", None, None), P("pipe", None), up_split, down_split),
        check_vma=False,
    )
```

time: 205 us -> 174 us (0.85)
  waiting for transfers between devices: 78.4 us -> 49.7 us
  local copies, waits for them, and re-layouts: 10.8 us -> 1.8 us
  starting transfers between devices: 43.7 us -> 51 us
  Pallas kernels: 55 us -> 52.9 us
    ppermute x30 -> x36, waiting for transfers between devices: 78.4 us -> 49.7 us  [to_partner(): lax.ppermute(array, axis, [(i, i ^ k) for i in range(lax.axis_size(axis))])]
    unnamed x59 -> x26, local copies, waits for them, and re-layouts: 10.8 us -> 1.8 us
    ppermute x30 -> x36, starting transfers between devices: 43.7 us -> 51 us  [to_partner(): lax.ppermute(array, axis, [(i, i ^ k) for i in range(lax.axis_size(axis))])]
    pallas_call x2 -> x4, Pallas kernels: 31.3 us -> 25.4 us  [expert_products(): pl.pallas_call(functools.partial(expert_body, parts, rows, capacity if bl...]
    pallas_call x6 -> x11, Pallas kernels: 16.1 us -> 17.2 us  [the longest x2 10.1 us: epilogue(): pl.pallas_call(functools.partial(epilogue_body, m, seqs, last, len(earlie...]
  transfers between devices with their start and end apart: 31 -> 37, of which waited for: 10 -> 14; matrix products, arithmetic and copies ran while one was open for 8% -> 10% of each run, Pallas kernels for 23% -> 26%
where the time goes in v3:
time: 174 us
  Pallas kernels  52.9 us (30%)
  starting transfers between devices  51 us (29%)
  waiting for transfers between devices  49.7 us (29%)
  matrix products  17.3 us (10%)
  local copies, waits for them, and re-layouts  1.8 us (1%)
    ppermute x36, starting transfers between devices, to_partner(): lax.ppermute(array, axis, [(i, i ^ k) for i in range(lax.axis_size(axis))])  51 us
    ppermute x36, waiting for transfers between devices, to_partner(): lax.ppermute(array, axis, [(i, i ^ k) for i in range(lax.axis_size(axis))])  49.7 us
    pallas_call x4, Pallas kernels, expert_products(): pl.pallas_call(functools.partial(expert_body, parts, rows, capacity if bl...  25.4 us
    pallas_call x2, Pallas kernels, epilogue(): pl.pallas_call(functools.partial(epilogue_body, m, seqs, last, len(earlie...  10.1 us
    dot_general x1, matrix products, local(): lax.dot_general(all_in, all_pre, over_rows, preferred_element_type=f32)  9.29 us
    dot_general x1, matrix products, local(): lax.dot_general(all_acted, all_grad, over_rows, preferred_element_type=f32)  7.99 us
    pallas_call x3, Pallas kernels, frame_sums(): pl.pallas_call(functools.partial(frame_sums_body, m, len(blocks), frames,...  5.45 us
    pallas_call x1, Pallas kernels, second_send(): pl.pallas_call(functools.partial(second_send_body, experts, capacity), ou...  3.83 us
  transfers between devices with their start and end apart: 37, of which 14 were waited for; matrix products, arithmetic and copies ran while one was open for 10% of the time, Pallas kernels for 26%

profile of v3, /device:TPU:0, one launch (start us, length us, event | category | flops | bytes accessed | tf_op | source)
XLA Modules:
  0.0 173.7 jit_solution(5951757440751699343)
XLA Ops:
  0.6 3.2 %first_send.1._.refs_0_ = bf16[144,1536]{1,0:T(8,128)(2,1)} custom-call(bf16[2,64,1536]{2,1,0:T(8,128)(2,1)} %bitcast.32, bf16[2,64,1536]{2,1,0:T(8,128)(2,1)} %bitcast.38, s32[2,2,64]{2,1,0:T(2,128)} %bitcast.48, f32[2,2,64]{2,1,0:T(2,128)} %bitcast.50, f32[31,1,1536]{2,1,0:T(1,128)} %bitcast.42, f32[1,1536]{1,0:T(1,128)} %refs_10_.3), custom_call_target="tpu_custom_call" | custom-call | flops 1 | bytes 1 | tf_op jit(solution)/shard_map/first_send/pallas_call | solution.py:151
  3.9 3.1 %collective-permute-start = (bf16[144,1536]{1,0:T(8,128)(2,1)}, bf16[144,1536]{1,0:T(8,128)(2,1)S(1)}, u32[]{:S(2)}, u32[]{:S(2)}) collective-permute-start(bf16[144,1536]{1,0:T(8,128)(2,1)} %first_send.1._.refs_0_), channel_id=1, source_target_pairs={{0,4},{4,0},{8,12},{12,8},{1,5},{5,1},{9,13},{13,9},{2,6},{6,2},{1... | collective-permute-start | bytes 1327112 | tf_op jit(solution)/shard_map/ppermute | solution.py:620
  7.0 2.6 %collective-permute-start.4 = (bf16[144,1536]{1,0:T(8,128)(2,1)}, bf16[144,1536]{1,0:T(8,128)(2,1)S(1)}, u32[]{:S(2)}, u32[]{:S(2)}) collective-permute-start(bf16[144,1536]{1,0:T(8,128)(2,1)} %first_send.1._.refs_0_), channel_id=1, source_target_pairs={{0,8},{4,12},{8,0},{12,4},{1,9},{5,13},{9,1},{13,5},{2,10},{6,14},... | collective-permute-start | bytes 1327112 | tf_op jit(solution)/shard_map/ppermute | solution.py:620
  9.6 3.8 %second_send.1 = (bf16[72,1536]{1,0:T(8,128)(2,1)}, bf16[72,1536]{1,0:T(8,128)(2,1)}, bf16[72,1536]{1,0:T(8,128)(2,1)}, bf16[72,1536]{1,0:T(8,128)(2,1)}) custom-call(bf16[2,64,1536]{2,1,0:T(8,128)(2,1)} %bitcast.33, bf16[2,64,1536]{2,1,0:T(8,128)(2,1)} %bitcast.39, s32[2,2,64]{2,1,0:T(2,128)} %bitcast.49, f32[2,2,64]{2,1,0:T(2,128)} %bitcast.51, ...), custom_call_target="tpu_custom_call" | custom-call | flops 13800000512 | bytes 1 | tf_op jit(solution)/shard_map/second_send/pallas_call | solution.py:196
  17.0 5.1 %collective-permute-done.1.refs_3_ = bf16[72,1536]{1,0:T(8,128)(2,1)S(1)} collective-permute-done((bf16[72,1536]{1,0:T(8,128)(2,1)}, bf16[72,1536]{1,0:T(8,128)(2,1)S(1)}, u32[]{:S(2)}, u32[]{:S(2)}) %collective-permute-start.1) | collective-permute-done | bytes 221216 | tf_op jit(solution)/shard_map/ppermute | solution.py:620
  22.1 4.2 %collective-permute-done.2.refs_4_ = bf16[72,1536]{1,0:T(8,128)(2,1)S(1)} collective-permute-done((bf16[72,1536]{1,0:T(8,128)(2,1)}, bf16[72,1536]{1,0:T(8,128)(2,1)S(1)}, u32[]{:S(2)}, u32[]{:S(2)}) %collective-permute-start.2) | collective-permute-done | bytes 221216 | tf_op jit(solution)/shard_map/ppermute | solution.py:620
  32.2 3.3 %collective-permute-start.10 = (bf16[4,72,1536]{2,1,0:T(8,128)(2,1)S(1)}, bf16[4,72,1536]{2,1,0:T(8,128)(2,1)S(1)}, u32[]{:S(2)}, u32[]{:S(2)}) collective-permute-start(bf16[4,72,1536]{2,1,0:T(8,128)(2,1)S(1)} %passed.6), channel_id=1, source_target_pairs={{0,8},{4,12},{8,0},{12,4},{1,9},{5,13},{9,1},{13,5},{2,10},{6,14},... | collective-permute-start | bytes 2654216 | tf_op jit(solution)/shard_map/ppermute | solution.py:620
  37.9 3.8 %collective-permute-done.6.refs_2_.refs_1_ = bf16[144,1536]{1,0:T(8,128)(2,1)S(1)} collective-permute-done((bf16[144,1536]{1,0:T(8,128)(2,1)S(1)}, bf16[144,1536]{1,0:T(8,128)(2,1)S(1)}, u32[]{:S(2)}, u32[]{:S(2)}) %collective-permute-start.6) | collective-permute-done | bytes 442400 | tf_op jit(solution)/shard_map/ppermute | solution.py:620
  41.7 8.8 %collective-permute-done.7.refs_3_.refs_2_ = bf16[144,1536]{1,0:T(8,128)(2,1)S(1)} collective-permute-done((bf16[144,1536]{1,0:T(8,128)(2,1)S(1)}, bf16[144,1536]{1,0:T(8,128)(2,1)S(1)}, u32[]{:S(2)}, u32[]{:S(2)}) %collective-permute-start.7) | collective-permute-done | bytes 442400 | tf_op jit(solution)/shard_map/ppermute | solution.py:620
  56.1 5.6 %expert_products.4 = (bf16[72,1536]{1,0:T(8,128)(2,1)S(1)}, bf16[72,1536]{1,0:T(8,128)(2,1)S(1)}, bf16[72,1536]{1,0:T(8,128)(2,1)S(1)}, bf16[72,1536]{1,0:T(8,12...) custom-call(bf16[144,1536]{1,0:T(8,128)(2,1)S(1)} %get-tuple-element, ...), custom_call_target="tpu_custom_call" | custom-call | flops 13800000512 | bytes 1 | tf_op jit(solution)/shard_map/expert_products/pallas_call | solution.py:415
  61.7 10.5 %collective-permute-done.10.refs_0_ = bf16[4,72,1536]{2,1,0:T(8,128)(2,1)S(1)} collective-permute-done((bf16[4,72,1536]{2,1,0:T(8,128)(2,1)S(1)}, bf16[4,72,1536]{2,1,0:T(8,128)(2,1)S(1)}, u32[]{:S(2)}, u32[]{:S(2)}) %collective-permute-start.10) | collective-permute-done | bytes 884768 | tf_op jit(solution)/shard_map/ppermute | solution.py:620
  73.9 5.7 %expert_products.5 = (bf16[144,1536]{1,0:T(8,128)(2,1)S(1)}, bf16[144,1536]{1,0:T(8,128)(2,1)S(1)}, bf16[144,1536]{1,0:T(8,128)(2,1)S(1)}, bf16[144,1536]{1,0:T(...) custom-call(bf16[144,1536]{1,0:T(8,128)(2,1)S(1)} %get-tuple-element, ...), custom_call_target="tpu_custom_call", output_to_operand_aliasing={{4}: (10, {}), {5}: (11, {}), {6}: (12, {}), {7}: (13, {})} | custom-call | flops 1 | bytes 1 | tf_op jit(solution)/shard_map/expert_products/pallas_call | solution.py:415
  83.1 5.4 %collective-permute-done.9.refs_1_ = bf16[4,72,1536]{2,1,0:T(8,128)(2,1)S(1)} collective-permute-done((bf16[4,72,1536]{2,1,0:T(8,128)(2,1)S(1)}, bf16[4,72,1536]{2,1,0:T(8,128)(2,1)S(1)}, u32[]{:S(2)}, u32[]{:S(2)}) %collective-permute-start.9) | collective-permute-done | bytes 884768 | tf_op jit(solution)/shard_map/ppermute | solution.py:620
  88.5 8.8 %expert_products.6 = (bf16[112,1536]{1,0:T(8,128)(2,1)S(1)}, bf16[112,1536]{1,0:T(8,128)(2,1)S(1)}, bf16[112,1536]{1,0:T(8,128)(2,1)S(1)}, bf16[112,1536]{1,0:T(...) custom-call(bf16[4,72,1536]{2,1,0:T(8,128)(2,1)S(1)} %passed.5.refs_, ...), custom_call_target="tpu_custom_call", output_to_operand_aliasing={{4}: (5, {}), {5}: (6, {}), {6}: (7, {}), {7}: (8, {})} | custom-call | flops 1 | bytes 1 | tf_op jit(solution)/shard_map/expert_products/pallas_call | solution.py:415
  100.2 4.2 %collective-permute-done.17.refs_0_ = bf16[4,72,1536]{2,1,0:T(8,128)(2,1)S(1)} collective-permute-done((bf16[4,72,1536]{2,1,0:T(8,128)(2,1)S(1)}, bf16[4,72,1536]{2,1,0:T(8,128)(2,1)S(1)}, u32[]{:S(2)}, u32[]{:S(2)}) %collective-permute-start.17) | collective-permute-done | bytes 884768 | tf_op jit(solution)/shard_map/ppermute | solution.py:620
  106.6 5.3 %expert_products.7 = (bf16[48,1536]{1,0:T(8,128)(2,1)S(1)}, bf16[48,1536]{1,0:T(8,128)(2,1)S(1)}, bf16[48,1536]{1,0:T(8,128)(2,1)S(1)}, bf16[48,1536]{1,0:T(8,12...) custom-call(bf16[4,72,1536]{2,1,0:T(8,128)(2,1)S(1)} %collective-per, ...), custom_call_target="tpu_custom_call", output_to_operand_aliasing={{4}: (3, {}), {5}: (4, {}), {6}: (5, {}), {7}: (6, {})} | custom-call | flops 1 | bytes 1 | tf_op jit(solution)/shard_map/expert_products/pallas_call | solution.py:415
  114.4 3.2 %collective-permute-start.28 = (bf16[64,1536]{1,0:T(8,128)(2,1)S(1)}, bf16[64,1536]{1,0:T(8,128)(2,1)S(1)}, u32[]{:S(2)}, u32[]{:S(2)}) collective-permute-start(bf16[64,1536]{1,0:T(8,128)(2,1)S(1)} %get-tuple-element.127), channel_id=1, source_target_pairs={{0,8},{4,12},{8,0},{12,4},{1,9},{5,13},{9,1},{13,5},{2,10},{6,14},... | collective-permute-start | bytes 589832 | tf_op jit(solution)/shard_map/ppermute | solution.py:620
  118.6 2.5 %collective-permute-start.22 = (bf16[48,1536]{1,0:T(8,128)(2,1)S(1)}, bf16[48,1536]{1,0:T(8,128)(2,1)S(1)}, u32[]{:S(2)}, u32[]{:S(2)}) collective-permute-start(bf16[48,1536]{1,0:T(8,128)(2,1)S(1)} %get-tuple-element.118), channel_id=1, source_target_pairs={{0,3},{1,2},{2,1},{3,0},{4,7},{5,6},{6,5},{7,4},{8,11},{9,10},{10,... | collective-permute-start | bytes 442376 | tf_op jit(solution)/shard_map/ppermute | solution.py:620
  124.9 2.5 %collective-permute-start.19 = (bf16[64,1536]{1,0:T(8,128)(2,1)S(1)}, bf16[64,1536]{1,0:T(8,128)(2,1)S(1)}, u32[]{:S(2)}, u32[]{:S(2)}) collective-permute-start(bf16[64,1536]{1,0:T(8,128)(2,1)S(1)} %get-tuple-element.114), channel_id=1, source_target_pairs={{0,8},{4,12},{8,0},{12,4},{1,9},{5,13},{9,1},{13,5},{2,10},{6,14},... | collective-permute-start | bytes 589832 | tf_op jit(solution)/shard_map/ppermute | solution.py:620
  130.6 9.3 %convolution_convert_fusion.1.refs_11_ = bf16[1536,1536]{1,0:T(8,128)(2,1)S(1)} fusion(bf16[1216,1536]{1,0:T(8,128)(2,1)} %get-tuple-element.129, bf16[1216,1536]{1,0:T(8,128)(2,1)} %get-tuple-element.130), kind=kOutput, calls=%fused_computation.1 | convolution fusion | flops 5740167168 | bytes 12189696 | tf_op jit(solution)/shard_map/dot_general | solution.py:695
  140.0 4.9 %norm_conv_back.2 = (bf16[64,1536]{1,0:T(8,128)(2,1)S(1)}, f32[32,1536]{1,0:T(8,128)S(1)}) custom-call(f32[64,1536]{1,0:T(8,128)S(1)} %get-tuple-element.125.refs_0_, bf16[64,1536]{1,0:T(8,128)(2,1)S(1)} %collective-permute-done.27.refs_1_, bf16[64,1536]{1,0:T(8,128)(2,1)S(1)} %collective-permute-done.28.refs_2_, ...), custom_call_target="tpu_custom_call" | custom-call | flops 1 | bytes 1 | tf_op jit(solution)/shard_map/norm_conv_back/pallas_call | solution.py:564
  145.0 5.1 %norm_conv_back.3 = (bf16[2,64,1536]{2,1,0:T(8,128)(2,1)S(1)}, bf16[32,1536]{1,0:T(8,128)(2,1)S(1)}) custom-call(f32[64,1536]{1,0:T(8,128)S(1)} %get-tuple-element.112.refs_0_, bf16[64,1536]{1,0:T(8,128)(2,1)S(1)} %collective-permute-done.18.refs_1_, bf16[64,1536]{1,0:T(8,128)(2,1)S(1)} %collective-permute-done.19.refs_2_, ...), custom_call_target="tpu_custom_call" | custom-call | flops 1 | bytes 1 | tf_op jit(solution)/shard_map/norm_conv_back/pallas_call | solution.py:564
  157.4 4.3 %collective-permute-start.34 = (bf16[32,1536]{1,0:T(8,128)(2,1)S(1)}, bf16[32,1536]{1,0:T(8,128)(2,1)S(1)}, u32[]{:S(2)}, u32[]{:S(2)}) collective-permute-start(bf16[32,1536]{1,0:T(8,128)(2,1)S(1)} %add_convert_fusion.refs_0_), channel_id=1, source_target_pairs={{0,4},{4,0},{8,12},{12,8},{1,5},{5,1},{9,13},{13,9},{2,6},{6,2},{1... | collective-permute-start | bytes 294920 | tf_op jit(solution)/shard_map/ppermute | solution.py:620
  164.2 8.0 %fusion = bf16[1,1,1536,1536]{3,2,1,0:T(8,128)(2,1)} fusion(bf16[1216,1536]{1,0:T(8,128)(2,1)S(1)} %copy-done.9, bf16[1216,1536]{1,0:T(8,128)(2,1)S(1)} %copy-done.8), kind=kOutput, calls=%fused_computation.2 | convolution fusion | flops 5740167168 | bytes 12189696 | tf_op jit(solution)/shard_map/dot_general | solution.py:696
  (99 shorter events, 49.5 us)
Async XLA Ops:
  3.9 22.8 %collective-permute-start = (bf16[144,1536]{1,0:T(8,128)(2,1)}, bf16[144,1536]{1,0:T(8,128)(2,1)S(1)}, u32[]{:S(2)}, u32[]{:S(2)}) collective-permute-start(bf16[144,1536]{1,0:T(8,128)(2,1)} %first_send.1._.refs_0_), channel_id=1, source_target_pairs={{0,4},{4,0},{8,12},{12,8},{1,5},{5,1},{9,13},{13,9},{2,6},{6,2},{1... | collective-permute-start | bytes 1327112 | tf_op jit(solution)/shard_map/ppermute | solution.py:620
  7.0 25.1 %collective-permute-start.4 = (bf16[144,1536]{1,0:T(8,128)(2,1)}, bf16[144,1536]{1,0:T(8,128)(2,1)S(1)}, u32[]{:S(2)}, u32[]{:S(2)}) collective-permute-start(bf16[144,1536]{1,0:T(8,128)(2,1)} %first_send.1._.refs_0_), channel_id=1, source_target_pairs={{0,8},{4,12},{8,0},{12,4},{1,9},{5,13},{9,1},{13,5},{2,10},{6,14},... | collective-permute-start | bytes 1327112 | tf_op jit(solution)/shard_map/ppermute | solution.py:620
  30.2 20.2 %collective-permute-start.7 = (bf16[144,1536]{1,0:T(8,128)(2,1)S(1)}, bf16[144,1536]{1,0:T(8,128)(2,1)S(1)}, u32[]{:S(2)}, u32[]{:S(2)}) collective-permute-start(bf16[144,1536]{1,0:T(8,128)(2,1)S(1)} %get-tuple-element.79), channel_id=1, source_target_pairs={{0,2},{1,3},{2,0},{3,1},{4,6},{5,7},{6,4},{7,5},{8,10},{9,11},{10,... | collective-permute-start | bytes 1327112 | tf_op jit(solution)/shard_map/ppermute | solution.py:620
  31.7 18.7 %collective-permute-start.8 = (bf16[144,1536]{1,0:T(8,128)(2,1)S(1)}, bf16[144,1536]{1,0:T(8,128)(2,1)S(1)}, u32[]{:S(2)}, u32[]{:S(2)}) collective-permute-start(bf16[144,1536]{1,0:T(8,128)(2,1)S(1)} %get-tuple-element.80), channel_id=1, source_target_pairs={{0,3},{1,2},{2,1},{3,0},{4,7},{5,6},{6,5},{7,4},{8,11},{9,10},{10,... | collective-permute-start | bytes 1327112 | tf_op jit(solution)/shard_map/ppermute | solution.py:620
  32.0 19.6 %collective-permute-start.5 = (bf16[144,1536]{1,0:T(8,128)(2,1)S(1)}, bf16[144,1536]{1,0:T(8,128)(2,1)S(1)}, u32[]{:S(2)}, u32[]{:S(2)}) collective-permute-start(bf16[144,1536]{1,0:T(8,128)(2,1)S(1)} %passed.4.refs_0_.refs_1_), channel_id=1, source_target_pairs={{0,4},{4,0},{8,12},{12,8},{1,5},{5,1},{9,13},{13,9},{2,6},{6,2},{1... | collective-permute-start | bytes 1327112 | tf_op jit(solution)/shard_map/ppermute | solution.py:620
  32.2 40.1 %collective-permute-start.10 = (bf16[4,72,1536]{2,1,0:T(8,128)(2,1)S(1)}, bf16[4,72,1536]{2,1,0:T(8,128)(2,1)S(1)}, u32[]{:S(2)}, u32[]{:S(2)}) collective-permute-start(bf16[4,72,1536]{2,1,0:T(8,128)(2,1)S(1)} %passed.6), channel_id=1, source_target_pairs={{0,8},{4,12},{8,0},{12,4},{1,9},{5,13},{9,1},{13,5},{2,10},{6,14},... | collective-permute-start | bytes 2654216 | tf_op jit(solution)/shard_map/ppermute | solution.py:620
  52.5 19.7 %collective-permute-start.11 = (bf16[144,1536]{1,0:T(8,128)(2,1)S(1)}, bf16[144,1536]{1,0:T(8,128)(2,1)S(1)}, u32[]{:S(2)}, u32[]{:S(2)}) collective-permute-start(bf16[144,1536]{1,0:T(8,128)(2,1)S(1)} %get-tuple-element.86), channel_id=1, source_target_pairs={{0,1},{1,0},{2,3},{3,2},{4,5},{5,4},{6,7},{7,6},{8,9},{9,8},{10,11... | collective-permute-start | bytes 1327112 | tf_op jit(solution)/shard_map/ppermute | solution.py:620
  53.9 20.0 %collective-permute-start.12 = (bf16[144,1536]{1,0:T(8,128)(2,1)S(1)}, bf16[144,1536]{1,0:T(8,128)(2,1)S(1)}, u32[]{:S(2)}, u32[]{:S(2)}) collective-permute-start(bf16[144,1536]{1,0:T(8,128)(2,1)S(1)} %get-tuple-element.87), channel_id=1, source_target_pairs={{0,2},{1,3},{2,0},{3,1},{4,6},{5,7},{6,4},{7,5},{8,10},{9,11},{10,... | collective-permute-start | bytes 1327112 | tf_op jit(solution)/shard_map/ppermute | solution.py:620
  55.4 18.5 %collective-permute-start.13 = (bf16[144,1536]{1,0:T(8,128)(2,1)S(1)}, bf16[144,1536]{1,0:T(8,128)(2,1)S(1)}, u32[]{:S(2)}, u32[]{:S(2)}) collective-permute-start(bf16[144,1536]{1,0:T(8,128)(2,1)S(1)} %get-tuple-element.88), channel_id=1, source_target_pairs={{0,3},{1,2},{2,1},{3,0},{4,7},{5,6},{6,5},{7,4},{8,11},{9,10},{10,... | collective-permute-start | bytes 1327112 | tf_op jit(solution)/shard_map/ppermute | solution.py:620
  56.0 32.5 %collective-permute-start.9 = (bf16[4,72,1536]{2,1,0:T(8,128)(2,1)S(1)}, bf16[4,72,1536]{2,1,0:T(8,128)(2,1)S(1)}, u32[]{:S(2)}, u32[]{:S(2)}) collective-permute-start(bf16[4,72,1536]{2,1,0:T(8,128)(2,1)S(1)} %passed.5.refs_0_), channel_id=1, source_target_pairs={{0,4},{4,0},{8,12},{12,8},{1,5},{5,1},{9,13},{13,9},{2,6},{6,2},{1... | collective-permute-start | bytes 2654216 | tf_op jit(solution)/shard_map/ppermute | solution.py:620
  72.2 32.3 %collective-permute-start.17 = (bf16[4,72,1536]{2,1,0:T(8,128)(2,1)S(1)}, bf16[4,72,1536]{2,1,0:T(8,128)(2,1)S(1)}, u32[]{:S(2)}, u32[]{:S(2)}) collective-permute-start(bf16[4,72,1536]{2,1,0:T(8,128)(2,1)S(1)} %passed.7.refs_2_), channel_id=1, source_target_pairs={{0,4},{4,0},{8,12},{12,8},{1,5},{5,1},{9,13},{13,9},{2,6},{6,2},{1... | collective-permute-start | bytes 2654216 | tf_op jit(solution)/shard_map/ppermute | solution.py:620
  79.6 19.1 %collective-permute-start.24 = (bf16[144,1536]{1,0:T(8,128)(2,1)S(1)}, bf16[144,1536]{1,0:T(8,128)(2,1)S(1)}, u32[]{:S(2)}, u32[]{:S(2)}) collective-permute-start(bf16[144,1536]{1,0:T(8,128)(2,1)S(1)} %get-tuple-element.122), channel_id=1, source_target_pairs={{0,1},{1,0},{2,3},{3,2},{4,5},{5,4},{6,7},{7,6},{8,9},{9,8},{10,11... | collective-permute-start | bytes 1327112 | tf_op jit(solution)/shard_map/ppermute | solution.py:620
  80.9 31.1 %collective-permute-start.25 = (bf16[144,1536]{1,0:T(8,128)(2,1)S(1)}, bf16[144,1536]{1,0:T(8,128)(2,1)S(1)}, u32[]{:S(2)}, u32[]{:S(2)}) collective-permute-start(bf16[144,1536]{1,0:T(8,128)(2,1)S(1)} %get-tuple-element.123), channel_id=1, source_target_pairs={{0,2},{1,3},{2,0},{3,1},{4,6},{5,7},{6,4},{7,5},{8,10},{9,11},{10,... | collective-permute-start | bytes 1327112 | tf_op jit(solution)/shard_map/ppermute | solution.py:620
  81.7 30.3 %collective-permute-start.26 = (bf16[144,1536]{1,0:T(8,128)(2,1)S(1)}, bf16[144,1536]{1,0:T(8,128)(2,1)S(1)}, u32[]{:S(2)}, u32[]{:S(2)}) collective-permute-start(bf16[144,1536]{1,0:T(8,128)(2,1)S(1)} %get-tuple-element.124), channel_id=1, source_target_pairs={{0,3},{1,2},{2,1},{3,0},{4,7},{5,6},{6,5},{7,4},{8,11},{9,10},{10,... | collective-permute-start | bytes 1327112 | tf_op jit(solution)/shard_map/ppermute | solution.py:620
  97.3 20.2 %collective-permute-start.14 = (bf16[112,1536]{1,0:T(8,128)(2,1)S(1)}, bf16[112,1536]{1,0:T(8,128)(2,1)S(1)}, u32[]{:S(2)}, u32[]{:S(2)}) collective-permute-start(bf16[112,1536]{1,0:T(8,128)(2,1)S(1)} %get-tuple-element.101), channel_id=1, source_target_pairs={{0,1},{1,0},{2,3},{3,2},{4,5},{5,4},{6,7},{7,6},{8,9},{9,8},{10,11... | collective-permute-start | bytes 1032200 | tf_op jit(solution)/shard_map/ppermute | solution.py:620
  98.7 19.4 %collective-permute-start.15 = (bf16[112,1536]{1,0:T(8,128)(2,1)S(1)}, bf16[112,1536]{1,0:T(8,128)(2,1)S(1)}, u32[]{:S(2)}, u32[]{:S(2)}) collective-permute-start(bf16[112,1536]{1,0:T(8,128)(2,1)S(1)} %get-tuple-element.102), channel_id=1, source_target_pairs={{0,2},{1,3},{2,0},{3,1},{4,6},{5,7},{6,4},{7,5},{8,10},{9,11},{10,... | collective-permute-start | bytes 1032200 | tf_op jit(solution)/shard_map/ppermute | solution.py:620
  114.3 14.4 %collective-permute-start.27 = (bf16[64,1536]{1,0:T(8,128)(2,1)S(1)}, bf16[64,1536]{1,0:T(8,128)(2,1)S(1)}, u32[]{:S(2)}, u32[]{:S(2)}) collective-permute-start(bf16[64,1536]{1,0:T(8,128)(2,1)S(1)} %get-tuple-element.126), channel_id=1, source_target_pairs={{0,4},{4,0},{8,12},{12,8},{1,5},{5,1},{9,13},{13,9},{2,6},{6,2},{1... | collective-permute-start | bytes 589832 | tf_op jit(solution)/shard_map/ppermute | solution.py:620
  114.4 25.6 %collective-permute-start.28 = (bf16[64,1536]{1,0:T(8,128)(2,1)S(1)}, bf16[64,1536]{1,0:T(8,128)(2,1)S(1)}, u32[]{:S(2)}, u32[]{:S(2)}) collective-permute-start(bf16[64,1536]{1,0:T(8,128)(2,1)S(1)} %get-tuple-element.127), channel_id=1, source_target_pairs={{0,8},{4,12},{8,0},{12,4},{1,9},{5,13},{9,1},{13,5},{2,10},{6,14},... | collective-permute-start | bytes 589832 | tf_op jit(solution)/shard_map/ppermute | solution.py:620
  122.9 17.0 %collective-permute-start.29 = (bf16[64,1536]{1,0:T(8,128)(2,1)S(1)}, bf16[64,1536]{1,0:T(8,128)(2,1)S(1)}, u32[]{:S(2)}, u32[]{:S(2)}) collective-permute-start(bf16[64,1536]{1,0:T(8,128)(2,1)S(1)} %get-tuple-element.128), channel_id=1, source_target_pairs={{0,12},{4,8},{8,4},{12,0},{1,13},{5,9},{9,5},{13,1},{2,14},{6,10},... | collective-permute-start | bytes 589832 | tf_op jit(solution)/shard_map/ppermute | solution.py:620
  124.8 20.1 %collective-permute-start.18 = (bf16[64,1536]{1,0:T(8,128)(2,1)S(1)}, bf16[64,1536]{1,0:T(8,128)(2,1)S(1)}, u32[]{:S(2)}, u32[]{:S(2)}) collective-permute-start(bf16[64,1536]{1,0:T(8,128)(2,1)S(1)} %get-tuple-element.113), channel_id=1, source_target_pairs={{0,4},{4,0},{8,12},{12,8},{1,5},{5,1},{9,13},{13,9},{2,6},{6,2},{1... | collective-permute-start | bytes 589832 | tf_op jit(solution)/shard_map/ppermute | solution.py:620
  124.9 20.1 %collective-permute-start.19 = (bf16[64,1536]{1,0:T(8,128)(2,1)S(1)}, bf16[64,1536]{1,0:T(8,128)(2,1)S(1)}, u32[]{:S(2)}, u32[]{:S(2)}) collective-permute-start(bf16[64,1536]{1,0:T(8,128)(2,1)S(1)} %get-tuple-element.114), channel_id=1, source_target_pairs={{0,8},{4,12},{8,0},{12,4},{1,9},{5,13},{9,1},{13,5},{2,10},{6,14},... | collective-permute-start | bytes 589832 | tf_op jit(solution)/shard_map/ppermute | solution.py:620
  128.7 16.3 %collective-permute-start.23 = (bf16[64,1536]{1,0:T(8,128)(2,1)S(1)}, bf16[64,1536]{1,0:T(8,128)(2,1)S(1)}, u32[]{:S(2)}, u32[]{:S(2)}) collective-permute-start(bf16[64,1536]{1,0:T(8,128)(2,1)S(1)} %frame_sums.4), channel_id=1, source_target_pairs={{0,12},{4,8},{8,4},{12,0},{1,13},{5,9},{9,5},{13,1},{2,14},{6,10},... | collective-permute-start | bytes 589832 | tf_op jit(solution)/shard_map/ppermute | solution.py:620
  153.8 19.2 %collective-permute-start.30 = (bf16[2,64,1536]{2,1,0:T(8,128)(2,1)S(1)}, bf16[2,64,1536]{2,1,0:T(8,128)(2,1)S(1)}, u32[]{:S(2)}, u32[]{:S(2)}) collective-permute-start(bf16[2,64,1536]{2,1,0:T(8,128)(2,1)S(1)} %get-tuple-element.133), channel_id=1, source_target_pairs={{0,16},{16,0},{1,17},{17,1},{2,18},{18,2},{3,19},{19,3},{4,20},{20... | collective-permute-start | bytes 1179656 | tf_op jit(solution)/shard_map/ppermute | solution.py:702
  157.4 14.7 %collective-permute-start.34 = (bf16[32,1536]{1,0:T(8,128)(2,1)S(1)}, bf16[32,1536]{1,0:T(8,128)(2,1)S(1)}, u32[]{:S(2)}, u32[]{:S(2)}) collective-permute-start(bf16[32,1536]{1,0:T(8,128)(2,1)S(1)} %add_convert_fusion.refs_0_), channel_id=1, source_target_pairs={{0,4},{4,0},{8,12},{12,8},{1,5},{5,1},{9,13},{13,9},{2,6},{6,2},{1... | collective-permute-start | bytes 294920 | tf_op jit(solution)/shard_map/ppermute | solution.py:620
  (25 other events, 323.5 us)

commit v4 on v3

--- a/solution.py
+++ b/solution.py
@@ -15,7 +15,7 @@
 SEND_MIB = 60
 EXPERT_MIB = 24
 NOWHERE = -512.0
-COSTS = (0, 0, 0, 0, 12, 0, 0, 0, 0, 2, 0, 0, 0, 0, 12)
+COSTS = (0, 0, 0, 0, 12, 0, 10, 0, 0, 2, 0, 0, 0, 0, 12, 0)
 MIB = 1024 * 1024
 SMALL = pl.CostEstimate(flops=1, bytes_accessed=1, transcendentals=0)
 bf16 = jnp.bfloat16
@@ -440,8 +440,8 @@
     return out[:parts], out[parts:]
 
 
-def frame_sums_body(m, experts, frames, pieces, *refs):
-    map_refs, slot_refs, out_refs, picking = refs[:2], refs[2 : 2 + experts], refs[-1 - len(pieces) : -1], refs[-1]
+def frame_sums_body(m, experts, frames, pieces, groups, *refs):
+    map_refs, slot_refs, out_refs, picking = refs[:2], refs[2 : 2 + experts], refs[-1 - len(groups) : -1], refs[-1]
     total = len(pieces) * frames
     rows = slot_refs[0].shape[0]
     same = lax.broadcasted_iota(jnp.int32, (frames, frames), 0) == lax.broadcasted_iota(
@@ -467,25 +467,27 @@
         acc = jnp.zeros((total, PART), f32)
         for e in range(experts):
             acc = acc + jnp.dot(picking[e], slot_refs[e][:, cols], preferred_element_type=f32)
-        for i, out_ref in enumerate(out_refs):
-            out_ref[:, cols] = acc[i * frames : (i + 1) * frames, :].astype(out_ref.dtype)
+        for group, out_ref in zip(groups, out_refs):
+            for place, i in enumerate(group):
+                out_ref[place * frames : (place + 1) * frames, cols] = acc[
+                    i * frames : (i + 1) * frames, :
+                ].astype(out_ref.dtype)
         return carry
 
     lax.fori_loop(0, slot_refs[0].shape[1] // PART, feature, 0)
 
 
-def frame_sums(m, maps, blocks, frames, pieces, earlier, handed=()):
+def frame_sums(m, maps, blocks, frames, pieces, groups, earlier, handed=()):
     rows, features = blocks[0].shape
     first = 2 + len(blocks) + len(earlier)
     out = pl.pallas_call(
-        functools.partial(frame_sums_body, m, len(blocks), frames, pieces),
+        functools.partial(frame_sums_body, m, len(blocks), frames, pieces, tuple(g for g, _ in groups)),
         out_shape=tuple(pltpu.HBM(h.shape, h.dtype) for h in handed)
         + tuple(
-            jax.ShapeDtypeStruct((frames, features), f32 if piece[:2] == (0, 0) else bf16)
-            for piece in pieces
+            jax.ShapeDtypeStruct((len(group) * frames, features), kind) for group, kind in groups
         ),
         in_specs=whole(2 + len(blocks)) + after(len(earlier)) + far(len(handed)),
-        out_specs=tuple(far(len(handed)) + whole(len(pieces))),
+        out_specs=tuple(far(len(handed)) + whole(len(groups))),
         input_output_aliases={first + i: i for i in range(len(handed))},
         scratch_shapes=[pltpu.VMEM((len(blocks), len(pieces) * frames, rows), bf16)],
         compiler_params=params(16),
@@ -495,13 +497,30 @@
     return out[: len(handed)], out[len(handed) :]
 
 
+def pair_sum_body(own_ref, got_ref, out_ref):
+    first = got_ref.shape[0] - own_ref.shape[0]
+    out_ref[...] = (own_ref[...] + got_ref[first:, :].astype(f32)).astype(bf16)
+
+
+def pair_sum(own, got):
+    return pl.pallas_call(
+        pair_sum_body,
+        out_shape=jax.ShapeDtypeStruct(own.shape, bf16),
+        in_specs=whole(2),
+        out_specs=whole(1)[0],
+        compiler_params=params(16),
+        cost_estimate=cost(COSTS[15]),
+        name="pair_sum",
+    )(own, got)
+
+
 def epilogue_body(m, seqs, last, waits, *refs):
     norm_refs = refs[:seqs]
     (x_all, up_all, conv_ref, mixed_ref, scale_ref, taps_ref, gain_ref) = refs[seqs : seqs + 7]
     before, refs = refs[seqs + 7 : seqs + 7 + 2 * last], refs[seqs + 7 + 2 * last + waits :]
     if last:
         sums_ref, other_ref = before
-    prev_ref, term_ref, norm_grad, pad_x, pad_g, x_ref, up_ref, sems = refs
+    prev_ref, term_ref, norm_grad, pad_x, pad_g, parts, gain_parts, x_ref, up_ref, sems = refs
     if last:
         prev_ref[0] = other_ref[...]
         prev_ref = prev_ref.at[1]
@@ -515,19 +534,17 @@
     pad_g[...] = jnp.zeros(pad_g.shape, f32)
     scale = scale_ref[...]
 
-    def put(row, cols, value):
-        if last:
-            value = value + sums_ref[row : row + 1, cols]
-        term_ref[row : row + 1, cols] = value.astype(term_ref.dtype)
+    def tiles_sum(values):
+        return jnp.sum(values.reshape(frames // 8, 8, LANES), axis=0)
 
     def gather(c, inner):
         cols = pl.ds(pl.multiple_of(c * LANES, LANES), LANES)
-        grad = norm_refs[0][:, cols].astype(f32)
+        grad = norm_refs[0][:frames, cols].astype(f32)
         for k in range(1, seqs):
-            grad = grad + norm_refs[k][:, cols].astype(f32)
+            grad = grad + norm_refs[k][:frames, cols].astype(f32)
         norm_grad[:, cols] = grad
         weighed = grad * mixed_ref[:, cols]
-        put(tap_count, cols, jnp.sum(weighed * scale, axis=0, keepdims=True))
+        gain_parts[c] = tiles_sum(weighed * scale)
         return inner + weighed * gain_ref[:, cols]
 
     inner = lax.fori_loop(0, features // LANES, gather, jnp.zeros((frames, LANES), f32))
@@ -547,10 +564,17 @@
         pad_g[lead : lead + frames, :] = conv_grad
         acc = mixed_grad
         for j, rows in shifted(pad_x, [lead + j - margin for j in range(tap_count)], frames):
-            put(j, cols, jnp.sum(conv_grad * rows, axis=0, keepdims=True))
+            parts[8 * j : 8 * j + 8, :] = tiles_sum(conv_grad * rows)
         for j, rows in shifted(pad_g, [lead + margin - j for j in range(tap_count)], frames):
             acc = acc + taps_ref[j, :, cols] * rows
         prev_ref[:, cols] = acc.astype(bf16)
+        parts[8 * tap_count :, :] = gain_parts[c]
+        sums = parts[pl.ds(0, tap_count + 1, stride=8), :]
+        for row in range(1, 8):
+            sums = sums + parts[pl.ds(row, tap_count + 1, stride=8), :]
+        if last:
+            sums = sums + sums_ref[:, cols]
+        term_ref[:, cols] = sums.astype(term_ref.dtype)
         return carry
 
     lax.fori_loop(0, features // LANES, chunk, 0)
@@ -573,6 +597,8 @@
             pltpu.VMEM((frames, features), f32),
             pltpu.VMEM((frames + 2 * lead, LANES), f32),
             pltpu.VMEM((frames + 2 * lead, LANES), f32),
+            pltpu.VMEM((8 * (taps.shape[0] + 1), LANES), f32),
+            pltpu.VMEM((features // LANES, 8, LANES), f32),
         ]
         + [
             pltpu.VMEM((frames, features), bf16),
@@ -644,7 +670,7 @@
     sent = first_send(xs, ups, routes, combine, taps, norm_gain)
     pieces = second_send(xs, ups, routes, combine, taps, norm_gain, experts, capacity, sent)
     half = round_up(seqs // 2 * capacity, 8)
-    most, last = round_up((seqs - 1) * capacity, 16), round_up(capacity, 16)
+    most, last = round_up((seqs - 1) * capacity, 8), round_up(capacity, 8)
     near_places = ((0, capacity), (0, capacity))
     wide_places = ((0, capacity), (2 * capacity, 0))
 
@@ -667,9 +693,8 @@
     )
     at = experts * half
     back, kept = products(near, rows=half, first_row=0, before=(), kept=(), earlier=(saved[2],), stage=4)
-    early = passed(pieces, later)
-    pieces = passed(pieces, near[1])
-    later = passed(to_partner(early, "dp", 2), back[0])
+    pieces = passed(pieces, later)
+    later = passed(to_partner(pieces, "dp", 2), back[0])
     second = [pieces, to_partner(pieces, "dp", 1), later, to_partner(later, "dp", 1)]
     wide, wide_map, _ = slots(first[2:], experts, capacity, frames, wide_places, earlier=tuple(near[1:]))
     maps = (near_map, wide_map)
@@ -678,23 +703,37 @@
     first_back = exchanged(back, "expert")
     back, kept = products(second[:-1], rows=most, first_row=2 * at, before=(), kept=kept, stage=6)
     most_back = exchanged(back, "expert")
+
+    _, (own_sum, far_sum, sent) = frame_sums(
+        0,
+        maps,
+        first_back,
+        frames,
+        ((0, 0, 0), (0, 1, 0), (1, 0, half), (1, 1, half)),
+        (((0,), f32), ((2,), f32), ((1, 3), bf16)),
+        [back[0]],
+    )
+    got = to_partner(sent, "dp", 1)
+    first_norm = [own_sum, got, to_partner(pair_sum(far_sum, got), "dp", 2)]
     back, kept = products(
-        second[-1:], rows=last, first_row=2 * at + experts * most, before=(), kept=kept, stage=7
+        second[-1:], rows=last, first_row=2 * at + experts * most, before=(), kept=kept, stage=7, earlier=(own_sum,)
     )
     last_back = exchanged(back, "expert")
-
-    _, sent = frame_sums(
-        0, maps, first_back, frames, ((0, 0, 0), (0, 1, 0), (1, 0, half), (1, 1, half)), [back[0]]
-    )
-    first_norm = exchanged(sent, "dp")
     (all_in, all_grad, all_acted, all_pre), sent = frame_sums(
-        1, maps, most_back, frames, ((0, 0, 0), (0, 1, 0), (1, 0, 0)), [], kept
+        1,
+        maps,
+        most_back,
+        frames,
+        ((0, 0, 0), (0, 1, 0), (1, 0, 0)),
+        (((0,), f32), ((1,), bf16), ((2,), bf16)),
+        [],
+        kept,
     )
     second_norm = exchanged(sent, "dp")
     over_rows = (((0,), (0,)), ((), ()))
     up_grad = lax.dot_general(all_in, all_pre, over_rows, preferred_element_type=f32).astype(bf16)
     down_grad = lax.dot_general(all_acted, all_grad, over_rows, preferred_element_type=f32).astype(bf16)
-    _, sent = frame_sums(1, maps, last_back, frames, ((1, 1, 0),), [])
+    _, sent = frame_sums(1, maps, last_back, frames, ((1, 1, 0),), (((0,), bf16),), [])
     second_norm.append(to_partner(sent[0], "dp", seqs - 1))
     prev, sums = epilogue(0, first_norm, xs, ups, saved, taps, norm_gain, earlier=(up_grad,))
     prev, sums = epilogue(1, second_norm, xs, ups, saved, taps, norm_gain, before=(sums, prev))

time: 174 us -> 169 us (0.971)
  starting transfers between devices: 51 us -> 43.4 us
  local copies, waits for them, and re-layouts: 1.8 us -> 4.07 us
    ppermute x36 -> x35, starting transfers between devices: 51 us -> 43.4 us  [to_partner(): lax.ppermute(array, axis, [(i, i ^ k) for i in range(lax.axis_size(axis))])]
    unnamed x26 -> x23, local copies, waits for them, and re-layouts: 1.8 us -> 4.07 us
    ppermute x36 -> x35, waiting for transfers between devices: 49.7 us -> 50.3 us  [to_partner(): lax.ppermute(array, axis, [(i, i ^ k) for i in range(lax.axis_size(axis))])]
  transfers between devices with their start and end apart: 37 -> 36, of which waited for: 14 -> 14; matrix products, arithmetic and copies ran while one was open for 10% -> 10% of each run, Pallas kernels for 26% -> 26%
where the time goes in v4:
time: 169 us; the launch traced here: 168 us
  Pallas kernels  52.4 us (31%)
  waiting for transfers between devices  50.3 us (30%)
  starting transfers between devices  43.4 us (26%)
  matrix products  17.2 us (10%)
  local copies, waits for them, and re-layouts  4.07 us (2%)
    ppermute x35, waiting for transfers between devices, to_partner(): lax.ppermute(array, axis, [(i, i ^ k) for i in range(lax.axis_size(axis))])  50.3 us
    ppermute x35, starting transfers between devices, to_partner(): lax.ppermute(array, axis, [(i, i ^ k) for i in range(lax.axis_size(axis))])  43.4 us
    pallas_call x4, Pallas kernels, expert_products(): pl.pallas_call(functools.partial(expert_body, parts, rows, capacity if bl...  25.5 us
    pallas_call x2, Pallas kernels, epilogue(): pl.pallas_call(functools.partial(epilogue_body, m, seqs, last, len(earlie...  9.63 us
    dot_general x1, matrix products, local(): lax.dot_general(all_in, all_pre, over_rows, preferred_element_type=f32)  9.24 us
    dot_general x1, matrix products, local(): lax.dot_general(all_acted, all_grad, over_rows, preferred_element_type=f32)  7.98 us
    pallas_call x3, Pallas kernels, frame_sums(): pl.pallas_call(functools.partial(frame_sums_body, m, len(blocks), frames,...  5.27 us
    unnamed x23, local copies, waits for them, and re-layouts  4.07 us
  transfers between devices with their start and end apart: 36, of which 14 were waited for; matrix products, arithmetic and copies ran while one was open for 10% of the time, Pallas kernels for 26%

profile of v4, /device:TPU:0, one launch (start us, length us, event | category | flops | bytes accessed | tf_op | source)
XLA Modules:
  0.0 168.4 jit_solution(15096356974289236939)
XLA Ops:
  0.6 3.2 %first_send.1._.refs_0_ = bf16[144,1536]{1,0:T(8,128)(2,1)} custom-call(bf16[2,64,1536]{2,1,0:T(8,128)(2,1)} %bitcast.30, bf16[2,64,1536]{2,1,0:T(8,128)(2,1)} %bitcast.36, s32[2,2,64]{2,1,0:T(2,128)} %bitcast.46, f32[2,2,64]{2,1,0:T(2,128)} %bitcast.48, f32[31,1,1536]{2,1,0:T(1,128)} %bitcast.40, f32[1,1536]{1,0:T(1,128)} %refs_10_.1), custom_call_target="tpu_custom_call" | custom-call | flops 1 | bytes 1 | tf_op jit(solution)/shard_map/first_send/pallas_call | solution.py:151
  3.9 3.1 %collective-permute-start = (bf16[144,1536]{1,0:T(8,128)(2,1)}, bf16[144,1536]{1,0:T(8,128)(2,1)S(1)}, u32[]{:S(2)}, u32[]{:S(2)}) collective-permute-start(bf16[144,1536]{1,0:T(8,128)(2,1)} %first_send.1._.refs_0_), channel_id=1, source_target_pairs={{0,4},{4,0},{8,12},{12,8},{1,5},{5,1},{9,13},{13,9},{2,6},{6,2},{1... | collective-permute-start | bytes 1327112 | tf_op jit(solution)/shard_map/ppermute | solution.py:646
  7.0 2.6 %collective-permute-start.4 = (bf16[144,1536]{1,0:T(8,128)(2,1)}, bf16[144,1536]{1,0:T(8,128)(2,1)S(1)}, u32[]{:S(2)}, u32[]{:S(2)}) collective-permute-start(bf16[144,1536]{1,0:T(8,128)(2,1)} %first_send.1._.refs_0_), channel_id=1, source_target_pairs={{0,8},{4,12},{8,0},{12,4},{1,9},{5,13},{9,1},{13,5},{2,10},{6,14},... | collective-permute-start | bytes 1327112 | tf_op jit(solution)/shard_map/ppermute | solution.py:646
  9.6 3.8 %second_send.1 = (bf16[72,1536]{1,0:T(8,128)(2,1)}, bf16[72,1536]{1,0:T(8,128)(2,1)}, bf16[72,1536]{1,0:T(8,128)(2,1)}, bf16[72,1536]{1,0:T(8,128)(2,1)}) custom-call(bf16[2,64,1536]{2,1,0:T(8,128)(2,1)} %bitcast.31, bf16[2,64,1536]{2,1,0:T(8,128)(2,1)} %bitcast.37, s32[2,2,64]{2,1,0:T(2,128)} %bitcast.47, f32[2,2,64]{2,1,0:T(2,128)} %bitcast.49, ...), custom_call_target="tpu_custom_call" | custom-call | flops 13800000512 | bytes 1 | tf_op jit(solution)/shard_map/second_send/pallas_call | solution.py:196
  17.0 5.1 %collective-permute-done.1.refs_3_ = bf16[72,1536]{1,0:T(8,128)(2,1)S(1)} collective-permute-done((bf16[72,1536]{1,0:T(8,128)(2,1)}, bf16[72,1536]{1,0:T(8,128)(2,1)S(1)}, u32[]{:S(2)}, u32[]{:S(2)}) %collective-permute-start.1) | collective-permute-done | bytes 221216 | tf_op jit(solution)/shard_map/ppermute | solution.py:646
  22.1 4.2 %collective-permute-done.2.refs_4_ = bf16[72,1536]{1,0:T(8,128)(2,1)S(1)} collective-permute-done((bf16[72,1536]{1,0:T(8,128)(2,1)}, bf16[72,1536]{1,0:T(8,128)(2,1)S(1)}, u32[]{:S(2)}, u32[]{:S(2)}) %collective-permute-start.2) | collective-permute-done | bytes 221216 | tf_op jit(solution)/shard_map/ppermute | solution.py:646
  32.1 3.2 %collective-permute-start.10 = (bf16[4,72,1536]{2,1,0:T(8,128)(2,1)S(1)}, bf16[4,72,1536]{2,1,0:T(8,128)(2,1)S(1)}, u32[]{:S(2)}, u32[]{:S(2)}) collective-permute-start(bf16[4,72,1536]{2,1,0:T(8,128)(2,1)S(1)} %passed.4.refs_0_), channel_id=1, source_target_pairs={{0,8},{4,12},{8,0},{12,4},{1,9},{5,13},{9,1},{13,5},{2,10},{6,14},... | collective-permute-start | bytes 2654216 | tf_op jit(solution)/shard_map/ppermute | solution.py:646
  35.3 2.4 %saved_frames.1 = (f32[2,64,1536]{2,1,0:T(8,128)S(1)}, f32[2,64,1536]{2,1,0:T(8,128)S(1)}, f32[2,64,1]{2,1,0:T(8,128)S(1)}) custom-call(bf16[2,64,1536]{2,1,0:T(8,128)(2,1)S(1)} %bitcast.32, f32[31,1,1536]{2,1,0:T(1,128)S(1)} %bitcast.42, bf16[144,1536]{1,0:T(8,128)(2,1)S(1)} %collective-permute-done.refs_1_._), custom_call_target="tpu_custom_call" | custom-call | flops 1 | bytes 1 | tf_op jit(solution)/shard_map/saved_frames/pallas_call | solution.py:215
  37.7 3.9 %collective-permute-done.6.refs_2_.refs_1_ = bf16[144,1536]{1,0:T(8,128)(2,1)S(1)} collective-permute-done((bf16[144,1536]{1,0:T(8,128)(2,1)S(1)}, bf16[144,1536]{1,0:T(8,128)(2,1)S(1)}, u32[]{:S(2)}, u32[]{:S(2)}) %collective-permute-start.6) | collective-permute-done | bytes 442400 | tf_op jit(solution)/shard_map/ppermute | solution.py:646
  41.7 8.8 %collective-permute-done.7.refs_3_.refs_2_ = bf16[144,1536]{1,0:T(8,128)(2,1)S(1)} collective-permute-done((bf16[144,1536]{1,0:T(8,128)(2,1)S(1)}, bf16[144,1536]{1,0:T(8,128)(2,1)S(1)}, u32[]{:S(2)}, u32[]{:S(2)}) %collective-permute-start.7) | collective-permute-done | bytes 442400 | tf_op jit(solution)/shard_map/ppermute | solution.py:646
  50.4 2.4 %collective-permute-done.5.refs_1_ = bf16[144,1536]{1,0:T(8,128)(2,1)S(1)} collective-permute-done((bf16[144,1536]{1,0:T(8,128)(2,1)S(1)}, bf16[144,1536]{1,0:T(8,128)(2,1)S(1)}, u32[]{:S(2)}, u32[]{:S(2)}) %collective-permute-start.5) | collective-permute-done | bytes 442400 | tf_op jit(solution)/shard_map/ppermute | solution.py:646
  59.6 5.6 %expert_products.4 = (bf16[72,1536]{1,0:T(8,128)(2,1)S(1)}, bf16[72,1536]{1,0:T(8,128)(2,1)S(1)}, bf16[72,1536]{1,0:T(8,128)(2,1)S(1)}, bf16[72,1536]{1,0:T(8,12...) custom-call(bf16[144,1536]{1,0:T(8,128)(2,1)S(1)} %get-tuple-element, ...), custom_call_target="tpu_custom_call" | custom-call | flops 13800000512 | bytes 1 | tf_op jit(solution)/shard_map/expert_products/pallas_call | solution.py:415
  66.9 7.3 %collective-permute-done.12.refs_2_ = bf16[144,1536]{1,0:T(8,128)(2,1)S(1)} collective-permute-done((bf16[144,1536]{1,0:T(8,128)(2,1)S(1)}, bf16[144,1536]{1,0:T(8,128)(2,1)S(1)}, u32[]{:S(2)}, u32[]{:S(2)}) %collective-permute-start.12) | collective-permute-done | bytes 442400 | tf_op jit(solution)/shard_map/ppermute | solution.py:646
  74.2 5.7 %expert_products.5 = (bf16[144,1536]{1,0:T(8,128)(2,1)S(1)}, bf16[144,1536]{1,0:T(8,128)(2,1)S(1)}, bf16[144,1536]{1,0:T(8,128)(2,1)S(1)}, bf16[144,1536]{1,0:T(...) custom-call(bf16[144,1536]{1,0:T(8,128)(2,1)S(1)} %get-tuple-element, ...), custom_call_target="tpu_custom_call", output_to_operand_aliasing={{4}: (10, {}), {5}: (11, {}), {6}: (12, {}), {7}: (13, {})} | custom-call | flops 1 | bytes 1 | tf_op jit(solution)/shard_map/expert_products/pallas_call | solution.py:415
  83.5 8.8 %expert_products.6 = (bf16[112,1536]{1,0:T(8,128)(2,1)S(1)}, bf16[112,1536]{1,0:T(8,128)(2,1)S(1)}, bf16[112,1536]{1,0:T(8,128)(2,1)S(1)}, bf16[112,1536]{1,0:T(...) custom-call(bf16[4,72,1536]{2,1,0:T(8,128)(2,1)S(1)} %passed.4.refs_, ...), custom_call_target="tpu_custom_call", output_to_operand_aliasing={{4}: (5, {}), {5}: (6, {}), {6}: (7, {}), {7}: (8, {})} | custom-call | flops 11500000256 | bytes 1 | tf_op jit(solution)/shard_map/expert_products/pallas_call | solution.py:415
  93.1 6.2 %collective-permute-done.19.refs_4_ = bf16[144,1536]{1,0:T(8,128)(2,1)S(1)} collective-permute-done((bf16[144,1536]{1,0:T(8,128)(2,1)S(1)}, bf16[144,1536]{1,0:T(8,128)(2,1)S(1)}, u32[]{:S(2)}, u32[]{:S(2)}) %collective-permute-start.19) | collective-permute-done | bytes 442400 | tf_op jit(solution)/shard_map/ppermute | solution.py:646
  105.0 5.0 %collective-permute-done.27.got_ref.refs_1_ = bf16[128,1536]{1,0:T(8,128)(2,1)S(1)} collective-permute-done((bf16[128,1536]{1,0:T(8,128)(2,1)S(1)}, bf16[128,1536]{1,0:T(8,128)(2,1)S(1)}, u32[]{:S(2)}, u32[]{:S(2)}) %collective-permute-start.27) | collective-permute-done | bytes 393248 | tf_op jit(solution)/shard_map/ppermute | solution.py:646
  110.2 5.3 %expert_products.7 = (bf16[40,1536]{1,0:T(8,128)(2,1)S(1)}, bf16[40,1536]{1,0:T(8,128)(2,1)S(1)}, bf16[40,1536]{1,0:T(8,128)(2,1)S(1)}, bf16[40,1536]{1,0:T(8,12...) custom-call(bf16[4,72,1536]{2,1,0:T(8,128)(2,1)S(1)} %collective-per, ...), custom_call_target="tpu_custom_call", output_to_operand_aliasing={{4}: (4, {}), {5}: (5, {}), {6}: (6, {}), {7}: (7, {})} | custom-call | flops 1 | bytes 1 | tf_op jit(solution)/shard_map/expert_products/pallas_call | solution.py:415
  121.0 2.5 %collective-permute-start.21 = (bf16[64,1536]{1,0:T(8,128)(2,1)S(1)}, bf16[64,1536]{1,0:T(8,128)(2,1)S(1)}, u32[]{:S(2)}, u32[]{:S(2)}) collective-permute-start(bf16[64,1536]{1,0:T(8,128)(2,1)S(1)} %get-tuple-element.117), channel_id=1, source_target_pairs={{0,4},{4,0},{8,12},{12,8},{1,5},{5,1},{9,13},{13,9},{2,6},{6,2},{1... | collective-permute-start | bytes 589832 | tf_op jit(solution)/shard_map/ppermute | solution.py:646
  127.3 9.2 %convolution_convert_fusion.1.refs_10_ = bf16[1536,1536]{1,0:T(8,128)(2,1)S(1)} fusion(bf16[1184,1536]{1,0:T(8,128)(2,1)} %get-tuple-element.127, bf16[1184,1536]{1,0:T(8,128)(2,1)} %get-tuple-element.128), kind=kOutput, calls=%fused_computation.1 | convolution fusion | flops 5589172224 | bytes 11993088 | tf_op jit(solution)/shard_map/dot_general | solution.py:734
  136.6 4.8 %norm_conv_back.2 = (bf16[64,1536]{1,0:T(8,128)(2,1)S(1)}, f32[32,1536]{1,0:T(8,128)S(1)}) custom-call(f32[64,1536]{1,0:T(8,128)S(1)} %get-tuple-element.107.refs_3_.refs_0_, bf16[128,1536]{1,0:T(8,128)(2,1)S(1)} %collective-permute-done.27.got_ref.refs_1_, bf16[64,1536]{1,0:T(8,128)(2,1)S(1)} %collective-permute-done.28.refs_2_, ...), custom_call_target="tpu_custom_call" | custom-call | flops 1 | bytes 1 | tf_op jit(solution)/shard_map/norm_conv_back/pallas_call | solution.py:588
  141.5 4.8 %norm_conv_back.3 = (bf16[2,64,1536]{2,1,0:T(8,128)(2,1)S(1)}, bf16[32,1536]{1,0:T(8,128)(2,1)S(1)}) custom-call(f32[64,1536]{1,0:T(8,128)S(1)} %get-tuple-element.116.refs_0_, bf16[64,1536]{1,0:T(8,128)(2,1)S(1)} %collective-permute-done.21.refs_1_, bf16[64,1536]{1,0:T(8,128)(2,1)S(1)} %collective-permute-done.22.refs_2_, ...), custom_call_target="tpu_custom_call" | custom-call | flops 1 | bytes 1 | tf_op jit(solution)/shard_map/norm_conv_back/pallas_call | solution.py:588
  151.6 2.8 %collective-permute-done.32 = bf16[32,1536]{1,0:T(8,128)(2,1)S(1)} collective-permute-done((bf16[32,1536]{1,0:T(8,128)(2,1)S(1)}, bf16[32,1536]{1,0:T(8,128)(2,1)S(1)}, u32[]{:S(2)}, u32[]{:S(2)}) %collective-permute-start.32) | collective-permute-done | bytes 98336 | tf_op jit(solution)/shard_map/ppermute | solution.py:646
  158.9 8.0 %fusion = bf16[1,1,1536,1536]{3,2,1,0:T(8,128)(2,1)} fusion(bf16[1184,1536]{1,0:T(8,128)(2,1)S(1)} %copy-done.10, bf16[1184,1536]{1,0:T(8,128)(2,1)S(1)} %copy-done.9), kind=kOutput, calls=%fused_computation.2 | convolution fusion | flops 5589172224 | bytes 11993088 | tf_op jit(solution)/shard_map/dot_general | solution.py:735
  (93 shorter events, 48.6 us)
Async XLA Ops:
  3.9 22.8 %collective-permute-start = (bf16[144,1536]{1,0:T(8,128)(2,1)}, bf16[144,1536]{1,0:T(8,128)(2,1)S(1)}, u32[]{:S(2)}, u32[]{:S(2)}) collective-permute-start(bf16[144,1536]{1,0:T(8,128)(2,1)} %first_send.1._.refs_0_), channel_id=1, source_target_pairs={{0,4},{4,0},{8,12},{12,8},{1,5},{5,1},{9,13},{13,9},{2,6},{6,2},{1... | collective-permute-start | bytes 1327112 | tf_op jit(solution)/shard_map/ppermute | solution.py:646
  7.0 25.1 %collective-permute-start.4 = (bf16[144,1536]{1,0:T(8,128)(2,1)}, bf16[144,1536]{1,0:T(8,128)(2,1)S(1)}, u32[]{:S(2)}, u32[]{:S(2)}) collective-permute-start(bf16[144,1536]{1,0:T(8,128)(2,1)} %first_send.1._.refs_0_), channel_id=1, source_target_pairs={{0,8},{4,12},{8,0},{12,4},{1,9},{5,13},{9,1},{13,5},{2,10},{6,14},... | collective-permute-start | bytes 1327112 | tf_op jit(solution)/shard_map/ppermute | solution.py:646
  28.5 13.2 %collective-permute-start.6 = (bf16[144,1536]{1,0:T(8,128)(2,1)S(1)}, bf16[144,1536]{1,0:T(8,128)(2,1)S(1)}, u32[]{:S(2)}, u32[]{:S(2)}) collective-permute-start(bf16[144,1536]{1,0:T(8,128)(2,1)S(1)} %get-tuple-element.77), channel_id=1, source_target_pairs={{0,1},{1,0},{2,3},{3,2},{4,5},{5,4},{6,7},{7,6},{8,9},{9,8},{10,11... | collective-permute-start | bytes 1327112 | tf_op jit(solution)/shard_map/ppermute | solution.py:646
  30.2 20.2 %collective-permute-start.7 = (bf16[144,1536]{1,0:T(8,128)(2,1)S(1)}, bf16[144,1536]{1,0:T(8,128)(2,1)S(1)}, u32[]{:S(2)}, u32[]{:S(2)}) collective-permute-start(bf16[144,1536]{1,0:T(8,128)(2,1)S(1)} %get-tuple-element.78), channel_id=1, source_target_pairs={{0,2},{1,3},{2,0},{3,1},{4,6},{5,7},{6,4},{7,5},{8,10},{9,11},{10,... | collective-permute-start | bytes 1327112 | tf_op jit(solution)/shard_map/ppermute | solution.py:646
  31.7 18.7 %collective-permute-start.8 = (bf16[144,1536]{1,0:T(8,128)(2,1)S(1)}, bf16[144,1536]{1,0:T(8,128)(2,1)S(1)}, u32[]{:S(2)}, u32[]{:S(2)}) collective-permute-start(bf16[144,1536]{1,0:T(8,128)(2,1)S(1)} %get-tuple-element.79), channel_id=1, source_target_pairs={{0,3},{1,2},{2,1},{3,0},{4,7},{5,6},{6,5},{7,4},{8,11},{9,10},{10,... | collective-permute-start | bytes 1327112 | tf_op jit(solution)/shard_map/ppermute | solution.py:646
  32.0 20.8 %collective-permute-start.5 = (bf16[144,1536]{1,0:T(8,128)(2,1)S(1)}, bf16[144,1536]{1,0:T(8,128)(2,1)S(1)}, u32[]{:S(2)}, u32[]{:S(2)}) collective-permute-start(bf16[144,1536]{1,0:T(8,128)(2,1)S(1)} %passed.3.refs_0_.refs_1_), channel_id=1, source_target_pairs={{0,4},{4,0},{8,12},{12,8},{1,5},{5,1},{9,13},{13,9},{2,6},{6,2},{1... | collective-permute-start | bytes 1327112 | tf_op jit(solution)/shard_map/ppermute | solution.py:646
  32.1 51.4 %collective-permute-start.10 = (bf16[4,72,1536]{2,1,0:T(8,128)(2,1)S(1)}, bf16[4,72,1536]{2,1,0:T(8,128)(2,1)S(1)}, u32[]{:S(2)}, u32[]{:S(2)}) collective-permute-start(bf16[4,72,1536]{2,1,0:T(8,128)(2,1)S(1)} %passed.4.refs_0_), channel_id=1, source_target_pairs={{0,8},{4,12},{8,0},{12,4},{1,9},{5,13},{9,1},{13,5},{2,10},{6,14},... | collective-permute-start | bytes 2654216 | tf_op jit(solution)/shard_map/ppermute | solution.py:646
  41.7 41.8 %collective-permute-start.9 = (bf16[4,72,1536]{2,1,0:T(8,128)(2,1)S(1)}, bf16[4,72,1536]{2,1,0:T(8,128)(2,1)S(1)}, u32[]{:S(2)}, u32[]{:S(2)}) collective-permute-start(bf16[4,72,1536]{2,1,0:T(8,128)(2,1)S(1)} %passed.4.refs_0_), channel_id=1, source_target_pairs={{0,4},{4,0},{8,12},{12,8},{1,5},{5,1},{9,13},{13,9},{2,6},{6,2},{1... | collective-permute-start | bytes 2654216 | tf_op jit(solution)/shard_map/ppermute | solution.py:646
  53.7 13.2 %collective-permute-start.11 = (bf16[144,1536]{1,0:T(8,128)(2,1)S(1)}, bf16[144,1536]{1,0:T(8,128)(2,1)S(1)}, u32[]{:S(2)}, u32[]{:S(2)}) collective-permute-start(bf16[144,1536]{1,0:T(8,128)(2,1)S(1)} %get-tuple-element.85), channel_id=1, source_target_pairs={{0,1},{1,0},{2,3},{3,2},{4,5},{5,4},{6,7},{7,6},{8,9},{9,8},{10,11... | collective-permute-start | bytes 1327112 | tf_op jit(solution)/shard_map/ppermute | solution.py:646
  55.3 19.0 %collective-permute-start.12 = (bf16[144,1536]{1,0:T(8,128)(2,1)S(1)}, bf16[144,1536]{1,0:T(8,128)(2,1)S(1)}, u32[]{:S(2)}, u32[]{:S(2)}) collective-permute-start(bf16[144,1536]{1,0:T(8,128)(2,1)S(1)} %get-tuple-element.86), channel_id=1, source_target_pairs={{0,2},{1,3},{2,0},{3,1},{4,6},{5,7},{6,4},{7,5},{8,10},{9,11},{10,... | collective-permute-start | bytes 1327112 | tf_op jit(solution)/shard_map/ppermute | solution.py:646
  56.8 17.4 %collective-permute-start.13 = (bf16[144,1536]{1,0:T(8,128)(2,1)S(1)}, bf16[144,1536]{1,0:T(8,128)(2,1)S(1)}, u32[]{:S(2)}, u32[]{:S(2)}) collective-permute-start(bf16[144,1536]{1,0:T(8,128)(2,1)S(1)} %get-tuple-element.87), channel_id=1, source_target_pairs={{0,3},{1,2},{2,1},{3,0},{4,7},{5,6},{6,5},{7,4},{8,11},{9,10},{10,... | collective-permute-start | bytes 1327112 | tf_op jit(solution)/shard_map/ppermute | solution.py:646
  79.9 13.2 %collective-permute-start.18 = (bf16[144,1536]{1,0:T(8,128)(2,1)S(1)}, bf16[144,1536]{1,0:T(8,128)(2,1)S(1)}, u32[]{:S(2)}, u32[]{:S(2)}) collective-permute-start(bf16[144,1536]{1,0:T(8,128)(2,1)S(1)} %get-tuple-element.104), channel_id=1, source_target_pairs={{0,1},{1,0},{2,3},{3,2},{4,5},{5,4},{6,7},{7,6},{8,9},{9,8},{10,11... | collective-permute-start | bytes 1327112 | tf_op jit(solution)/shard_map/ppermute | solution.py:646
  81.2 18.0 %collective-permute-start.19 = (bf16[144,1536]{1,0:T(8,128)(2,1)S(1)}, bf16[144,1536]{1,0:T(8,128)(2,1)S(1)}, u32[]{:S(2)}, u32[]{:S(2)}) collective-permute-start(bf16[144,1536]{1,0:T(8,128)(2,1)S(1)} %get-tuple-element.105), channel_id=1, source_target_pairs={{0,2},{1,3},{2,0},{3,1},{4,6},{5,7},{6,4},{7,5},{8,10},{9,11},{10,... | collective-permute-start | bytes 1327112 | tf_op jit(solution)/shard_map/ppermute | solution.py:646
  82.1 17.2 %collective-permute-start.20 = (bf16[144,1536]{1,0:T(8,128)(2,1)S(1)}, bf16[144,1536]{1,0:T(8,128)(2,1)S(1)}, u32[]{:S(2)}, u32[]{:S(2)}) collective-permute-start(bf16[144,1536]{1,0:T(8,128)(2,1)S(1)} %get-tuple-element.106), channel_id=1, source_target_pairs={{0,3},{1,2},{2,1},{3,0},{4,7},{5,6},{6,5},{7,4},{8,11},{9,10},{10,... | collective-permute-start | bytes 1327112 | tf_op jit(solution)/shard_map/ppermute | solution.py:646
  83.5 26.7 %collective-permute-start.17 = (bf16[4,72,1536]{2,1,0:T(8,128)(2,1)S(1)}, bf16[4,72,1536]{2,1,0:T(8,128)(2,1)S(1)}, u32[]{:S(2)}, u32[]{:S(2)}) collective-permute-start(bf16[4,72,1536]{2,1,0:T(8,128)(2,1)S(1)} %passed.5.refs_2_), channel_id=1, source_target_pairs={{0,4},{4,0},{8,12},{12,8},{1,5},{5,1},{9,13},{13,9},{2,6},{6,2},{1... | collective-permute-start | bytes 2654216 | tf_op jit(solution)/shard_map/ppermute | solution.py:646
  101.4 15.2 %collective-permute-start.14 = (bf16[112,1536]{1,0:T(8,128)(2,1)S(1)}, bf16[112,1536]{1,0:T(8,128)(2,1)S(1)}, u32[]{:S(2)}, u32[]{:S(2)}) collective-permute-start(bf16[112,1536]{1,0:T(8,128)(2,1)S(1)} %get-tuple-element.100), channel_id=1, source_target_pairs={{0,1},{1,0},{2,3},{3,2},{4,5},{5,4},{6,7},{7,6},{8,9},{9,8},{10,11... | collective-permute-start | bytes 1032200 | tf_op jit(solution)/shard_map/ppermute | solution.py:646
  102.1 16.5 %collective-permute-start.15 = (bf16[112,1536]{1,0:T(8,128)(2,1)S(1)}, bf16[112,1536]{1,0:T(8,128)(2,1)S(1)}, u32[]{:S(2)}, u32[]{:S(2)}) collective-permute-start(bf16[112,1536]{1,0:T(8,128)(2,1)S(1)} %get-tuple-element.101), channel_id=1, source_target_pairs={{0,2},{1,3},{2,0},{3,1},{4,6},{5,7},{6,4},{7,5},{8,10},{9,11},{10,... | collective-permute-start | bytes 1032200 | tf_op jit(solution)/shard_map/ppermute | solution.py:646
  103.6 15.5 %collective-permute-start.16 = (bf16[112,1536]{1,0:T(8,128)(2,1)S(1)}, bf16[112,1536]{1,0:T(8,128)(2,1)S(1)}, u32[]{:S(2)}, u32[]{:S(2)}) collective-permute-start(bf16[112,1536]{1,0:T(8,128)(2,1)S(1)} %get-tuple-element.102), channel_id=1, source_target_pairs={{0,3},{1,2},{2,1},{3,0},{4,7},{5,6},{6,5},{7,4},{8,11},{9,10},{10,... | collective-permute-start | bytes 1032200 | tf_op jit(solution)/shard_map/ppermute | solution.py:646
  110.0 26.5 %collective-permute-start.28 = (bf16[64,1536]{1,0:T(8,128)(2,1)S(1)}, bf16[64,1536]{1,0:T(8,128)(2,1)S(1)}, u32[]{:S(2)}, u32[]{:S(2)}) collective-permute-start(bf16[64,1536]{1,0:T(8,128)(2,1)S(1)} %pair_sum.1), channel_id=1, source_target_pairs={{0,8},{4,12},{8,0},{12,4},{1,9},{5,13},{9,1},{13,5},{2,10},{6,14},... | collective-permute-start | bytes 589832 | tf_op jit(solution)/shard_map/ppermute | solution.py:646
  121.0 20.5 %collective-permute-start.21 = (bf16[64,1536]{1,0:T(8,128)(2,1)S(1)}, bf16[64,1536]{1,0:T(8,128)(2,1)S(1)}, u32[]{:S(2)}, u32[]{:S(2)}) collective-permute-start(bf16[64,1536]{1,0:T(8,128)(2,1)S(1)} %get-tuple-element.117), channel_id=1, source_target_pairs={{0,4},{4,0},{8,12},{12,8},{1,5},{5,1},{9,13},{13,9},{2,6},{6,2},{1... | collective-permute-start | bytes 589832 | tf_op jit(solution)/shard_map/ppermute | solution.py:646
  123.5 18.0 %collective-permute-start.22 = (bf16[64,1536]{1,0:T(8,128)(2,1)S(1)}, bf16[64,1536]{1,0:T(8,128)(2,1)S(1)}, u32[]{:S(2)}, u32[]{:S(2)}) collective-permute-start(bf16[64,1536]{1,0:T(8,128)(2,1)S(1)} %get-tuple-element.118), channel_id=1, source_target_pairs={{0,8},{4,12},{8,0},{12,4},{1,9},{5,13},{9,1},{13,5},{2,10},{6,14},... | collective-permute-start | bytes 589832 | tf_op jit(solution)/shard_map/ppermute | solution.py:646
  125.7 15.8 %collective-permute-start.26 = (bf16[64,1536]{1,0:T(8,128)(2,1)S(1)}, bf16[64,1536]{1,0:T(8,128)(2,1)S(1)}, u32[]{:S(2)}, u32[]{:S(2)}) collective-permute-start(bf16[64,1536]{1,0:T(8,128)(2,1)S(1)} %frame_sums.5), channel_id=1, source_target_pairs={{0,12},{4,8},{8,4},{12,0},{1,13},{5,9},{9,5},{13,1},{2,14},{6,10},... | collective-permute-start | bytes 589832 | tf_op jit(solution)/shard_map/ppermute | solution.py:646
  149.8 17.8 %collective-permute-start.29 = (bf16[2,64,1536]{2,1,0:T(8,128)(2,1)S(1)}, bf16[2,64,1536]{2,1,0:T(8,128)(2,1)S(1)}, u32[]{:S(2)}, u32[]{:S(2)}) collective-permute-start(bf16[2,64,1536]{2,1,0:T(8,128)(2,1)S(1)} %get-tuple-element.131), channel_id=1, source_target_pairs={{0,16},{16,0},{1,17},{17,1},{2,18},{18,2},{3,19},{19,3},{4,20},{20... | collective-permute-start | bytes 1179656 | tf_op jit(solution)/shard_map/ppermute | solution.py:741
  154.4 12.4 %collective-permute-start.33 = (bf16[32,1536]{1,0:T(8,128)(2,1)S(1)}, bf16[32,1536]{1,0:T(8,128)(2,1)S(1)}, u32[]{:S(2)}, u32[]{:S(2)}) collective-permute-start(bf16[32,1536]{1,0:T(8,128)(2,1)S(1)} %add_convert_fusion.refs_0_), channel_id=1, source_target_pairs={{0,4},{4,0},{8,12},{12,8},{1,5},{5,1},{9,13},{13,9},{2,6},{6,2},{1... | collective-permute-start | bytes 294920 | tf_op jit(solution)/shard_map/ppermute | solution.py:646
  (23 other events, 258.4 us)

commit v5 on v4

--- a/solution.py
+++ b/solution.py
@@ -696,7 +696,7 @@
     pieces = passed(pieces, later)
     later = passed(to_partner(pieces, "dp", 2), back[0])
     second = [pieces, to_partner(pieces, "dp", 1), later, to_partner(later, "dp", 1)]
-    wide, wide_map, _ = slots(first[2:], experts, capacity, frames, wide_places, earlier=tuple(near[1:]))
+    wide, wide_map, _ = slots(first[2:], experts, capacity, frames, wide_places)
     maps = (near_map, wide_map)
     wide = exchanged(wide, "expert")
     back, kept = products(wide, rows=half, first_row=at, before=back, kept=kept, stage=5)
@@ -735,7 +735,7 @@
     down_grad = lax.dot_general(all_acted, all_grad, over_rows, preferred_element_type=f32).astype(bf16)
     _, sent = frame_sums(1, maps, last_back, frames, ((1, 1, 0),), (((0,), bf16),), [])
     second_norm.append(to_partner(sent[0], "dp", seqs - 1))
-    prev, sums = epilogue(0, first_norm, xs, ups, saved, taps, norm_gain, earlier=(up_grad,))
+    prev, sums = epilogue(0, first_norm, xs, ups, saved, taps, norm_gain)
     prev, sums = epilogue(1, second_norm, xs, ups, saved, taps, norm_gain, before=(sums, prev))
     peers = lax.axis_size("pipe")
     handed = lax.ppermute(prev, "pipe", [(i, (i - 1) % peers) for i in range(peers)])

time: 169 us -> 165 us (0.976)
  waiting for transfers between devices: 50.3 us -> 40.4 us
  starting transfers between devices: 43.4 us -> 48.7 us
  local copies, waits for them, and re-layouts: 4.07 us -> 6.41 us
    ppermute x35, waiting for transfers between devices: 50.3 us -> 40.4 us  [to_partner(): lax.ppermute(array, axis, [(i, i ^ k) for i in range(lax.axis_size(axis))])]
    ppermute x35, starting transfers between devices: 43.4 us -> 48.7 us  [to_partner(): lax.ppermute(array, axis, [(i, i ^ k) for i in range(lax.axis_size(axis))])]
    unnamed x23 -> x29, local copies, waits for them, and re-layouts: 4.07 us -> 6.41 us
  transfers between devices with their start and end apart: 36 -> 36, of which waited for: 14 -> 12; matrix products, arithmetic and copies ran while one was open for 10% -> 10% of each run, Pallas kernels for 26% -> 27%
where the time goes in v5:
time: 165 us
  Pallas kernels  52.3 us (32%)
  starting transfers between devices  48.7 us (30%)
  waiting for transfers between devices  40.4 us (24%)
  matrix products  16 us (10%)
  local copies, waits for them, and re-layouts  6.41 us (4%)
    ppermute x35, starting transfers between devices, to_partner(): lax.ppermute(array, axis, [(i, i ^ k) for i in range(lax.axis_size(axis))])  48.7 us
    ppermute x35, waiting for transfers between devices, to_partner(): lax.ppermute(array, axis, [(i, i ^ k) for i in range(lax.axis_size(axis))])  40.4 us
    pallas_call x4, Pallas kernels, expert_products(): pl.pallas_call(functools.partial(expert_body, parts, rows, capacity if bl...  25.5 us
    pallas_call x2, Pallas kernels, epilogue(): pl.pallas_call(functools.partial(epilogue_body, m, seqs, last, len(earlie...  9.62 us
    dot_general x1, matrix products, local(): lax.dot_general(all_acted, all_grad, over_rows, preferred_element_type=f32)  8 us
    dot_general x1, matrix products, local(): lax.dot_general(all_in, all_pre, over_rows, preferred_element_type=f32)  7.97 us
    unnamed x29, local copies, waits for them, and re-layouts  6.41 us
    pallas_call x3, Pallas kernels, frame_sums(): pl.pallas_call(functools.partial(frame_sums_body, m, len(blocks), frames,...  5.27 us
  transfers between devices with their start and end apart: 36, of which 12 were waited for; matrix products, arithmetic and copies ran while one was open for 10% of the time, Pallas kernels for 27%

profile of v5, /device:TPU:0, one launch (start us, length us, event | category | flops | bytes accessed | tf_op | source)
XLA Modules:
  0.0 164.7 jit_solution(3910412505732754120)
XLA Ops:
  0.6 3.2 %first_send.1._.refs_0_ = bf16[144,1536]{1,0:T(8,128)(2,1)} custom-call(bf16[2,64,1536]{2,1,0:T(8,128)(2,1)} %bitcast.31, bf16[2,64,1536]{2,1,0:T(8,128)(2,1)} %bitcast.36, s32[2,2,64]{2,1,0:T(2,128)} %bitcast.46, f32[2,2,64]{2,1,0:T(2,128)} %bitcast.48, f32[31,1,1536]{2,1,0:T(1,128)} %bitcast.40, f32[1,1536]{1,0:T(1,128)} %refs_10_.1), custom_call_target="tpu_custom_call" | custom-call | flops 1 | bytes 1 | tf_op jit(solution)/shard_map/first_send/pallas_call | solution.py:151
  3.9 3.1 %collective-permute-start = (bf16[144,1536]{1,0:T(8,128)(2,1)}, bf16[144,1536]{1,0:T(8,128)(2,1)S(1)}, u32[]{:S(2)}, u32[]{:S(2)}) collective-permute-start(bf16[144,1536]{1,0:T(8,128)(2,1)} %first_send.1._.refs_0_), channel_id=1, source_target_pairs={{0,4},{4,0},{8,12},{12,8},{1,5},{5,1},{9,13},{13,9},{2,6},{6,2},{1... | collective-permute-start | bytes 1327112 | tf_op jit(solution)/shard_map/ppermute | solution.py:646
  7.0 2.6 %collective-permute-start.4 = (bf16[144,1536]{1,0:T(8,128)(2,1)}, bf16[144,1536]{1,0:T(8,128)(2,1)S(1)}, u32[]{:S(2)}, u32[]{:S(2)}) collective-permute-start(bf16[144,1536]{1,0:T(8,128)(2,1)} %first_send.1._.refs_0_), channel_id=1, source_target_pairs={{0,8},{4,12},{8,0},{12,4},{1,9},{5,13},{9,1},{13,5},{2,10},{6,14},... | collective-permute-start | bytes 1327112 | tf_op jit(solution)/shard_map/ppermute | solution.py:646
  9.6 3.8 %second_send.1 = (bf16[72,1536]{1,0:T(8,128)(2,1)}, bf16[72,1536]{1,0:T(8,128)(2,1)}, bf16[72,1536]{1,0:T(8,128)(2,1)}, bf16[72,1536]{1,0:T(8,128)(2,1)}) custom-call(bf16[2,64,1536]{2,1,0:T(8,128)(2,1)} %bitcast.32, bf16[2,64,1536]{2,1,0:T(8,128)(2,1)} %bitcast.37, s32[2,2,64]{2,1,0:T(2,128)} %bitcast.47, f32[2,2,64]{2,1,0:T(2,128)} %bitcast.49, ...), custom_call_target="tpu_custom_call" | custom-call | flops 13800000512 | bytes 1 | tf_op jit(solution)/shard_map/second_send/pallas_call | solution.py:196
  17.0 5.1 %collective-permute-done.1.refs_3_ = bf16[72,1536]{1,0:T(8,128)(2,1)S(1)} collective-permute-done((bf16[72,1536]{1,0:T(8,128)(2,1)}, bf16[72,1536]{1,0:T(8,128)(2,1)S(1)}, u32[]{:S(2)}, u32[]{:S(2)}) %collective-permute-start.1) | collective-permute-done | bytes 221216 | tf_op jit(solution)/shard_map/ppermute | solution.py:646
  22.1 4.2 %collective-permute-done.2.refs_4_ = bf16[72,1536]{1,0:T(8,128)(2,1)S(1)} collective-permute-done((bf16[72,1536]{1,0:T(8,128)(2,1)}, bf16[72,1536]{1,0:T(8,128)(2,1)S(1)}, u32[]{:S(2)}, u32[]{:S(2)}) %collective-permute-start.2) | collective-permute-done | bytes 221216 | tf_op jit(solution)/shard_map/ppermute | solution.py:646
  29.7 2.4 %collective-permute-start.10 = (bf16[144,1536]{1,0:T(8,128)(2,1)S(1)}, bf16[144,1536]{1,0:T(8,128)(2,1)S(1)}, u32[]{:S(2)}, u32[]{:S(2)}) collective-permute-start(bf16[144,1536]{1,0:T(8,128)(2,1)S(1)} %get-tuple-element.81), channel_id=1, source_target_pairs={{0,3},{1,2},{2,1},{3,0},{4,7},{5,6},{6,5},{7,4},{8,11},{9,10},{10,... | collective-permute-start | bytes 1327112 | tf_op jit(solution)/shard_map/ppermute | solution.py:646
  33.2 2.6 %collective-permute-start.7 = (bf16[4,72,1536]{2,1,0:T(8,128)(2,1)S(1)}, bf16[4,72,1536]{2,1,0:T(8,128)(2,1)S(1)}, u32[]{:S(2)}, u32[]{:S(2)}) collective-permute-start(bf16[4,72,1536]{2,1,0:T(8,128)(2,1)S(1)} %passed.4.refs_0_), channel_id=1, source_target_pairs={{0,8},{4,12},{8,0},{12,4},{1,9},{5,13},{9,1},{13,5},{2,10},{6,14},... | collective-permute-start | bytes 2654216 | tf_op jit(solution)/shard_map/ppermute | solution.py:646
  38.2 7.8 %collective-permute-done.5.refs_1_ = bf16[144,1536]{1,0:T(8,128)(2,1)S(1)} collective-permute-done((bf16[144,1536]{1,0:T(8,128)(2,1)S(1)}, bf16[144,1536]{1,0:T(8,128)(2,1)S(1)}, u32[]{:S(2)}, u32[]{:S(2)}) %collective-permute-start.5) | collective-permute-done | bytes 442400 | tf_op jit(solution)/shard_map/ppermute | solution.py:646
  48.3 4.9 %collective-permute-done.8.refs_1_ = bf16[144,1536]{1,0:T(8,128)(2,1)S(1)} collective-permute-done((bf16[144,1536]{1,0:T(8,128)(2,1)S(1)}, bf16[144,1536]{1,0:T(8,128)(2,1)S(1)}, u32[]{:S(2)}, u32[]{:S(2)}) %collective-permute-start.8) | collective-permute-done | bytes 442400 | tf_op jit(solution)/shard_map/ppermute | solution.py:646
  60.9 5.6 %expert_products.4 = (bf16[72,1536]{1,0:T(8,128)(2,1)S(1)}, bf16[72,1536]{1,0:T(8,128)(2,1)S(1)}, bf16[72,1536]{1,0:T(8,128)(2,1)S(1)}, bf16[72,1536]{1,0:T(8,12...) custom-call(bf16[144,1536]{1,0:T(8,128)(2,1)S(1)} %get-tuple-element, ...), custom_call_target="tpu_custom_call" | custom-call | flops 13800000512 | bytes 1 | tf_op jit(solution)/shard_map/expert_products/pallas_call | solution.py:415
  66.5 4.5 %collective-permute-done.12.refs_2_ = bf16[144,1536]{1,0:T(8,128)(2,1)S(1)} collective-permute-done((bf16[144,1536]{1,0:T(8,128)(2,1)S(1)}, bf16[144,1536]{1,0:T(8,128)(2,1)S(1)}, u32[]{:S(2)}, u32[]{:S(2)}) %collective-permute-start.12) | collective-permute-done | bytes 442400 | tf_op jit(solution)/shard_map/ppermute | solution.py:646
  71.0 5.7 %expert_products.5 = (bf16[144,1536]{1,0:T(8,128)(2,1)S(1)}, bf16[144,1536]{1,0:T(8,128)(2,1)S(1)}, bf16[144,1536]{1,0:T(8,128)(2,1)S(1)}, bf16[144,1536]{1,0:T(...) custom-call(bf16[144,1536]{1,0:T(8,128)(2,1)S(1)} %get-tuple-element, ...), custom_call_target="tpu_custom_call", output_to_operand_aliasing={{4}: (10, {}), {5}: (11, {}), {6}: (12, {}), {7}: (13, {})} | custom-call | flops 1 | bytes 1 | tf_op jit(solution)/shard_map/expert_products/pallas_call | solution.py:415
  81.9 8.8 %expert_products.6 = (bf16[112,1536]{1,0:T(8,128)(2,1)S(1)}, bf16[112,1536]{1,0:T(8,128)(2,1)S(1)}, bf16[112,1536]{1,0:T(8,128)(2,1)S(1)}, bf16[112,1536]{1,0:T(...) custom-call(bf16[4,72,1536]{2,1,0:T(8,128)(2,1)S(1)} %passed.4.refs_, ...), custom_call_target="tpu_custom_call", output_to_operand_aliasing={{4}: (5, {}), {5}: (6, {}), {6}: (7, {}), {7}: (8, {})} | custom-call | flops 11500000256 | bytes 1 | tf_op jit(solution)/shard_map/expert_products/pallas_call | solution.py:415
  90.7 5.4 %collective-permute-done.19.refs_4_ = bf16[144,1536]{1,0:T(8,128)(2,1)S(1)} collective-permute-done((bf16[144,1536]{1,0:T(8,128)(2,1)S(1)}, bf16[144,1536]{1,0:T(8,128)(2,1)S(1)}, u32[]{:S(2)}, u32[]{:S(2)}) %collective-permute-start.19) | collective-permute-done | bytes 442400 | tf_op jit(solution)/shard_map/ppermute | solution.py:646
  103.1 4.7 %collective-permute-done.27.got_ref.refs_1_ = bf16[128,1536]{1,0:T(8,128)(2,1)S(1)} collective-permute-done((bf16[128,1536]{1,0:T(8,128)(2,1)S(1)}, bf16[128,1536]{1,0:T(8,128)(2,1)S(1)}, u32[]{:S(2)}, u32[]{:S(2)}) %collective-permute-start.27) | collective-permute-done | bytes 393248 | tf_op jit(solution)/shard_map/ppermute | solution.py:646
  107.8 2.9 %collective-permute-start.28 = (bf16[64,1536]{1,0:T(8,128)(2,1)S(1)}, bf16[64,1536]{1,0:T(8,128)(2,1)S(1)}, u32[]{:S(2)}, u32[]{:S(2)}) collective-permute-start(bf16[64,1536]{1,0:T(8,128)(2,1)S(1)} %pair_sum.1), channel_id=1, source_target_pairs={{0,8},{4,12},{8,0},{12,4},{1,9},{5,13},{9,1},{13,5},{2,10},{6,14},... | collective-permute-start | bytes 589832 | tf_op jit(solution)/shard_map/ppermute | solution.py:646
  110.7 5.3 %expert_products.7 = (bf16[40,1536]{1,0:T(8,128)(2,1)S(1)}, bf16[40,1536]{1,0:T(8,128)(2,1)S(1)}, bf16[40,1536]{1,0:T(8,128)(2,1)S(1)}, bf16[40,1536]{1,0:T(8,12...) custom-call(bf16[4,72,1536]{2,1,0:T(8,128)(2,1)S(1)} %collective-per, ...), custom_call_target="tpu_custom_call", output_to_operand_aliasing={{4}: (4, {}), {5}: (5, {}), {6}: (6, {}), {7}: (7, {})} | custom-call | flops 1 | bytes 1 | tf_op jit(solution)/shard_map/expert_products/pallas_call | solution.py:415
  124.4 2.9 %collective-permute-start.26 = (bf16[64,1536]{1,0:T(8,128)(2,1)S(1)}, bf16[64,1536]{1,0:T(8,128)(2,1)S(1)}, u32[]{:S(2)}, u32[]{:S(2)}) collective-permute-start(bf16[64,1536]{1,0:T(8,128)(2,1)S(1)} %frame_sums.5), channel_id=1, source_target_pairs={{0,12},{4,8},{8,4},{12,0},{1,13},{5,9},{9,5},{13,1},{2,14},{6,10},... | collective-permute-start | bytes 589832 | tf_op jit(solution)/shard_map/ppermute | solution.py:646
  127.3 4.8 %norm_conv_back.2 = (bf16[64,1536]{1,0:T(8,128)(2,1)S(1)}, f32[32,1536]{1,0:T(8,128)S(1)}) custom-call(f32[64,1536]{1,0:T(8,128)S(1)} %get-tuple-element.107.refs_3_.refs_0_, bf16[128,1536]{1,0:T(8,128)(2,1)S(1)} %collective-permute-done.27.got_ref.refs_1_, bf16[64,1536]{1,0:T(8,128)(2,1)S(1)} %collective-permute-done.28.refs_2_, ...), custom_call_target="tpu_custom_call" | custom-call | flops 1 | bytes 1 | tf_op jit(solution)/shard_map/norm_conv_back/pallas_call | solution.py:588
  133.2 4.8 %norm_conv_back.3 = (bf16[2,64,1536]{2,1,0:T(8,128)(2,1)S(1)}, bf16[32,1536]{1,0:T(8,128)(2,1)S(1)}) custom-call(f32[64,1536]{1,0:T(8,128)S(1)} %get-tuple-element.116.refs_0_, bf16[64,1536]{1,0:T(8,128)(2,1)S(1)} %collective-permute-done.21.refs_1_, bf16[64,1536]{1,0:T(8,128)(2,1)S(1)} %collective-permute-done.22.refs_2_, ...), custom_call_target="tpu_custom_call" | custom-call | flops 1 | bytes 1 | tf_op jit(solution)/shard_map/norm_conv_back/pallas_call | solution.py:588
  141.6 8.0 %fusion.1 = bf16[1,1,1536,1536]{3,2,1,0:T(8,128)(2,1)} fusion(bf16[1184,1536]{1,0:T(8,128)(2,1)S(1)} %copy-done.12, bf16[1184,1536]{1,0:T(8,128)(2,1)S(1)} %copy-done.11), kind=kOutput, calls=%fused_computation.3 | convolution fusion | flops 5589172224 | bytes 11993088 | tf_op jit(solution)/shard_map/dot_general | solution.py:735
  149.7 2.7 %collective-permute-start.33 = (bf16[32,1536]{1,0:T(8,128)(2,1)S(1)}, bf16[32,1536]{1,0:T(8,128)(2,1)S(1)}, u32[]{:S(2)}, u32[]{:S(2)}) collective-permute-start(bf16[32,1536]{1,0:T(8,128)(2,1)S(1)} %add_convert_fusion.refs_0_), channel_id=1, source_target_pairs={{0,4},{4,0},{8,12},{12,8},{1,5},{5,1},{9,13},{13,9},{2,6},{6,2},{1... | collective-permute-start | bytes 294920 | tf_op jit(solution)/shard_map/ppermute | solution.py:646
  154.9 8.0 %fusion = bf16[1,1,1536,1536]{3,2,1,0:T(8,128)(2,1)} fusion(bf16[1184,1536]{1,0:T(8,128)(2,1)S(1)} %copy-done.10, bf16[1184,1536]{1,0:T(8,128)(2,1)S(1)} %copy-done.13), kind=kOutput, calls=%fused_computation.2 | convolution fusion | flops 5589172224 | bytes 11993088 | tf_op jit(solution)/shard_map/dot_general | solution.py:734
  (99 shorter events, 49.8 us)
Async XLA Ops:
  3.9 22.8 %collective-permute-start = (bf16[144,1536]{1,0:T(8,128)(2,1)}, bf16[144,1536]{1,0:T(8,128)(2,1)S(1)}, u32[]{:S(2)}, u32[]{:S(2)}) collective-permute-start(bf16[144,1536]{1,0:T(8,128)(2,1)} %first_send.1._.refs_0_), channel_id=1, source_target_pairs={{0,4},{4,0},{8,12},{12,8},{1,5},{5,1},{9,13},{13,9},{2,6},{6,2},{1... | collective-permute-start | bytes 1327112 | tf_op jit(solution)/shard_map/ppermute | solution.py:646
  7.0 22.3 %collective-permute-start.4 = (bf16[144,1536]{1,0:T(8,128)(2,1)}, bf16[144,1536]{1,0:T(8,128)(2,1)S(1)}, u32[]{:S(2)}, u32[]{:S(2)}) collective-permute-start(bf16[144,1536]{1,0:T(8,128)(2,1)} %first_send.1._.refs_0_), channel_id=1, source_target_pairs={{0,8},{4,12},{8,0},{12,4},{1,9},{5,13},{9,1},{13,5},{2,10},{6,14},... | collective-permute-start | bytes 1327112 | tf_op jit(solution)/shard_map/ppermute | solution.py:646
  15.0 11.3 %collective-permute-start.2 = (bf16[72,1536]{1,0:T(8,128)(2,1)}, bf16[72,1536]{1,0:T(8,128)(2,1)S(1)}, u32[]{:S(2)}, u32[]{:S(2)}) collective-permute-start(bf16[72,1536]{1,0:T(8,128)(2,1)} %get-tuple-element.73), channel_id=1, source_target_pairs={{0,2},{1,3},{2,0},{3,1},{4,6},{5,7},{6,4},{7,5},{8,10},{9,11},{10,... | collective-permute-start | bytes 663560 | tf_op jit(solution)/shard_map/ppermute | solution.py:646
  29.2 16.8 %collective-permute-start.5 = (bf16[144,1536]{1,0:T(8,128)(2,1)S(1)}, bf16[144,1536]{1,0:T(8,128)(2,1)S(1)}, u32[]{:S(2)}, u32[]{:S(2)}) collective-permute-start(bf16[144,1536]{1,0:T(8,128)(2,1)S(1)} %passed.3.refs_0_.refs_1_), channel_id=1, source_target_pairs={{0,4},{4,0},{8,12},{12,8},{1,5},{5,1},{9,13},{13,9},{2,6},{6,2},{1... | collective-permute-start | bytes 1327112 | tf_op jit(solution)/shard_map/ppermute | solution.py:646
  29.7 17.2 %collective-permute-start.10 = (bf16[144,1536]{1,0:T(8,128)(2,1)S(1)}, bf16[144,1536]{1,0:T(8,128)(2,1)S(1)}, u32[]{:S(2)}, u32[]{:S(2)}) collective-permute-start(bf16[144,1536]{1,0:T(8,128)(2,1)S(1)} %get-tuple-element.81), channel_id=1, source_target_pairs={{0,3},{1,2},{2,1},{3,0},{4,7},{5,6},{6,5},{7,4},{8,11},{9,10},{10,... | collective-permute-start | bytes 1327112 | tf_op jit(solution)/shard_map/ppermute | solution.py:646
  32.1 21.1 %collective-permute-start.8 = (bf16[144,1536]{1,0:T(8,128)(2,1)S(1)}, bf16[144,1536]{1,0:T(8,128)(2,1)S(1)}, u32[]{:S(2)}, u32[]{:S(2)}) collective-permute-start(bf16[144,1536]{1,0:T(8,128)(2,1)S(1)} %get-tuple-element.79), channel_id=1, source_target_pairs={{0,1},{1,0},{2,3},{3,2},{4,5},{5,4},{6,7},{7,6},{8,9},{9,8},{10,11... | collective-permute-start | bytes 1327112 | tf_op jit(solution)/shard_map/ppermute | solution.py:646
  32.7 21.1 %collective-permute-start.9 = (bf16[144,1536]{1,0:T(8,128)(2,1)S(1)}, bf16[144,1536]{1,0:T(8,128)(2,1)S(1)}, u32[]{:S(2)}, u32[]{:S(2)}) collective-permute-start(bf16[144,1536]{1,0:T(8,128)(2,1)S(1)} %get-tuple-element.80), channel_id=1, source_target_pairs={{0,2},{1,3},{2,0},{3,1},{4,6},{5,7},{6,4},{7,5},{8,10},{9,11},{10,... | collective-permute-start | bytes 1327112 | tf_op jit(solution)/shard_map/ppermute | solution.py:646
  33.2 47.1 %collective-permute-start.7 = (bf16[4,72,1536]{2,1,0:T(8,128)(2,1)S(1)}, bf16[4,72,1536]{2,1,0:T(8,128)(2,1)S(1)}, u32[]{:S(2)}, u32[]{:S(2)}) collective-permute-start(bf16[4,72,1536]{2,1,0:T(8,128)(2,1)S(1)} %passed.4.refs_0_), channel_id=1, source_target_pairs={{0,8},{4,12},{8,0},{12,4},{1,9},{5,13},{9,1},{13,5},{2,10},{6,14},... | collective-permute-start | bytes 2654216 | tf_op jit(solution)/shard_map/ppermute | solution.py:646
  46.0 35.8 %collective-permute-start.6 = (bf16[4,72,1536]{2,1,0:T(8,128)(2,1)S(1)}, bf16[4,72,1536]{2,1,0:T(8,128)(2,1)S(1)}, u32[]{:S(2)}, u32[]{:S(2)}) collective-permute-start(bf16[4,72,1536]{2,1,0:T(8,128)(2,1)S(1)} %passed.4.refs_0_), channel_id=1, source_target_pairs={{0,4},{4,0},{8,12},{12,8},{1,5},{5,1},{9,13},{13,9},{2,6},{6,2},{1... | collective-permute-start | bytes 2654216 | tf_op jit(solution)/shard_map/ppermute | solution.py:646
  46.9 19.6 %collective-permute-start.11 = (bf16[144,1536]{1,0:T(8,128)(2,1)S(1)}, bf16[144,1536]{1,0:T(8,128)(2,1)S(1)}, u32[]{:S(2)}, u32[]{:S(2)}) collective-permute-start(bf16[144,1536]{1,0:T(8,128)(2,1)S(1)} %get-tuple-element.85), channel_id=1, source_target_pairs={{0,1},{1,0},{2,3},{3,2},{4,5},{5,4},{6,7},{7,6},{8,9},{9,8},{10,11... | collective-permute-start | bytes 1327112 | tf_op jit(solution)/shard_map/ppermute | solution.py:646
  53.2 17.8 %collective-permute-start.12 = (bf16[144,1536]{1,0:T(8,128)(2,1)S(1)}, bf16[144,1536]{1,0:T(8,128)(2,1)S(1)}, u32[]{:S(2)}, u32[]{:S(2)}) collective-permute-start(bf16[144,1536]{1,0:T(8,128)(2,1)S(1)} %get-tuple-element.86), channel_id=1, source_target_pairs={{0,2},{1,3},{2,0},{3,1},{4,6},{5,7},{6,4},{7,5},{8,10},{9,11},{10,... | collective-permute-start | bytes 1327112 | tf_op jit(solution)/shard_map/ppermute | solution.py:646
  53.8 17.2 %collective-permute-start.13 = (bf16[144,1536]{1,0:T(8,128)(2,1)S(1)}, bf16[144,1536]{1,0:T(8,128)(2,1)S(1)}, u32[]{:S(2)}, u32[]{:S(2)}) collective-permute-start(bf16[144,1536]{1,0:T(8,128)(2,1)S(1)} %get-tuple-element.87), channel_id=1, source_target_pairs={{0,3},{1,2},{2,1},{3,0},{4,7},{5,6},{6,5},{7,4},{8,11},{9,10},{10,... | collective-permute-start | bytes 1327112 | tf_op jit(solution)/shard_map/ppermute | solution.py:646
  76.7 14.0 %collective-permute-start.18 = (bf16[144,1536]{1,0:T(8,128)(2,1)S(1)}, bf16[144,1536]{1,0:T(8,128)(2,1)S(1)}, u32[]{:S(2)}, u32[]{:S(2)}) collective-permute-start(bf16[144,1536]{1,0:T(8,128)(2,1)S(1)} %get-tuple-element.104), channel_id=1, source_target_pairs={{0,1},{1,0},{2,3},{3,2},{4,5},{5,4},{6,7},{7,6},{8,9},{9,8},{10,11... | collective-permute-start | bytes 1327112 | tf_op jit(solution)/shard_map/ppermute | solution.py:646
  78.3 17.8 %collective-permute-start.19 = (bf16[144,1536]{1,0:T(8,128)(2,1)S(1)}, bf16[144,1536]{1,0:T(8,128)(2,1)S(1)}, u32[]{:S(2)}, u32[]{:S(2)}) collective-permute-start(bf16[144,1536]{1,0:T(8,128)(2,1)S(1)} %get-tuple-element.105), channel_id=1, source_target_pairs={{0,2},{1,3},{2,0},{3,1},{4,6},{5,7},{6,4},{7,5},{8,10},{9,11},{10,... | collective-permute-start | bytes 1327112 | tf_op jit(solution)/shard_map/ppermute | solution.py:646
  78.8 17.2 %collective-permute-start.20 = (bf16[144,1536]{1,0:T(8,128)(2,1)S(1)}, bf16[144,1536]{1,0:T(8,128)(2,1)S(1)}, u32[]{:S(2)}, u32[]{:S(2)}) collective-permute-start(bf16[144,1536]{1,0:T(8,128)(2,1)S(1)} %get-tuple-element.106), channel_id=1, source_target_pairs={{0,3},{1,2},{2,1},{3,0},{4,7},{5,6},{6,5},{7,4},{8,11},{9,10},{10,... | collective-permute-start | bytes 1327112 | tf_op jit(solution)/shard_map/ppermute | solution.py:646
  80.3 30.4 %collective-permute-start.17 = (bf16[4,72,1536]{2,1,0:T(8,128)(2,1)S(1)}, bf16[4,72,1536]{2,1,0:T(8,128)(2,1)S(1)}, u32[]{:S(2)}, u32[]{:S(2)}) collective-permute-start(bf16[4,72,1536]{2,1,0:T(8,128)(2,1)S(1)} %passed.5.refs_2_), channel_id=1, source_target_pairs={{0,4},{4,0},{8,12},{12,8},{1,5},{5,1},{9,13},{13,9},{2,6},{6,2},{1... | collective-permute-start | bytes 2654216 | tf_op jit(solution)/shard_map/ppermute | solution.py:646
  99.6 16.7 %collective-permute-start.14 = (bf16[112,1536]{1,0:T(8,128)(2,1)S(1)}, bf16[112,1536]{1,0:T(8,128)(2,1)S(1)}, u32[]{:S(2)}, u32[]{:S(2)}) collective-permute-start(bf16[112,1536]{1,0:T(8,128)(2,1)S(1)} %get-tuple-element.100), channel_id=1, source_target_pairs={{0,1},{1,0},{2,3},{3,2},{4,5},{5,4},{6,7},{7,6},{8,9},{9,8},{10,11... | collective-permute-start | bytes 1032200 | tf_op jit(solution)/shard_map/ppermute | solution.py:646
  100.4 16.9 %collective-permute-start.15 = (bf16[112,1536]{1,0:T(8,128)(2,1)S(1)}, bf16[112,1536]{1,0:T(8,128)(2,1)S(1)}, u32[]{:S(2)}, u32[]{:S(2)}) collective-permute-start(bf16[112,1536]{1,0:T(8,128)(2,1)S(1)} %get-tuple-element.101), channel_id=1, source_target_pairs={{0,2},{1,3},{2,0},{3,1},{4,6},{5,7},{6,4},{7,5},{8,10},{9,11},{10,... | collective-permute-start | bytes 1032200 | tf_op jit(solution)/shard_map/ppermute | solution.py:646
  101.3 18.3 %collective-permute-start.16 = (bf16[112,1536]{1,0:T(8,128)(2,1)S(1)}, bf16[112,1536]{1,0:T(8,128)(2,1)S(1)}, u32[]{:S(2)}, u32[]{:S(2)}) collective-permute-start(bf16[112,1536]{1,0:T(8,128)(2,1)S(1)} %get-tuple-element.102), channel_id=1, source_target_pairs={{0,3},{1,2},{2,1},{3,0},{4,7},{5,6},{6,5},{7,4},{8,11},{9,10},{10,... | collective-permute-start | bytes 1032200 | tf_op jit(solution)/shard_map/ppermute | solution.py:646
  107.8 19.5 %collective-permute-start.28 = (bf16[64,1536]{1,0:T(8,128)(2,1)S(1)}, bf16[64,1536]{1,0:T(8,128)(2,1)S(1)}, u32[]{:S(2)}, u32[]{:S(2)}) collective-permute-start(bf16[64,1536]{1,0:T(8,128)(2,1)S(1)} %pair_sum.1), channel_id=1, source_target_pairs={{0,8},{4,12},{8,0},{12,4},{1,9},{5,13},{9,1},{13,5},{2,10},{6,14},... | collective-permute-start | bytes 589832 | tf_op jit(solution)/shard_map/ppermute | solution.py:646
  121.6 11.6 %collective-permute-start.22 = (bf16[64,1536]{1,0:T(8,128)(2,1)S(1)}, bf16[64,1536]{1,0:T(8,128)(2,1)S(1)}, u32[]{:S(2)}, u32[]{:S(2)}) collective-permute-start(bf16[64,1536]{1,0:T(8,128)(2,1)S(1)} %get-tuple-element.118), channel_id=1, source_target_pairs={{0,8},{4,12},{8,0},{12,4},{1,9},{5,13},{9,1},{13,5},{2,10},{6,14},... | collective-permute-start | bytes 589832 | tf_op jit(solution)/shard_map/ppermute | solution.py:646
  138.1 11.6 %collective-permute-start.30 = (bf16[32,1536]{1,0:T(8,128)(2,1)S(1)}, bf16[32,1536]{1,0:T(8,128)(2,1)S(1)}, u32[]{:S(2)}, u32[]{:S(2)}) collective-permute-start(bf16[32,1536]{1,0:T(8,128)(2,1)S(1)} %get-tuple-element.130), channel_id=1, source_target_pairs={{0,1},{1,0},{2,3},{3,2},{4,5},{5,4},{6,7},{7,6},{8,9},{9,8},{10,11... | collective-permute-start | bytes 294920 | tf_op jit(solution)/shard_map/ppermute | solution.py:646
  149.6 14.3 %collective-permute-start.29 = (bf16[2,64,1536]{2,1,0:T(8,128)(2,1)S(1)}, bf16[2,64,1536]{2,1,0:T(8,128)(2,1)S(1)}, u32[]{:S(2)}, u32[]{:S(2)}) collective-permute-start(bf16[2,64,1536]{2,1,0:T(8,128)(2,1)S(1)} %get-tuple-element.129), channel_id=1, source_target_pairs={{0,16},{16,0},{1,17},{17,1},{2,18},{18,2},{3,19},{19,3},{4,20},{20... | collective-permute-start | bytes 1179656 | tf_op jit(solution)/shard_map/ppermute | solution.py:741
  149.7 13.2 %collective-permute-start.33 = (bf16[32,1536]{1,0:T(8,128)(2,1)S(1)}, bf16[32,1536]{1,0:T(8,128)(2,1)S(1)}, u32[]{:S(2)}, u32[]{:S(2)}) collective-permute-start(bf16[32,1536]{1,0:T(8,128)(2,1)S(1)} %add_convert_fusion.refs_0_), channel_id=1, source_target_pairs={{0,4},{4,0},{8,12},{12,8},{1,5},{5,1},{9,13},{13,9},{2,6},{6,2},{1... | collective-permute-start | bytes 294920 | tf_op jit(solution)/shard_map/ppermute | solution.py:646
  (26 other events, 268.1 us)

commit v6 on v5

--- a/solution.py
+++ b/solution.py
@@ -102,7 +102,7 @@
         mixed_ref[:, cols] = mixed
         return squares + mixed * mixed
 
-    squares = lax.fori_loop(0, features // LANES, chunk, jnp.zeros((frames, LANES), f32))
+    squares = lax.fori_loop(0, features // LANES, chunk, jnp.zeros((frames, LANES), f32), unroll=2)
     return lax.rsqrt(jnp.sum(squares, axis=1, keepdims=True) / features + EPSILON)
 
 
@@ -577,7 +577,7 @@
         term_ref[:, cols] = sums.astype(term_ref.dtype)
         return carry
 
-    lax.fori_loop(0, features // LANES, chunk, 0)
+    lax.fori_loop(0, features // LANES, chunk, 0, unroll=2)
 
 
 def epilogue(m, norm_blocks, x, upstream, saved, taps, gain, before=(), earlier=()):
@@ -618,28 +618,33 @@
 
 
 def last_sum_body(*refs):
-    term_refs, taps_ref, gain_ref = refs[:-2], refs[-2], refs[-1]
+    term_refs, handed_ref, (taps_ref, gain_ref, out_ref, sem) = refs[:-5], refs[-5], refs[-4:]
+    copy = pltpu.make_async_copy(handed_ref, out_ref, sem)
+    copy.start()
     tap_count = taps_ref.shape[0]
     total = tree_sum([ref[...].astype(f32) for ref in term_refs])
     for j in range(tap_count):
         taps_ref[j] = total[j : j + 1, :]
     gain_ref[...] = total[tap_count:, :]
-
-
-def last_sum(terms):
+    copy.wait()
+
+
+def last_sum(terms, handed):
     rows, features = terms[0].shape
     return pl.pallas_call(
         last_sum_body,
         out_shape=(
             jax.ShapeDtypeStruct((rows - 1, 1, features), f32),
             jax.ShapeDtypeStruct((1, features), f32),
+            pltpu.HBM(handed.shape, handed.dtype),
         ),
-        in_specs=whole(len(terms)),
-        out_specs=tuple(whole(2)),
+        in_specs=whole(len(terms)) + after(1),
+        out_specs=tuple(whole(2) + far(1)),
+        scratch_shapes=[pltpu.SemaphoreType.DMA],
         compiler_params=params(16),
         cost_estimate=cost(COSTS[13]),
         name="last_sum",
-    )(*terms)
+    )(*terms, handed)
 
 
 def to_partner(array, axis, k):
@@ -739,8 +744,8 @@
     prev, sums = epilogue(1, second_norm, xs, ups, saved, taps, norm_gain, before=(sums, prev))
     peers = lax.axis_size("pipe")
     handed = lax.ppermute(prev, "pipe", [(i, (i - 1) % peers) for i in range(peers)])
-    sums = tree_sum([term.astype(f32) for term in from_all(sums, "expert")]).astype(bf16)
-    taps_grad, gain_grad = last_sum(from_all(sums, "dp"))
+    sums = tree_sum([term.astype(f32) for term in from_all(sums, "dp")]).astype(bf16)
+    taps_grad, gain_grad, handed = last_sum(from_all(sums, "expert"), handed)
     return (
         handed[None, :, None],
         taps_grad.transpose(1, 0, 2),

time: 165 us -> 164 us (level)
    unnamed x29 -> x28, local copies, waits for them, and re-layouts: 6.41 us -> 5.66 us
  transfers between devices with their start and end apart: 36 -> 36, of which waited for: 12 -> 11; matrix products, arithmetic and copies ran while one was open for 10% -> 10% of each run, Pallas kernels for 27% -> 26%
where the time goes in v6:
time: 164 us
  Pallas kernels  51.9 us (32%)
  starting transfers between devices  48.7 us (30%)
  waiting for transfers between devices  40.7 us (25%)
  matrix products  16 us (10%)
  local copies, waits for them, and re-layouts  5.66 us (3%)
    ppermute x35, starting transfers between devices, to_partner(): lax.ppermute(array, axis, [(i, i ^ k) for i in range(lax.axis_size(axis))])  48.7 us
    ppermute x35, waiting for transfers between devices, to_partner(): lax.ppermute(array, axis, [(i, i ^ k) for i in range(lax.axis_size(axis))])  40.7 us
    pallas_call x4, Pallas kernels, expert_products(): pl.pallas_call(functools.partial(expert_body, parts, rows, capacity if bl...  25.4 us
    pallas_call x2, Pallas kernels, epilogue(): pl.pallas_call(functools.partial(epilogue_body, m, seqs, last, len(earlie...  8.9 us
    dot_general x1, matrix products, local(): lax.dot_general(all_acted, all_grad, over_rows, preferred_element_type=f32)  8 us
    dot_general x1, matrix products, local(): lax.dot_general(all_in, all_pre, over_rows, preferred_element_type=f32)  7.97 us
    unnamed x28, local copies, waits for them, and re-layouts  5.66 us
    pallas_call x3, Pallas kernels, frame_sums(): pl.pallas_call(functools.partial(frame_sums_body, m, len(blocks), frames,...  5.27 us
  transfers between devices with their start and end apart: 36, of which 11 were waited for; matrix products, arithmetic and copies ran while one was open for 10% of the time, Pallas kernels for 26%

profile of v6, /device:TPU:0, one launch (start us, length us, event | category | flops | bytes accessed | tf_op | source)
XLA Modules:
  0.0 164.0 jit_solution(5813233359420955050)
XLA Ops:
  0.6 3.1 %first_send.1._.refs_0_ = bf16[144,1536]{1,0:T(8,128)(2,1)} custom-call(bf16[2,64,1536]{2,1,0:T(8,128)(2,1)} %bitcast.31, bf16[2,64,1536]{2,1,0:T(8,128)(2,1)} %bitcast.36, s32[2,2,64]{2,1,0:T(2,128)} %bitcast.45, f32[2,2,64]{2,1,0:T(2,128)} %bitcast.47, f32[31,1,1536]{2,1,0:T(1,128)} %bitcast.40, f32[1,1536]{1,0:T(1,128)} %refs_10_.1), custom_call_target="tpu_custom_call" | custom-call | flops 1 | bytes 1 | tf_op jit(solution)/shard_map/first_send/pallas_call | solution.py:151
  3.8 3.1 %collective-permute-start = (bf16[144,1536]{1,0:T(8,128)(2,1)}, bf16[144,1536]{1,0:T(8,128)(2,1)S(1)}, u32[]{:S(2)}, u32[]{:S(2)}) collective-permute-start(bf16[144,1536]{1,0:T(8,128)(2,1)} %first_send.1._.refs_0_), channel_id=1, source_target_pairs={{0,4},{4,0},{8,12},{12,8},{1,5},{5,1},{9,13},{13,9},{2,6},{6,2},{1... | collective-permute-start | bytes 1327112 | tf_op jit(solution)/shard_map/ppermute | solution.py:651
  6.8 2.6 %collective-permute-start.4 = (bf16[144,1536]{1,0:T(8,128)(2,1)}, bf16[144,1536]{1,0:T(8,128)(2,1)S(1)}, u32[]{:S(2)}, u32[]{:S(2)}) collective-permute-start(bf16[144,1536]{1,0:T(8,128)(2,1)} %first_send.1._.refs_0_), channel_id=1, source_target_pairs={{0,8},{4,12},{8,0},{12,4},{1,9},{5,13},{9,1},{13,5},{2,10},{6,14},... | collective-permute-start | bytes 1327112 | tf_op jit(solution)/shard_map/ppermute | solution.py:651
  9.4 3.7 %second_send.1 = (bf16[72,1536]{1,0:T(8,128)(2,1)}, bf16[72,1536]{1,0:T(8,128)(2,1)}, bf16[72,1536]{1,0:T(8,128)(2,1)}, bf16[72,1536]{1,0:T(8,128)(2,1)}) custom-call(bf16[2,64,1536]{2,1,0:T(8,128)(2,1)} %bitcast.32, bf16[2,64,1536]{2,1,0:T(8,128)(2,1)} %bitcast.37, s32[2,2,64]{2,1,0:T(2,128)} %bitcast.46, f32[2,2,64]{2,1,0:T(2,128)} %bitcast.48, ...), custom_call_target="tpu_custom_call" | custom-call | flops 13800000512 | bytes 1 | tf_op jit(solution)/shard_map/second_send/pallas_call | solution.py:196
  16.7 5.1 %collective-permute-done.1.refs_3_ = bf16[72,1536]{1,0:T(8,128)(2,1)S(1)} collective-permute-done((bf16[72,1536]{1,0:T(8,128)(2,1)}, bf16[72,1536]{1,0:T(8,128)(2,1)S(1)}, u32[]{:S(2)}, u32[]{:S(2)}) %collective-permute-start.1) | collective-permute-done | bytes 221216 | tf_op jit(solution)/shard_map/ppermute | solution.py:651
  21.8 4.2 %collective-permute-done.2.refs_4_ = bf16[72,1536]{1,0:T(8,128)(2,1)S(1)} collective-permute-done((bf16[72,1536]{1,0:T(8,128)(2,1)}, bf16[72,1536]{1,0:T(8,128)(2,1)S(1)}, u32[]{:S(2)}, u32[]{:S(2)}) %collective-permute-start.2) | collective-permute-done | bytes 221216 | tf_op jit(solution)/shard_map/ppermute | solution.py:651
  29.6 2.4 %collective-permute-start.10 = (bf16[144,1536]{1,0:T(8,128)(2,1)S(1)}, bf16[144,1536]{1,0:T(8,128)(2,1)S(1)}, u32[]{:S(2)}, u32[]{:S(2)}) collective-permute-start(bf16[144,1536]{1,0:T(8,128)(2,1)S(1)} %get-tuple-element.82), channel_id=1, source_target_pairs={{0,3},{1,2},{2,1},{3,0},{4,7},{5,6},{6,5},{7,4},{8,11},{9,10},{10,... | collective-permute-start | bytes 1327112 | tf_op jit(solution)/shard_map/ppermute | solution.py:651
  33.1 2.6 %collective-permute-start.7 = (bf16[4,72,1536]{2,1,0:T(8,128)(2,1)S(1)}, bf16[4,72,1536]{2,1,0:T(8,128)(2,1)S(1)}, u32[]{:S(2)}, u32[]{:S(2)}) collective-permute-start(bf16[4,72,1536]{2,1,0:T(8,128)(2,1)S(1)} %passed.4.refs_0_), channel_id=1, source_target_pairs={{0,8},{4,12},{8,0},{12,4},{1,9},{5,13},{9,1},{13,5},{2,10},{6,14},... | collective-permute-start | bytes 2654216 | tf_op jit(solution)/shard_map/ppermute | solution.py:651
  37.9 8.0 %collective-permute-done.5.refs_1_ = bf16[144,1536]{1,0:T(8,128)(2,1)S(1)} collective-permute-done((bf16[144,1536]{1,0:T(8,128)(2,1)S(1)}, bf16[144,1536]{1,0:T(8,128)(2,1)S(1)}, u32[]{:S(2)}, u32[]{:S(2)}) %collective-permute-start.5) | collective-permute-done | bytes 442400 | tf_op jit(solution)/shard_map/ppermute | solution.py:651
  48.2 4.9 %collective-permute-done.8.refs_1_ = bf16[144,1536]{1,0:T(8,128)(2,1)S(1)} collective-permute-done((bf16[144,1536]{1,0:T(8,128)(2,1)S(1)}, bf16[144,1536]{1,0:T(8,128)(2,1)S(1)}, u32[]{:S(2)}, u32[]{:S(2)}) %collective-permute-start.8) | collective-permute-done | bytes 442400 | tf_op jit(solution)/shard_map/ppermute | solution.py:651
  60.8 5.6 %expert_products.4 = (bf16[72,1536]{1,0:T(8,128)(2,1)S(1)}, bf16[72,1536]{1,0:T(8,128)(2,1)S(1)}, bf16[72,1536]{1,0:T(8,128)(2,1)S(1)}, bf16[72,1536]{1,0:T(8,12...) custom-call(bf16[144,1536]{1,0:T(8,128)(2,1)S(1)} %get-tuple-element, ...), custom_call_target="tpu_custom_call" | custom-call | flops 13800000512 | bytes 1 | tf_op jit(solution)/shard_map/expert_products/pallas_call | solution.py:415
  66.4 4.5 %collective-permute-done.12.refs_2_ = bf16[144,1536]{1,0:T(8,128)(2,1)S(1)} collective-permute-done((bf16[144,1536]{1,0:T(8,128)(2,1)S(1)}, bf16[144,1536]{1,0:T(8,128)(2,1)S(1)}, u32[]{:S(2)}, u32[]{:S(2)}) %collective-permute-start.12) | collective-permute-done | bytes 442400 | tf_op jit(solution)/shard_map/ppermute | solution.py:651
  70.9 5.7 %expert_products.5 = (bf16[144,1536]{1,0:T(8,128)(2,1)S(1)}, bf16[144,1536]{1,0:T(8,128)(2,1)S(1)}, bf16[144,1536]{1,0:T(8,128)(2,1)S(1)}, bf16[144,1536]{1,0:T(...) custom-call(bf16[144,1536]{1,0:T(8,128)(2,1)S(1)} %get-tuple-element, ...), custom_call_target="tpu_custom_call", output_to_operand_aliasing={{4}: (10, {}), {5}: (11, {}), {6}: (12, {}), {7}: (13, {})} | custom-call | flops 1 | bytes 1 | tf_op jit(solution)/shard_map/expert_products/pallas_call | solution.py:415
  81.8 8.8 %expert_products.6 = (bf16[112,1536]{1,0:T(8,128)(2,1)S(1)}, bf16[112,1536]{1,0:T(8,128)(2,1)S(1)}, bf16[112,1536]{1,0:T(8,128)(2,1)S(1)}, bf16[112,1536]{1,0:T(...) custom-call(bf16[4,72,1536]{2,1,0:T(8,128)(2,1)S(1)} %passed.4.refs_, ...), custom_call_target="tpu_custom_call", output_to_operand_aliasing={{4}: (5, {}), {5}: (6, {}), {6}: (7, {}), {7}: (8, {})} | custom-call | flops 11500000256 | bytes 1 | tf_op jit(solution)/shard_map/expert_products/pallas_call | solution.py:415
  90.5 5.4 %collective-permute-done.19.refs_4_ = bf16[144,1536]{1,0:T(8,128)(2,1)S(1)} collective-permute-done((bf16[144,1536]{1,0:T(8,128)(2,1)S(1)}, bf16[144,1536]{1,0:T(8,128)(2,1)S(1)}, u32[]{:S(2)}, u32[]{:S(2)}) %collective-permute-start.19) | collective-permute-done | bytes 442400 | tf_op jit(solution)/shard_map/ppermute | solution.py:651
  102.9 4.7 %collective-permute-done.27.got_ref.refs_1_ = bf16[128,1536]{1,0:T(8,128)(2,1)S(1)} collective-permute-done((bf16[128,1536]{1,0:T(8,128)(2,1)S(1)}, bf16[128,1536]{1,0:T(8,128)(2,1)S(1)}, u32[]{:S(2)}, u32[]{:S(2)}) %collective-permute-start.27) | collective-permute-done | bytes 393248 | tf_op jit(solution)/shard_map/ppermute | solution.py:651
  107.7 2.9 %collective-permute-start.28 = (bf16[64,1536]{1,0:T(8,128)(2,1)S(1)}, bf16[64,1536]{1,0:T(8,128)(2,1)S(1)}, u32[]{:S(2)}, u32[]{:S(2)}) collective-permute-start(bf16[64,1536]{1,0:T(8,128)(2,1)S(1)} %pair_sum.1), channel_id=1, source_target_pairs={{0,8},{4,12},{8,0},{12,4},{1,9},{5,13},{9,1},{13,5},{2,10},{6,14},... | collective-permute-start | bytes 589832 | tf_op jit(solution)/shard_map/ppermute | solution.py:651
  110.6 5.3 %expert_products.7 = (bf16[40,1536]{1,0:T(8,128)(2,1)S(1)}, bf16[40,1536]{1,0:T(8,128)(2,1)S(1)}, bf16[40,1536]{1,0:T(8,128)(2,1)S(1)}, bf16[40,1536]{1,0:T(8,12...) custom-call(bf16[4,72,1536]{2,1,0:T(8,128)(2,1)S(1)} %collective-per, ...), custom_call_target="tpu_custom_call", output_to_operand_aliasing={{4}: (4, {}), {5}: (5, {}), {6}: (6, {}), {7}: (7, {})} | custom-call | flops 1 | bytes 1 | tf_op jit(solution)/shard_map/expert_products/pallas_call | solution.py:415
  124.2 3.0 %collective-permute-start.26 = (bf16[64,1536]{1,0:T(8,128)(2,1)S(1)}, bf16[64,1536]{1,0:T(8,128)(2,1)S(1)}, u32[]{:S(2)}, u32[]{:S(2)}) collective-permute-start(bf16[64,1536]{1,0:T(8,128)(2,1)S(1)} %frame_sums.5), channel_id=1, source_target_pairs={{0,12},{4,8},{8,4},{12,0},{1,13},{5,9},{9,5},{13,1},{2,14},{6,10},... | collective-permute-start | bytes 589832 | tf_op jit(solution)/shard_map/ppermute | solution.py:651
  127.2 4.4 %norm_conv_back.2 = (bf16[64,1536]{1,0:T(8,128)(2,1)S(1)}, f32[32,1536]{1,0:T(8,128)S(1)}) custom-call(f32[64,1536]{1,0:T(8,128)S(1)} %get-tuple-element.108.refs_3_.refs_0_, bf16[128,1536]{1,0:T(8,128)(2,1)S(1)} %collective-permute-done.27.got_ref.refs_1_, bf16[64,1536]{1,0:T(8,128)(2,1)S(1)} %collective-permute-done.28.refs_2_, ...), custom_call_target="tpu_custom_call" | custom-call | flops 1 | bytes 1 | tf_op jit(solution)/shard_map/norm_conv_back/pallas_call | solution.py:588
  133.1 4.5 %norm_conv_back.3 = (bf16[2,64,1536]{2,1,0:T(8,128)(2,1)S(1)}, bf16[32,1536]{1,0:T(8,128)(2,1)S(1)}) custom-call(f32[64,1536]{1,0:T(8,128)S(1)} %get-tuple-element.117.refs_0_, bf16[64,1536]{1,0:T(8,128)(2,1)S(1)} %collective-permute-done.21.refs_1_, bf16[64,1536]{1,0:T(8,128)(2,1)S(1)} %collective-permute-done.22.refs_2_, ...), custom_call_target="tpu_custom_call" | custom-call | flops 1 | bytes 1 | tf_op jit(solution)/shard_map/norm_conv_back/pallas_call | solution.py:588
  137.6 2.7 %collective-permute-start.29 = (bf16[32,1536]{1,0:T(8,128)(2,1)S(1)}, bf16[32,1536]{1,0:T(8,128)(2,1)S(1)}, u32[]{:S(2)}, u32[]{:S(2)}) collective-permute-start(bf16[32,1536]{1,0:T(8,128)(2,1)S(1)} %get-tuple-element.130), channel_id=1, source_target_pairs={{0,4},{4,0},{8,12},{12,8},{1,5},{5,1},{9,13},{13,9},{2,6},{6,2},{1... | collective-permute-start | bytes 294920 | tf_op jit(solution)/shard_map/ppermute | solution.py:651
  142.8 8.0 %fusion.1 = bf16[1,1,1536,1536]{3,2,1,0:T(8,128)(2,1)} fusion(bf16[1184,1536]{1,0:T(8,128)(2,1)S(1)} %copy-done.12, bf16[1184,1536]{1,0:T(8,128)(2,1)S(1)} %copy-done.11), kind=kOutput, calls=%fused_computation.3 | convolution fusion | flops 5589172224 | bytes 11993088 | tf_op jit(solution)/shard_map/dot_general | solution.py:740
  154.4 8.0 %fusion = bf16[1,1,1536,1536]{3,2,1,0:T(8,128)(2,1)} fusion(bf16[1184,1536]{1,0:T(8,128)(2,1)S(1)} %copy-done.10, bf16[1184,1536]{1,0:T(8,128)(2,1)S(1)} %copy-done.13), kind=kOutput, calls=%fused_computation.2 | convolution fusion | flops 5589172224 | bytes 11993088 | tf_op jit(solution)/shard_map/dot_general | solution.py:739
  (98 shorter events, 49.6 us)
Async XLA Ops:
  3.8 22.8 %collective-permute-start = (bf16[144,1536]{1,0:T(8,128)(2,1)}, bf16[144,1536]{1,0:T(8,128)(2,1)S(1)}, u32[]{:S(2)}, u32[]{:S(2)}) collective-permute-start(bf16[144,1536]{1,0:T(8,128)(2,1)} %first_send.1._.refs_0_), channel_id=1, source_target_pairs={{0,4},{4,0},{8,12},{12,8},{1,5},{5,1},{9,13},{13,9},{2,6},{6,2},{1... | collective-permute-start | bytes 1327112 | tf_op jit(solution)/shard_map/ppermute | solution.py:651
  6.8 22.3 %collective-permute-start.4 = (bf16[144,1536]{1,0:T(8,128)(2,1)}, bf16[144,1536]{1,0:T(8,128)(2,1)S(1)}, u32[]{:S(2)}, u32[]{:S(2)}) collective-permute-start(bf16[144,1536]{1,0:T(8,128)(2,1)} %first_send.1._.refs_0_), channel_id=1, source_target_pairs={{0,8},{4,12},{8,0},{12,4},{1,9},{5,13},{9,1},{13,5},{2,10},{6,14},... | collective-permute-start | bytes 1327112 | tf_op jit(solution)/shard_map/ppermute | solution.py:651
  14.8 11.3 %collective-permute-start.2 = (bf16[72,1536]{1,0:T(8,128)(2,1)}, bf16[72,1536]{1,0:T(8,128)(2,1)S(1)}, u32[]{:S(2)}, u32[]{:S(2)}) collective-permute-start(bf16[72,1536]{1,0:T(8,128)(2,1)} %get-tuple-element.74), channel_id=1, source_target_pairs={{0,2},{1,3},{2,0},{3,1},{4,6},{5,7},{6,4},{7,5},{8,10},{9,11},{10,... | collective-permute-start | bytes 663560 | tf_op jit(solution)/shard_map/ppermute | solution.py:651
  29.1 16.8 %collective-permute-start.5 = (bf16[144,1536]{1,0:T(8,128)(2,1)S(1)}, bf16[144,1536]{1,0:T(8,128)(2,1)S(1)}, u32[]{:S(2)}, u32[]{:S(2)}) collective-permute-start(bf16[144,1536]{1,0:T(8,128)(2,1)S(1)} %passed.3.refs_0_.refs_1_), channel_id=1, source_target_pairs={{0,4},{4,0},{8,12},{12,8},{1,5},{5,1},{9,13},{13,9},{2,6},{6,2},{1... | collective-permute-start | bytes 1327112 | tf_op jit(solution)/shard_map/ppermute | solution.py:651
  29.6 17.2 %collective-permute-start.10 = (bf16[144,1536]{1,0:T(8,128)(2,1)S(1)}, bf16[144,1536]{1,0:T(8,128)(2,1)S(1)}, u32[]{:S(2)}, u32[]{:S(2)}) collective-permute-start(bf16[144,1536]{1,0:T(8,128)(2,1)S(1)} %get-tuple-element.82), channel_id=1, source_target_pairs={{0,3},{1,2},{2,1},{3,0},{4,7},{5,6},{6,5},{7,4},{8,11},{9,10},{10,... | collective-permute-start | bytes 1327112 | tf_op jit(solution)/shard_map/ppermute | solution.py:651
  32.0 21.1 %collective-permute-start.8 = (bf16[144,1536]{1,0:T(8,128)(2,1)S(1)}, bf16[144,1536]{1,0:T(8,128)(2,1)S(1)}, u32[]{:S(2)}, u32[]{:S(2)}) collective-permute-start(bf16[144,1536]{1,0:T(8,128)(2,1)S(1)} %get-tuple-element.80), channel_id=1, source_target_pairs={{0,1},{1,0},{2,3},{3,2},{4,5},{5,4},{6,7},{7,6},{8,9},{9,8},{10,11... | collective-permute-start | bytes 1327112 | tf_op jit(solution)/shard_map/ppermute | solution.py:651
  32.5 21.1 %collective-permute-start.9 = (bf16[144,1536]{1,0:T(8,128)(2,1)S(1)}, bf16[144,1536]{1,0:T(8,128)(2,1)S(1)}, u32[]{:S(2)}, u32[]{:S(2)}) collective-permute-start(bf16[144,1536]{1,0:T(8,128)(2,1)S(1)} %get-tuple-element.81), channel_id=1, source_target_pairs={{0,2},{1,3},{2,0},{3,1},{4,6},{5,7},{6,4},{7,5},{8,10},{9,11},{10,... | collective-permute-start | bytes 1327112 | tf_op jit(solution)/shard_map/ppermute | solution.py:651
  33.1 47.1 %collective-permute-start.7 = (bf16[4,72,1536]{2,1,0:T(8,128)(2,1)S(1)}, bf16[4,72,1536]{2,1,0:T(8,128)(2,1)S(1)}, u32[]{:S(2)}, u32[]{:S(2)}) collective-permute-start(bf16[4,72,1536]{2,1,0:T(8,128)(2,1)S(1)} %passed.4.refs_0_), channel_id=1, source_target_pairs={{0,8},{4,12},{8,0},{12,4},{1,9},{5,13},{9,1},{13,5},{2,10},{6,14},... | collective-permute-start | bytes 2654216 | tf_op jit(solution)/shard_map/ppermute | solution.py:651
  45.9 35.8 %collective-permute-start.6 = (bf16[4,72,1536]{2,1,0:T(8,128)(2,1)S(1)}, bf16[4,72,1536]{2,1,0:T(8,128)(2,1)S(1)}, u32[]{:S(2)}, u32[]{:S(2)}) collective-permute-start(bf16[4,72,1536]{2,1,0:T(8,128)(2,1)S(1)} %passed.4.refs_0_), channel_id=1, source_target_pairs={{0,4},{4,0},{8,12},{12,8},{1,5},{5,1},{9,13},{13,9},{2,6},{6,2},{1... | collective-permute-start | bytes 2654216 | tf_op jit(solution)/shard_map/ppermute | solution.py:651
  46.8 19.6 %collective-permute-start.11 = (bf16[144,1536]{1,0:T(8,128)(2,1)S(1)}, bf16[144,1536]{1,0:T(8,128)(2,1)S(1)}, u32[]{:S(2)}, u32[]{:S(2)}) collective-permute-start(bf16[144,1536]{1,0:T(8,128)(2,1)S(1)} %get-tuple-element.86), channel_id=1, source_target_pairs={{0,1},{1,0},{2,3},{3,2},{4,5},{5,4},{6,7},{7,6},{8,9},{9,8},{10,11... | collective-permute-start | bytes 1327112 | tf_op jit(solution)/shard_map/ppermute | solution.py:651
  53.1 17.8 %collective-permute-start.12 = (bf16[144,1536]{1,0:T(8,128)(2,1)S(1)}, bf16[144,1536]{1,0:T(8,128)(2,1)S(1)}, u32[]{:S(2)}, u32[]{:S(2)}) collective-permute-start(bf16[144,1536]{1,0:T(8,128)(2,1)S(1)} %get-tuple-element.87), channel_id=1, source_target_pairs={{0,2},{1,3},{2,0},{3,1},{4,6},{5,7},{6,4},{7,5},{8,10},{9,11},{10,... | collective-permute-start | bytes 1327112 | tf_op jit(solution)/shard_map/ppermute | solution.py:651
  53.7 17.2 %collective-permute-start.13 = (bf16[144,1536]{1,0:T(8,128)(2,1)S(1)}, bf16[144,1536]{1,0:T(8,128)(2,1)S(1)}, u32[]{:S(2)}, u32[]{:S(2)}) collective-permute-start(bf16[144,1536]{1,0:T(8,128)(2,1)S(1)} %get-tuple-element.88), channel_id=1, source_target_pairs={{0,3},{1,2},{2,1},{3,0},{4,7},{5,6},{6,5},{7,4},{8,11},{9,10},{10,... | collective-permute-start | bytes 1327112 | tf_op jit(solution)/shard_map/ppermute | solution.py:651
  76.6 13.9 %collective-permute-start.18 = (bf16[144,1536]{1,0:T(8,128)(2,1)S(1)}, bf16[144,1536]{1,0:T(8,128)(2,1)S(1)}, u32[]{:S(2)}, u32[]{:S(2)}) collective-permute-start(bf16[144,1536]{1,0:T(8,128)(2,1)S(1)} %get-tuple-element.105), channel_id=1, source_target_pairs={{0,1},{1,0},{2,3},{3,2},{4,5},{5,4},{6,7},{7,6},{8,9},{9,8},{10,11... | collective-permute-start | bytes 1327112 | tf_op jit(solution)/shard_map/ppermute | solution.py:651
  78.2 17.8 %collective-permute-start.19 = (bf16[144,1536]{1,0:T(8,128)(2,1)S(1)}, bf16[144,1536]{1,0:T(8,128)(2,1)S(1)}, u32[]{:S(2)}, u32[]{:S(2)}) collective-permute-start(bf16[144,1536]{1,0:T(8,128)(2,1)S(1)} %get-tuple-element.106), channel_id=1, source_target_pairs={{0,2},{1,3},{2,0},{3,1},{4,6},{5,7},{6,4},{7,5},{8,10},{9,11},{10,... | collective-permute-start | bytes 1327112 | tf_op jit(solution)/shard_map/ppermute | solution.py:651
  78.7 17.3 %collective-permute-start.20 = (bf16[144,1536]{1,0:T(8,128)(2,1)S(1)}, bf16[144,1536]{1,0:T(8,128)(2,1)S(1)}, u32[]{:S(2)}, u32[]{:S(2)}) collective-permute-start(bf16[144,1536]{1,0:T(8,128)(2,1)S(1)} %get-tuple-element.107), channel_id=1, source_target_pairs={{0,3},{1,2},{2,1},{3,0},{4,7},{5,6},{6,5},{7,4},{8,11},{9,10},{10,... | collective-permute-start | bytes 1327112 | tf_op jit(solution)/shard_map/ppermute | solution.py:651
  80.2 30.4 %collective-permute-start.17 = (bf16[4,72,1536]{2,1,0:T(8,128)(2,1)S(1)}, bf16[4,72,1536]{2,1,0:T(8,128)(2,1)S(1)}, u32[]{:S(2)}, u32[]{:S(2)}) collective-permute-start(bf16[4,72,1536]{2,1,0:T(8,128)(2,1)S(1)} %passed.5.refs_2_), channel_id=1, source_target_pairs={{0,4},{4,0},{8,12},{12,8},{1,5},{5,1},{9,13},{13,9},{2,6},{6,2},{1... | collective-permute-start | bytes 2654216 | tf_op jit(solution)/shard_map/ppermute | solution.py:651
  99.4 16.7 %collective-permute-start.14 = (bf16[112,1536]{1,0:T(8,128)(2,1)S(1)}, bf16[112,1536]{1,0:T(8,128)(2,1)S(1)}, u32[]{:S(2)}, u32[]{:S(2)}) collective-permute-start(bf16[112,1536]{1,0:T(8,128)(2,1)S(1)} %get-tuple-element.101), channel_id=1, source_target_pairs={{0,1},{1,0},{2,3},{3,2},{4,5},{5,4},{6,7},{7,6},{8,9},{9,8},{10,11... | collective-permute-start | bytes 1032200 | tf_op jit(solution)/shard_map/ppermute | solution.py:651
  100.2 16.9 %collective-permute-start.15 = (bf16[112,1536]{1,0:T(8,128)(2,1)S(1)}, bf16[112,1536]{1,0:T(8,128)(2,1)S(1)}, u32[]{:S(2)}, u32[]{:S(2)}) collective-permute-start(bf16[112,1536]{1,0:T(8,128)(2,1)S(1)} %get-tuple-element.102), channel_id=1, source_target_pairs={{0,2},{1,3},{2,0},{3,1},{4,6},{5,7},{6,4},{7,5},{8,10},{9,11},{10,... | collective-permute-start | bytes 1032200 | tf_op jit(solution)/shard_map/ppermute | solution.py:651
  101.1 18.3 %collective-permute-start.16 = (bf16[112,1536]{1,0:T(8,128)(2,1)S(1)}, bf16[112,1536]{1,0:T(8,128)(2,1)S(1)}, u32[]{:S(2)}, u32[]{:S(2)}) collective-permute-start(bf16[112,1536]{1,0:T(8,128)(2,1)S(1)} %get-tuple-element.103), channel_id=1, source_target_pairs={{0,3},{1,2},{2,1},{3,0},{4,7},{5,6},{6,5},{7,4},{8,11},{9,10},{10,... | collective-permute-start | bytes 1032200 | tf_op jit(solution)/shard_map/ppermute | solution.py:651
  107.7 19.5 %collective-permute-start.28 = (bf16[64,1536]{1,0:T(8,128)(2,1)S(1)}, bf16[64,1536]{1,0:T(8,128)(2,1)S(1)}, u32[]{:S(2)}, u32[]{:S(2)}) collective-permute-start(bf16[64,1536]{1,0:T(8,128)(2,1)S(1)} %pair_sum.1), channel_id=1, source_target_pairs={{0,8},{4,12},{8,0},{12,4},{1,9},{5,13},{9,1},{13,5},{2,10},{6,14},... | collective-permute-start | bytes 589832 | tf_op jit(solution)/shard_map/ppermute | solution.py:651
  121.5 11.6 %collective-permute-start.22 = (bf16[64,1536]{1,0:T(8,128)(2,1)S(1)}, bf16[64,1536]{1,0:T(8,128)(2,1)S(1)}, u32[]{:S(2)}, u32[]{:S(2)}) collective-permute-start(bf16[64,1536]{1,0:T(8,128)(2,1)S(1)} %get-tuple-element.119), channel_id=1, source_target_pairs={{0,8},{4,12},{8,0},{12,4},{1,9},{5,13},{9,1},{13,5},{2,10},{6,14},... | collective-permute-start | bytes 589832 | tf_op jit(solution)/shard_map/ppermute | solution.py:651
  137.6 13.2 %collective-permute-start.29 = (bf16[32,1536]{1,0:T(8,128)(2,1)S(1)}, bf16[32,1536]{1,0:T(8,128)(2,1)S(1)}, u32[]{:S(2)}, u32[]{:S(2)}) collective-permute-start(bf16[32,1536]{1,0:T(8,128)(2,1)S(1)} %get-tuple-element.130), channel_id=1, source_target_pairs={{0,4},{4,0},{8,12},{12,8},{1,5},{5,1},{9,13},{13,9},{2,6},{6,2},{1... | collective-permute-start | bytes 294920 | tf_op jit(solution)/shard_map/ppermute | solution.py:651
  150.8 11.6 %collective-permute-start.35 = (bf16[2,64,1536]{2,1,0:T(8,128)(2,1)S(1)}, bf16[2,64,1536]{2,1,0:T(8,128)(2,1)S(1)}, u32[]{:S(2)}, u32[]{:S(2)}) collective-permute-start(bf16[2,64,1536]{2,1,0:T(8,128)(2,1)S(1)} %get-tuple-element.131), channel_id=1, source_target_pairs={{0,16},{16,0},{1,17},{17,1},{2,18},{18,2},{3,19},{19,3},{4,20},{20... | collective-permute-start | bytes 1179656 | tf_op jit(solution)/shard_map/ppermute | solution.py:746
  150.9 11.5 %collective-permute-start.32 = (bf16[32,1536]{1,0:T(8,128)(2,1)S(1)}, bf16[32,1536]{1,0:T(8,128)(2,1)S(1)}, u32[]{:S(2)}, u32[]{:S(2)}) collective-permute-start(bf16[32,1536]{1,0:T(8,128)(2,1)S(1)} %add_convert_fusion.refs_0_), channel_id=1, source_target_pairs={{0,1},{1,0},{2,3},{3,2},{4,5},{5,4},{6,7},{7,6},{8,9},{9,8},{10,11... | collective-permute-start | bytes 294920 | tf_op jit(solution)/shard_map/ppermute | solution.py:651
  (26 other events, 266.6 us)

commit v7 on v6

--- a/solution.py
+++ b/solution.py
@@ -102,7 +102,7 @@
         mixed_ref[:, cols] = mixed
         return squares + mixed * mixed
 
-    squares = lax.fori_loop(0, features // LANES, chunk, jnp.zeros((frames, LANES), f32), unroll=2)
+    squares = lax.fori_loop(0, features // LANES, chunk, jnp.zeros((frames, LANES), f32), unroll=4)
     return lax.rsqrt(jnp.sum(squares, axis=1, keepdims=True) / features + EPSILON)
 
 
@@ -547,7 +547,7 @@
         gain_parts[c] = tiles_sum(weighed * scale)
         return inner + weighed * gain_ref[:, cols]
 
-    inner = lax.fori_loop(0, features // LANES, gather, jnp.zeros((frames, LANES), f32))
+    inner = lax.fori_loop(0, features // LANES, gather, jnp.zeros((frames, LANES), f32), unroll=4)
     for copy in copies:
         copy.wait()
     pull = scale * scale * scale * (jnp.sum(inner, axis=1, keepdims=True) / features)
@@ -577,7 +577,7 @@
         term_ref[:, cols] = sums.astype(term_ref.dtype)
         return carry
 
-    lax.fori_loop(0, features // LANES, chunk, 0, unroll=2)
+    lax.fori_loop(0, features // LANES, chunk, 0, unroll=4)
 
 
 def epilogue(m, norm_blocks, x, upstream, saved, taps, gain, before=(), earlier=()):

time: 164 us -> 163 us (level)
  Pallas kernels: 51.9 us -> 50.1 us
where the time goes in v7:
time: 163 us
  Pallas kernels  50.1 us (31%)
  starting transfers between devices  48.7 us (30%)
  waiting for transfers between devices  41.6 us (26%)
  matrix products  16 us (10%)
  local copies, waits for them, and re-layouts  5.66 us (3%)
    ppermute x35, starting transfers between devices, to_partner(): lax.ppermute(array, axis, [(i, i ^ k) for i in range(lax.axis_size(axis))])  48.7 us
    ppermute x35, waiting for transfers between devices, to_partner(): lax.ppermute(array, axis, [(i, i ^ k) for i in range(lax.axis_size(axis))])  41.6 us
    pallas_call x4, Pallas kernels, expert_products(): pl.pallas_call(functools.partial(expert_body, parts, rows, capacity if bl...  25.5 us
    dot_general x1, matrix products, local(): lax.dot_general(all_acted, all_grad, over_rows, preferred_element_type=f32)  8 us
    dot_general x1, matrix products, local(): lax.dot_general(all_in, all_pre, over_rows, preferred_element_type=f32)  7.99 us
    pallas_call x2, Pallas kernels, epilogue(): pl.pallas_call(functools.partial(epilogue_body, m, seqs, last, len(earlie...  7.34 us
    unnamed x28, local copies, waits for them, and re-layouts  5.66 us
    pallas_call x3, Pallas kernels, frame_sums(): pl.pallas_call(functools.partial(frame_sums_body, m, len(blocks), frames,...  5.27 us
  transfers between devices with their start and end apart: 36, of which 11 were waited for; matrix products, arithmetic and copies ran while one was open for 10% of the time, Pallas kernels for 26%

profile of v7, /device:TPU:0, one launch (start us, length us, event | category | flops | bytes accessed | tf_op | source)
XLA Modules:
  0.0 163.2 jit_solution(8683450666972989284)
XLA Ops:
  0.6 3.1 %first_send.1._.refs_0_ = bf16[144,1536]{1,0:T(8,128)(2,1)} custom-call(bf16[2,64,1536]{2,1,0:T(8,128)(2,1)} %bitcast.31, bf16[2,64,1536]{2,1,0:T(8,128)(2,1)} %bitcast.36, s32[2,2,64]{2,1,0:T(2,128)} %bitcast.45, f32[2,2,64]{2,1,0:T(2,128)} %bitcast.47, f32[31,1,1536]{2,1,0:T(1,128)} %bitcast.40, f32[1,1536]{1,0:T(1,128)} %refs_10_.1), custom_call_target="tpu_custom_call" | custom-call | flops 1 | bytes 1 | tf_op jit(solution)/shard_map/first_send/pallas_call | solution.py:151
  3.7 3.1 %collective-permute-start = (bf16[144,1536]{1,0:T(8,128)(2,1)}, bf16[144,1536]{1,0:T(8,128)(2,1)S(1)}, u32[]{:S(2)}, u32[]{:S(2)}) collective-permute-start(bf16[144,1536]{1,0:T(8,128)(2,1)} %first_send.1._.refs_0_), channel_id=1, source_target_pairs={{0,4},{4,0},{8,12},{12,8},{1,5},{5,1},{9,13},{13,9},{2,6},{6,2},{1... | collective-permute-start | bytes 1327112 | tf_op jit(solution)/shard_map/ppermute | solution.py:651
  6.8 2.6 %collective-permute-start.4 = (bf16[144,1536]{1,0:T(8,128)(2,1)}, bf16[144,1536]{1,0:T(8,128)(2,1)S(1)}, u32[]{:S(2)}, u32[]{:S(2)}) collective-permute-start(bf16[144,1536]{1,0:T(8,128)(2,1)} %first_send.1._.refs_0_), channel_id=1, source_target_pairs={{0,8},{4,12},{8,0},{12,4},{1,9},{5,13},{9,1},{13,5},{2,10},{6,14},... | collective-permute-start | bytes 1327112 | tf_op jit(solution)/shard_map/ppermute | solution.py:651
  9.4 3.7 %second_send.1 = (bf16[72,1536]{1,0:T(8,128)(2,1)}, bf16[72,1536]{1,0:T(8,128)(2,1)}, bf16[72,1536]{1,0:T(8,128)(2,1)}, bf16[72,1536]{1,0:T(8,128)(2,1)}) custom-call(bf16[2,64,1536]{2,1,0:T(8,128)(2,1)} %bitcast.32, bf16[2,64,1536]{2,1,0:T(8,128)(2,1)} %bitcast.37, s32[2,2,64]{2,1,0:T(2,128)} %bitcast.46, f32[2,2,64]{2,1,0:T(2,128)} %bitcast.48, ...), custom_call_target="tpu_custom_call" | custom-call | flops 13800000512 | bytes 1 | tf_op jit(solution)/shard_map/second_send/pallas_call | solution.py:196
  16.7 5.1 %collective-permute-done.1.refs_3_ = bf16[72,1536]{1,0:T(8,128)(2,1)S(1)} collective-permute-done((bf16[72,1536]{1,0:T(8,128)(2,1)}, bf16[72,1536]{1,0:T(8,128)(2,1)S(1)}, u32[]{:S(2)}, u32[]{:S(2)}) %collective-permute-start.1) | collective-permute-done | bytes 221216 | tf_op jit(solution)/shard_map/ppermute | solution.py:651
  21.7 4.2 %collective-permute-done.2.refs_4_ = bf16[72,1536]{1,0:T(8,128)(2,1)S(1)} collective-permute-done((bf16[72,1536]{1,0:T(8,128)(2,1)}, bf16[72,1536]{1,0:T(8,128)(2,1)S(1)}, u32[]{:S(2)}, u32[]{:S(2)}) %collective-permute-start.2) | collective-permute-done | bytes 221216 | tf_op jit(solution)/shard_map/ppermute | solution.py:651
  29.5 2.4 %collective-permute-start.10 = (bf16[144,1536]{1,0:T(8,128)(2,1)S(1)}, bf16[144,1536]{1,0:T(8,128)(2,1)S(1)}, u32[]{:S(2)}, u32[]{:S(2)}) collective-permute-start(bf16[144,1536]{1,0:T(8,128)(2,1)S(1)} %get-tuple-element.82), channel_id=1, source_target_pairs={{0,3},{1,2},{2,1},{3,0},{4,7},{5,6},{6,5},{7,4},{8,11},{9,10},{10,... | collective-permute-start | bytes 1327112 | tf_op jit(solution)/shard_map/ppermute | solution.py:651
  33.0 2.6 %collective-permute-start.7 = (bf16[4,72,1536]{2,1,0:T(8,128)(2,1)S(1)}, bf16[4,72,1536]{2,1,0:T(8,128)(2,1)S(1)}, u32[]{:S(2)}, u32[]{:S(2)}) collective-permute-start(bf16[4,72,1536]{2,1,0:T(8,128)(2,1)S(1)} %passed.4.refs_0_), channel_id=1, source_target_pairs={{0,8},{4,12},{8,0},{12,4},{1,9},{5,13},{9,1},{13,5},{2,10},{6,14},... | collective-permute-start | bytes 2654216 | tf_op jit(solution)/shard_map/ppermute | solution.py:651
  37.8 8.1 %collective-permute-done.5.refs_1_ = bf16[144,1536]{1,0:T(8,128)(2,1)S(1)} collective-permute-done((bf16[144,1536]{1,0:T(8,128)(2,1)S(1)}, bf16[144,1536]{1,0:T(8,128)(2,1)S(1)}, u32[]{:S(2)}, u32[]{:S(2)}) %collective-permute-start.5) | collective-permute-done | bytes 442400 | tf_op jit(solution)/shard_map/ppermute | solution.py:651
  48.2 4.9 %collective-permute-done.8.refs_1_ = bf16[144,1536]{1,0:T(8,128)(2,1)S(1)} collective-permute-done((bf16[144,1536]{1,0:T(8,128)(2,1)S(1)}, bf16[144,1536]{1,0:T(8,128)(2,1)S(1)}, u32[]{:S(2)}, u32[]{:S(2)}) %collective-permute-start.8) | collective-permute-done | bytes 442400 | tf_op jit(solution)/shard_map/ppermute | solution.py:651
  60.7 5.6 %expert_products.4 = (bf16[72,1536]{1,0:T(8,128)(2,1)S(1)}, bf16[72,1536]{1,0:T(8,128)(2,1)S(1)}, bf16[72,1536]{1,0:T(8,128)(2,1)S(1)}, bf16[72,1536]{1,0:T(8,12...) custom-call(bf16[144,1536]{1,0:T(8,128)(2,1)S(1)} %get-tuple-element, ...), custom_call_target="tpu_custom_call" | custom-call | flops 13800000512 | bytes 1 | tf_op jit(solution)/shard_map/expert_products/pallas_call | solution.py:415
  66.4 4.5 %collective-permute-done.12.refs_2_ = bf16[144,1536]{1,0:T(8,128)(2,1)S(1)} collective-permute-done((bf16[144,1536]{1,0:T(8,128)(2,1)S(1)}, bf16[144,1536]{1,0:T(8,128)(2,1)S(1)}, u32[]{:S(2)}, u32[]{:S(2)}) %collective-permute-start.12) | collective-permute-done | bytes 442400 | tf_op jit(solution)/shard_map/ppermute | solution.py:651
  70.9 5.7 %expert_products.5 = (bf16[144,1536]{1,0:T(8,128)(2,1)S(1)}, bf16[144,1536]{1,0:T(8,128)(2,1)S(1)}, bf16[144,1536]{1,0:T(8,128)(2,1)S(1)}, bf16[144,1536]{1,0:T(...) custom-call(bf16[144,1536]{1,0:T(8,128)(2,1)S(1)} %get-tuple-element, ...), custom_call_target="tpu_custom_call", output_to_operand_aliasing={{4}: (10, {}), {5}: (11, {}), {6}: (12, {}), {7}: (13, {})} | custom-call | flops 1 | bytes 1 | tf_op jit(solution)/shard_map/expert_products/pallas_call | solution.py:415
  81.7 8.8 %expert_products.6 = (bf16[112,1536]{1,0:T(8,128)(2,1)S(1)}, bf16[112,1536]{1,0:T(8,128)(2,1)S(1)}, bf16[112,1536]{1,0:T(8,128)(2,1)S(1)}, bf16[112,1536]{1,0:T(...) custom-call(bf16[4,72,1536]{2,1,0:T(8,128)(2,1)S(1)} %passed.4.refs_, ...), custom_call_target="tpu_custom_call", output_to_operand_aliasing={{4}: (5, {}), {5}: (6, {}), {6}: (7, {}), {7}: (8, {})} | custom-call | flops 11500000256 | bytes 1 | tf_op jit(solution)/shard_map/expert_products/pallas_call | solution.py:415
  90.5 5.4 %collective-permute-done.19.refs_4_ = bf16[144,1536]{1,0:T(8,128)(2,1)S(1)} collective-permute-done((bf16[144,1536]{1,0:T(8,128)(2,1)S(1)}, bf16[144,1536]{1,0:T(8,128)(2,1)S(1)}, u32[]{:S(2)}, u32[]{:S(2)}) %collective-permute-start.19) | collective-permute-done | bytes 442400 | tf_op jit(solution)/shard_map/ppermute | solution.py:651
  102.9 4.7 %collective-permute-done.27.got_ref.refs_1_ = bf16[128,1536]{1,0:T(8,128)(2,1)S(1)} collective-permute-done((bf16[128,1536]{1,0:T(8,128)(2,1)S(1)}, bf16[128,1536]{1,0:T(8,128)(2,1)S(1)}, u32[]{:S(2)}, u32[]{:S(2)}) %collective-permute-start.27) | collective-permute-done | bytes 393248 | tf_op jit(solution)/shard_map/ppermute | solution.py:651
  107.6 2.9 %collective-permute-start.28 = (bf16[64,1536]{1,0:T(8,128)(2,1)S(1)}, bf16[64,1536]{1,0:T(8,128)(2,1)S(1)}, u32[]{:S(2)}, u32[]{:S(2)}) collective-permute-start(bf16[64,1536]{1,0:T(8,128)(2,1)S(1)} %pair_sum.1), channel_id=1, source_target_pairs={{0,8},{4,12},{8,0},{12,4},{1,9},{5,13},{9,1},{13,5},{2,10},{6,14},... | collective-permute-start | bytes 589832 | tf_op jit(solution)/shard_map/ppermute | solution.py:651
  110.5 5.3 %expert_products.7 = (bf16[40,1536]{1,0:T(8,128)(2,1)S(1)}, bf16[40,1536]{1,0:T(8,128)(2,1)S(1)}, bf16[40,1536]{1,0:T(8,128)(2,1)S(1)}, bf16[40,1536]{1,0:T(8,12...) custom-call(bf16[4,72,1536]{2,1,0:T(8,128)(2,1)S(1)} %collective-per, ...), custom_call_target="tpu_custom_call", output_to_operand_aliasing={{4}: (4, {}), {5}: (5, {}), {6}: (6, {}), {7}: (7, {})} | custom-call | flops 1 | bytes 1 | tf_op jit(solution)/shard_map/expert_products/pallas_call | solution.py:415
  124.2 2.9 %collective-permute-start.26 = (bf16[64,1536]{1,0:T(8,128)(2,1)S(1)}, bf16[64,1536]{1,0:T(8,128)(2,1)S(1)}, u32[]{:S(2)}, u32[]{:S(2)}) collective-permute-start(bf16[64,1536]{1,0:T(8,128)(2,1)S(1)} %frame_sums.5), channel_id=1, source_target_pairs={{0,12},{4,8},{8,4},{12,0},{1,13},{5,9},{9,5},{13,1},{2,14},{6,10},... | collective-permute-start | bytes 589832 | tf_op jit(solution)/shard_map/ppermute | solution.py:651
  127.2 3.7 %norm_conv_back.2 = (bf16[64,1536]{1,0:T(8,128)(2,1)S(1)}, f32[32,1536]{1,0:T(8,128)S(1)}) custom-call(f32[64,1536]{1,0:T(8,128)S(1)} %get-tuple-element.108.refs_3_.refs_0_, bf16[128,1536]{1,0:T(8,128)(2,1)S(1)} %collective-permute-done.27.got_ref.refs_1_, bf16[64,1536]{1,0:T(8,128)(2,1)S(1)} %collective-permute-done.28.refs_2_, ...), custom_call_target="tpu_custom_call" | custom-call | flops 1 | bytes 1 | tf_op jit(solution)/shard_map/norm_conv_back/pallas_call | solution.py:588
  133.1 3.6 %norm_conv_back.3 = (bf16[2,64,1536]{2,1,0:T(8,128)(2,1)S(1)}, bf16[32,1536]{1,0:T(8,128)(2,1)S(1)}) custom-call(f32[64,1536]{1,0:T(8,128)S(1)} %get-tuple-element.117.refs_0_, bf16[64,1536]{1,0:T(8,128)(2,1)S(1)} %collective-permute-done.21.refs_1_, bf16[64,1536]{1,0:T(8,128)(2,1)S(1)} %collective-permute-done.22.refs_2_, ...), custom_call_target="tpu_custom_call" | custom-call | flops 1 | bytes 1 | tf_op jit(solution)/shard_map/norm_conv_back/pallas_call | solution.py:588
  136.7 2.7 %collective-permute-start.29 = (bf16[32,1536]{1,0:T(8,128)(2,1)S(1)}, bf16[32,1536]{1,0:T(8,128)(2,1)S(1)}, u32[]{:S(2)}, u32[]{:S(2)}) collective-permute-start(bf16[32,1536]{1,0:T(8,128)(2,1)S(1)} %get-tuple-element.130), channel_id=1, source_target_pairs={{0,4},{4,0},{8,12},{12,8},{1,5},{5,1},{9,13},{13,9},{2,6},{6,2},{1... | collective-permute-start | bytes 294920 | tf_op jit(solution)/shard_map/ppermute | solution.py:651
  141.9 8.0 %fusion.1 = bf16[1,1,1536,1536]{3,2,1,0:T(8,128)(2,1)} fusion(bf16[1184,1536]{1,0:T(8,128)(2,1)S(1)} %copy-done.12, bf16[1184,1536]{1,0:T(8,128)(2,1)S(1)} %copy-done.11), kind=kOutput, calls=%fused_computation.3 | convolution fusion | flops 5589172224 | bytes 11993088 | tf_op jit(solution)/shard_map/dot_general | solution.py:740
  153.6 8.0 %fusion = bf16[1,1,1536,1536]{3,2,1,0:T(8,128)(2,1)} fusion(bf16[1184,1536]{1,0:T(8,128)(2,1)S(1)} %copy-done.10, bf16[1184,1536]{1,0:T(8,128)(2,1)S(1)} %copy-done.13), kind=kOutput, calls=%fused_computation.2 | convolution fusion | flops 5589172224 | bytes 11993088 | tf_op jit(solution)/shard_map/dot_general | solution.py:739
  (98 shorter events, 50.4 us)
Async XLA Ops:
  3.7 22.8 %collective-permute-start = (bf16[144,1536]{1,0:T(8,128)(2,1)}, bf16[144,1536]{1,0:T(8,128)(2,1)S(1)}, u32[]{:S(2)}, u32[]{:S(2)}) collective-permute-start(bf16[144,1536]{1,0:T(8,128)(2,1)} %first_send.1._.refs_0_), channel_id=1, source_target_pairs={{0,4},{4,0},{8,12},{12,8},{1,5},{5,1},{9,13},{13,9},{2,6},{6,2},{1... | collective-permute-start | bytes 1327112 | tf_op jit(solution)/shard_map/ppermute | solution.py:651
  6.8 22.3 %collective-permute-start.4 = (bf16[144,1536]{1,0:T(8,128)(2,1)}, bf16[144,1536]{1,0:T(8,128)(2,1)S(1)}, u32[]{:S(2)}, u32[]{:S(2)}) collective-permute-start(bf16[144,1536]{1,0:T(8,128)(2,1)} %first_send.1._.refs_0_), channel_id=1, source_target_pairs={{0,8},{4,12},{8,0},{12,4},{1,9},{5,13},{9,1},{13,5},{2,10},{6,14},... | collective-permute-start | bytes 1327112 | tf_op jit(solution)/shard_map/ppermute | solution.py:651
  14.7 11.3 %collective-permute-start.2 = (bf16[72,1536]{1,0:T(8,128)(2,1)}, bf16[72,1536]{1,0:T(8,128)(2,1)S(1)}, u32[]{:S(2)}, u32[]{:S(2)}) collective-permute-start(bf16[72,1536]{1,0:T(8,128)(2,1)} %get-tuple-element.74), channel_id=1, source_target_pairs={{0,2},{1,3},{2,0},{3,1},{4,6},{5,7},{6,4},{7,5},{8,10},{9,11},{10,... | collective-permute-start | bytes 663560 | tf_op jit(solution)/shard_map/ppermute | solution.py:651
  29.1 16.8 %collective-permute-start.5 = (bf16[144,1536]{1,0:T(8,128)(2,1)S(1)}, bf16[144,1536]{1,0:T(8,128)(2,1)S(1)}, u32[]{:S(2)}, u32[]{:S(2)}) collective-permute-start(bf16[144,1536]{1,0:T(8,128)(2,1)S(1)} %passed.3.refs_0_.refs_1_), channel_id=1, source_target_pairs={{0,4},{4,0},{8,12},{12,8},{1,5},{5,1},{9,13},{13,9},{2,6},{6,2},{1... | collective-permute-start | bytes 1327112 | tf_op jit(solution)/shard_map/ppermute | solution.py:651
  29.5 17.2 %collective-permute-start.10 = (bf16[144,1536]{1,0:T(8,128)(2,1)S(1)}, bf16[144,1536]{1,0:T(8,128)(2,1)S(1)}, u32[]{:S(2)}, u32[]{:S(2)}) collective-permute-start(bf16[144,1536]{1,0:T(8,128)(2,1)S(1)} %get-tuple-element.82), channel_id=1, source_target_pairs={{0,3},{1,2},{2,1},{3,0},{4,7},{5,6},{6,5},{7,4},{8,11},{9,10},{10,... | collective-permute-start | bytes 1327112 | tf_op jit(solution)/shard_map/ppermute | solution.py:651
  32.0 21.1 %collective-permute-start.8 = (bf16[144,1536]{1,0:T(8,128)(2,1)S(1)}, bf16[144,1536]{1,0:T(8,128)(2,1)S(1)}, u32[]{:S(2)}, u32[]{:S(2)}) collective-permute-start(bf16[144,1536]{1,0:T(8,128)(2,1)S(1)} %get-tuple-element.80), channel_id=1, source_target_pairs={{0,1},{1,0},{2,3},{3,2},{4,5},{5,4},{6,7},{7,6},{8,9},{9,8},{10,11... | collective-permute-start | bytes 1327112 | tf_op jit(solution)/shard_map/ppermute | solution.py:651
  32.5 21.1 %collective-permute-start.9 = (bf16[144,1536]{1,0:T(8,128)(2,1)S(1)}, bf16[144,1536]{1,0:T(8,128)(2,1)S(1)}, u32[]{:S(2)}, u32[]{:S(2)}) collective-permute-start(bf16[144,1536]{1,0:T(8,128)(2,1)S(1)} %get-tuple-element.81), channel_id=1, source_target_pairs={{0,2},{1,3},{2,0},{3,1},{4,6},{5,7},{6,4},{7,5},{8,10},{9,11},{10,... | collective-permute-start | bytes 1327112 | tf_op jit(solution)/shard_map/ppermute | solution.py:651
  33.0 47.1 %collective-permute-start.7 = (bf16[4,72,1536]{2,1,0:T(8,128)(2,1)S(1)}, bf16[4,72,1536]{2,1,0:T(8,128)(2,1)S(1)}, u32[]{:S(2)}, u32[]{:S(2)}) collective-permute-start(bf16[4,72,1536]{2,1,0:T(8,128)(2,1)S(1)} %passed.4.refs_0_), channel_id=1, source_target_pairs={{0,8},{4,12},{8,0},{12,4},{1,9},{5,13},{9,1},{13,5},{2,10},{6,14},... | collective-permute-start | bytes 2654216 | tf_op jit(solution)/shard_map/ppermute | solution.py:651
  45.9 35.8 %collective-permute-start.6 = (bf16[4,72,1536]{2,1,0:T(8,128)(2,1)S(1)}, bf16[4,72,1536]{2,1,0:T(8,128)(2,1)S(1)}, u32[]{:S(2)}, u32[]{:S(2)}) collective-permute-start(bf16[4,72,1536]{2,1,0:T(8,128)(2,1)S(1)} %passed.4.refs_0_), channel_id=1, source_target_pairs={{0,4},{4,0},{8,12},{12,8},{1,5},{5,1},{9,13},{13,9},{2,6},{6,2},{1... | collective-permute-start | bytes 2654216 | tf_op jit(solution)/shard_map/ppermute | solution.py:651
  46.7 19.6 %collective-permute-start.11 = (bf16[144,1536]{1,0:T(8,128)(2,1)S(1)}, bf16[144,1536]{1,0:T(8,128)(2,1)S(1)}, u32[]{:S(2)}, u32[]{:S(2)}) collective-permute-start(bf16[144,1536]{1,0:T(8,128)(2,1)S(1)} %get-tuple-element.86), channel_id=1, source_target_pairs={{0,1},{1,0},{2,3},{3,2},{4,5},{5,4},{6,7},{7,6},{8,9},{9,8},{10,11... | collective-permute-start | bytes 1327112 | tf_op jit(solution)/shard_map/ppermute | solution.py:651
  53.1 17.8 %collective-permute-start.12 = (bf16[144,1536]{1,0:T(8,128)(2,1)S(1)}, bf16[144,1536]{1,0:T(8,128)(2,1)S(1)}, u32[]{:S(2)}, u32[]{:S(2)}) collective-permute-start(bf16[144,1536]{1,0:T(8,128)(2,1)S(1)} %get-tuple-element.87), channel_id=1, source_target_pairs={{0,2},{1,3},{2,0},{3,1},{4,6},{5,7},{6,4},{7,5},{8,10},{9,11},{10,... | collective-permute-start | bytes 1327112 | tf_op jit(solution)/shard_map/ppermute | solution.py:651
  53.6 17.2 %collective-permute-start.13 = (bf16[144,1536]{1,0:T(8,128)(2,1)S(1)}, bf16[144,1536]{1,0:T(8,128)(2,1)S(1)}, u32[]{:S(2)}, u32[]{:S(2)}) collective-permute-start(bf16[144,1536]{1,0:T(8,128)(2,1)S(1)} %get-tuple-element.88), channel_id=1, source_target_pairs={{0,3},{1,2},{2,1},{3,0},{4,7},{5,6},{6,5},{7,4},{8,11},{9,10},{10,... | collective-permute-start | bytes 1327112 | tf_op jit(solution)/shard_map/ppermute | solution.py:651
  76.6 14.0 %collective-permute-start.18 = (bf16[144,1536]{1,0:T(8,128)(2,1)S(1)}, bf16[144,1536]{1,0:T(8,128)(2,1)S(1)}, u32[]{:S(2)}, u32[]{:S(2)}) collective-permute-start(bf16[144,1536]{1,0:T(8,128)(2,1)S(1)} %get-tuple-element.105), channel_id=1, source_target_pairs={{0,1},{1,0},{2,3},{3,2},{4,5},{5,4},{6,7},{7,6},{8,9},{9,8},{10,11... | collective-permute-start | bytes 1327112 | tf_op jit(solution)/shard_map/ppermute | solution.py:651
  78.1 17.8 %collective-permute-start.19 = (bf16[144,1536]{1,0:T(8,128)(2,1)S(1)}, bf16[144,1536]{1,0:T(8,128)(2,1)S(1)}, u32[]{:S(2)}, u32[]{:S(2)}) collective-permute-start(bf16[144,1536]{1,0:T(8,128)(2,1)S(1)} %get-tuple-element.106), channel_id=1, source_target_pairs={{0,2},{1,3},{2,0},{3,1},{4,6},{5,7},{6,4},{7,5},{8,10},{9,11},{10,... | collective-permute-start | bytes 1327112 | tf_op jit(solution)/shard_map/ppermute | solution.py:651
  78.7 17.2 %collective-permute-start.20 = (bf16[144,1536]{1,0:T(8,128)(2,1)S(1)}, bf16[144,1536]{1,0:T(8,128)(2,1)S(1)}, u32[]{:S(2)}, u32[]{:S(2)}) collective-permute-start(bf16[144,1536]{1,0:T(8,128)(2,1)S(1)} %get-tuple-element.107), channel_id=1, source_target_pairs={{0,3},{1,2},{2,1},{3,0},{4,7},{5,6},{6,5},{7,4},{8,11},{9,10},{10,... | collective-permute-start | bytes 1327112 | tf_op jit(solution)/shard_map/ppermute | solution.py:651
  80.1 30.4 %collective-permute-start.17 = (bf16[4,72,1536]{2,1,0:T(8,128)(2,1)S(1)}, bf16[4,72,1536]{2,1,0:T(8,128)(2,1)S(1)}, u32[]{:S(2)}, u32[]{:S(2)}) collective-permute-start(bf16[4,72,1536]{2,1,0:T(8,128)(2,1)S(1)} %passed.5.refs_2_), channel_id=1, source_target_pairs={{0,4},{4,0},{8,12},{12,8},{1,5},{5,1},{9,13},{13,9},{2,6},{6,2},{1... | collective-permute-start | bytes 2654216 | tf_op jit(solution)/shard_map/ppermute | solution.py:651
  99.4 16.7 %collective-permute-start.14 = (bf16[112,1536]{1,0:T(8,128)(2,1)S(1)}, bf16[112,1536]{1,0:T(8,128)(2,1)S(1)}, u32[]{:S(2)}, u32[]{:S(2)}) collective-permute-start(bf16[112,1536]{1,0:T(8,128)(2,1)S(1)} %get-tuple-element.101), channel_id=1, source_target_pairs={{0,1},{1,0},{2,3},{3,2},{4,5},{5,4},{6,7},{7,6},{8,9},{9,8},{10,11... | collective-permute-start | bytes 1032200 | tf_op jit(solution)/shard_map/ppermute | solution.py:651
  100.2 16.9 %collective-permute-start.15 = (bf16[112,1536]{1,0:T(8,128)(2,1)S(1)}, bf16[112,1536]{1,0:T(8,128)(2,1)S(1)}, u32[]{:S(2)}, u32[]{:S(2)}) collective-permute-start(bf16[112,1536]{1,0:T(8,128)(2,1)S(1)} %get-tuple-element.102), channel_id=1, source_target_pairs={{0,2},{1,3},{2,0},{3,1},{4,6},{5,7},{6,4},{7,5},{8,10},{9,11},{10,... | collective-permute-start | bytes 1032200 | tf_op jit(solution)/shard_map/ppermute | solution.py:651
  101.1 18.3 %collective-permute-start.16 = (bf16[112,1536]{1,0:T(8,128)(2,1)S(1)}, bf16[112,1536]{1,0:T(8,128)(2,1)S(1)}, u32[]{:S(2)}, u32[]{:S(2)}) collective-permute-start(bf16[112,1536]{1,0:T(8,128)(2,1)S(1)} %get-tuple-element.103), channel_id=1, source_target_pairs={{0,3},{1,2},{2,1},{3,0},{4,7},{5,6},{6,5},{7,4},{8,11},{9,10},{10,... | collective-permute-start | bytes 1032200 | tf_op jit(solution)/shard_map/ppermute | solution.py:651
  107.6 19.5 %collective-permute-start.28 = (bf16[64,1536]{1,0:T(8,128)(2,1)S(1)}, bf16[64,1536]{1,0:T(8,128)(2,1)S(1)}, u32[]{:S(2)}, u32[]{:S(2)}) collective-permute-start(bf16[64,1536]{1,0:T(8,128)(2,1)S(1)} %pair_sum.1), channel_id=1, source_target_pairs={{0,8},{4,12},{8,0},{12,4},{1,9},{5,13},{9,1},{13,5},{2,10},{6,14},... | collective-permute-start | bytes 589832 | tf_op jit(solution)/shard_map/ppermute | solution.py:651
  121.4 11.6 %collective-permute-start.22 = (bf16[64,1536]{1,0:T(8,128)(2,1)S(1)}, bf16[64,1536]{1,0:T(8,128)(2,1)S(1)}, u32[]{:S(2)}, u32[]{:S(2)}) collective-permute-start(bf16[64,1536]{1,0:T(8,128)(2,1)S(1)} %get-tuple-element.119), channel_id=1, source_target_pairs={{0,8},{4,12},{8,0},{12,4},{1,9},{5,13},{9,1},{13,5},{2,10},{6,14},... | collective-permute-start | bytes 589832 | tf_op jit(solution)/shard_map/ppermute | solution.py:651
  136.7 13.2 %collective-permute-start.29 = (bf16[32,1536]{1,0:T(8,128)(2,1)S(1)}, bf16[32,1536]{1,0:T(8,128)(2,1)S(1)}, u32[]{:S(2)}, u32[]{:S(2)}) collective-permute-start(bf16[32,1536]{1,0:T(8,128)(2,1)S(1)} %get-tuple-element.130), channel_id=1, source_target_pairs={{0,4},{4,0},{8,12},{12,8},{1,5},{5,1},{9,13},{13,9},{2,6},{6,2},{1... | collective-permute-start | bytes 294920 | tf_op jit(solution)/shard_map/ppermute | solution.py:651
  149.9 11.6 %collective-permute-start.35 = (bf16[2,64,1536]{2,1,0:T(8,128)(2,1)S(1)}, bf16[2,64,1536]{2,1,0:T(8,128)(2,1)S(1)}, u32[]{:S(2)}, u32[]{:S(2)}) collective-permute-start(bf16[2,64,1536]{2,1,0:T(8,128)(2,1)S(1)} %get-tuple-element.131), channel_id=1, source_target_pairs={{0,16},{16,0},{1,17},{17,1},{2,18},{18,2},{3,19},{19,3},{4,20},{20... | collective-permute-start | bytes 1179656 | tf_op jit(solution)/shard_map/ppermute | solution.py:746
  150.0 11.5 %collective-permute-start.32 = (bf16[32,1536]{1,0:T(8,128)(2,1)S(1)}, bf16[32,1536]{1,0:T(8,128)(2,1)S(1)}, u32[]{:S(2)}, u32[]{:S(2)}) collective-permute-start(bf16[32,1536]{1,0:T(8,128)(2,1)S(1)} %add_convert_fusion.refs_0_), channel_id=1, source_target_pairs={{0,1},{1,0},{2,3},{3,2},{4,5},{5,4},{6,7},{7,6},{8,9},{9,8},{10,11... | collective-permute-start | bytes 294920 | tf_op jit(solution)/shard_map/ppermute | solution.py:651
  (26 other events, 264.4 us)
